TPU v7x, 128 devices: a whole 4x4x4 slice. The times are simulated.
128 devices in a mesh: row: 16 (over x, y_hi, core), col: 8 (over y_lo, z).
Axes of the slice: x: 4, y: 4 (y_hi: 2, y_lo: 2; y = y_hi * 2 + y_lo), z: 4, core: 2. Of those that a mesh axis runs over, the one named last changes fastest.
Arguments:
- node_feats: bfloat16 [4, 384, 256], P(None, 'row'), may hold values from -6 to 6
- pair_feats: bfloat16 [4, 384, 384, 128], P(None, 'row', 'col'), may hold values from -6 to 6
- distances: float32 [4, 384, 384], P(None, 'row', 'col'), may hold values from -4 to 4
- lengths: int32 [4], replicated, may hold values from 64 to 384, as said below
- node_cotan: bfloat16 [4, 384, 256], P(None, 'row'), may hold values from -6 to 6
- pair_cotan: bfloat16 [4, 384, 384, 128], P(None, 'row', 'col'), may hold values from -6 to 6
- w_qkv: bfloat16 [256, 768], replicated, may hold values from -0.375 to 0.375
- w_bias: bfloat16 [128, 8], replicated, may hold values from -0.5 to 0.5
- w_dist: float32 [8], replicated, may hold values from -1 to 1
- w_node_out: bfloat16 [256, 256], replicated, may hold values from -2 to 2
- g_node: float32 [256], replicated, may hold values from 0.1 to 1.9
- w_ab: bfloat16 [256, 64], replicated, may hold values from -0.375 to 0.375
- w_outer: bfloat16 [32, 4096], replicated, may hold values from -0.1875 to 0.1875
- b_outer: float32 [128], replicated, may hold values from -3 to 3
- g_tin: float32 [2, 128], replicated, may hold values from 0.1 to 1.9
- w_tin: bfloat16 [2, 128, 640], replicated, may hold values from -0.5 to 0.5
- g_tout: float32 [2, 128], replicated, may hold values from 0.1 to 1.9
- w_tout: bfloat16 [2, 128, 128], replicated, may hold values from -0.5 to 0.5
- g_trans: float32 [128], replicated, may hold values from 0.1 to 1.9
- w_up: bfloat16 [128, 512], replicated, may hold values from -0.5 to 0.5
- w_down: bfloat16 [512, 128], replicated, may hold values from -0.25 to 0.25
Outputs:
- node_out: float32 [4, 384, 256], P(None, 'row')
- pair_out: float32 [4, 384, 384, 128], P(None, 'row', 'col')
- grad_node: float32 [4, 384, 256], P(None, 'row')
- grad_pair: float32 [4, 384, 384, 128], P(None, 'row', 'col')
- grad_dist: float32 [4, 384, 384], P(None, 'row', 'col')
- grad_w_qkv: float32 [256, 768], replicated
- grad_w_bias: float32 [128, 8], replicated
- grad_w_dist: float32 [8], replicated
- grad_w_node_out: float32 [256, 256], replicated
- grad_g_node: float32 [256], replicated
- grad_w_ab: float32 [256, 64], replicated
- grad_w_outer: float32 [32, 4096], replicated
- grad_b_outer: float32 [128], replicated
- grad_g_tin: float32 [2, 128], replicated
- grad_w_tin: float32 [2, 128, 640], replicated
- grad_g_tout: float32 [2, 128], replicated
- grad_w_tout: float32 [2, 128, 128], replicated
- grad_g_trans: float32 [128], replicated
- grad_w_up: float32 [128, 512], replicated
- grad_w_down: float32 [512, 128], replicated
Inputs may be any that keep to these rules, and one draw needn't show every extreme that they name: `lengths`: residues of each protein; in every draw at least one protein fills all 384 slots.
All inputs are finite; a program needn't handle non-finite values.
Results may differ from a plain program's by a relative error of at most 0.019.
Values may be sent and summed in bfloat16 or wider, within the bound.
No kernel may reach another device: no remote copies, remote signals or barrier semaphores. Data moves between devices by JAX's collectives and lax.ppermute only.
A program may use at most 256 MiB of HBM per device.

v0:
```python
import jax
import jax.numpy as jnp
from jax import lax
from jax.sharding import PartitionSpec as P

D = 256
C = 128
H = 8
HD = 32
CH = 128
OP = 32
ITEM_BLOCK = 2


eps = 1e-05


def layer_norm(values, gain_vec):
    centered = values - jnp.mean(values, axis=-1, keepdims=True)
    spread = jnp.mean(centered * centered, axis=-1, keepdims=True)
    return centered * lax.rsqrt(spread + eps) * gain_vec


def to_half(values):
    return values.astype(jnp.bfloat16)


def matmul(inputs, weight):
    return jnp.dot(inputs, weight, preferred_element_type=jnp.float32)


def weight_grad(inputs, grad_vals):
    flat_in = inputs.reshape(-1, inputs.shape[-1])
    flat_grad = grad_vals.reshape(-1, grad_vals.shape[-1])
    return lax.dot_general(
        flat_in, flat_grad, (((0,), (0,)), ((), ())), preferred_element_type=jnp.float32
    )


def input_grad(grad_vals, weight):
    return lax.dot_general(
        grad_vals,
        weight,
        (((grad_vals.ndim - 1,), (1,)), ((), ())),
        preferred_element_type=jnp.float32,
    )


def norm_back(values, gain_vec, grad_vals):
    unused, pullback = jax.vjp(layer_norm, values, gain_vec)
    return pullback(grad_vals)


def sum_weights(grad_list):
    return lax.psum(
        (
            grad_list[0],
            grad_list[1],
            grad_list[2],
            grad_list[3],
            grad_list[4],
            grad_list[5],
            grad_list[6],
            grad_list[7],
            grad_list[8],
            grad_list[9],
            grad_list[10],
            grad_list[11],
            grad_list[12],
            grad_list[13],
            grad_list[14],
        ),
        ("row", "col"),
    )


def per_device(
    node_feats,
    pair_feats,
    distances,
    lengths,
    node_cotan,
    pair_cotan,
    w_qkv,
    w_bias,
    w_dist,
    w_node_out,
    g_node,
    w_ab,
    w_outer,
    b_outer,
    g_tin,
    w_tin,
    g_tout,
    w_tout,
    g_trans,
    w_up,
    w_down,
):
    col_count = lax.axis_size("col")
    row_index = lax.axis_index("row")
    col_index = lax.axis_index("col")
    tile_rows = pair_feats.shape[1]
    tile_cols = pair_feats.shape[2]
    residues = tile_rows * lax.axis_size("row")
    heads_here = H // col_count
    head_width = heads_here * HD
    head_start = col_index * head_width
    score_scale = HD ** (-0.5)
    blk_items = ITEM_BLOCK
    step_count = node_feats.shape[0] // blk_items
    w_local = jnp.concatenate(
        [
            lax.dynamic_slice_in_dim(w_qkv, part_index * D + head_start, head_width, 1)
            for part_index in range(3)
        ],
        axis=1,
    )
    wo_local = lax.dynamic_slice_in_dim(w_node_out, head_start, head_width, 0)
    row_ids = row_index * tile_rows + jnp.arange(tile_rows, dtype=jnp.int32)
    col_ids = col_index * tile_cols + jnp.arange(tile_cols, dtype=jnp.int32)
    all_ids = jnp.arange(residues, dtype=jnp.int32)

    def tri_front(values, pair_keep, tri_index):
        normed = to_half(layer_norm(values, g_tin[tri_index]))
        projected = matmul(normed, w_tin[tri_index])
        left_side = to_half(
            jax.nn.sigmoid(projected[..., CH : 2 * CH]) * projected[..., :CH] * pair_keep
        )
        right_side = to_half(
            jax.nn.sigmoid(projected[..., 3 * CH : 4 * CH])
            * projected[..., 2 * CH : 3 * CH]
            * pair_keep
        )
        return (normed, projected, left_side, right_side)

    def tri_rear(values, projected, product, tri_index):
        normed = to_half(layer_norm(product, g_tout[tri_index]))
        update = matmul(normed, w_tout[tri_index])
        return (values + jax.nn.sigmoid(projected[..., 4 * CH :]) * update, normed, update)

    def rear_back(grad_vals, projected, product, normed, update, tri_index):
        gate_vals = jax.nn.sigmoid(projected[..., 4 * CH :])
        d_update = to_half(grad_vals * gate_vals)
        dw_out = weight_grad(normed, d_update)
        d_normed = to_half(input_grad(d_update, w_tout[tri_index]))
        d_product, dg_out = norm_back(product, g_tout[tri_index], d_normed.astype(jnp.float32))
        d_gate = grad_vals * update * gate_vals * (1.0 - gate_vals)
        return (to_half(d_product), d_gate, dw_out, dg_out)

    def front_back(values, pair_keep, normed, projected, d_left, d_right, d_gate, tri_index):
        sig_left = jax.nn.sigmoid(projected[..., CH : 2 * CH])
        sig_right = jax.nn.sigmoid(projected[..., 3 * CH : 4 * CH])
        left_grad = d_left.astype(jnp.float32) * pair_keep
        right_grad = d_right.astype(jnp.float32) * pair_keep
        d_proj = to_half(
            jnp.concatenate(
                [
                    left_grad * sig_left,
                    left_grad * projected[..., :CH] * sig_left * (1.0 - sig_left),
                    right_grad * sig_right,
                    right_grad * projected[..., 2 * CH : 3 * CH] * sig_right * (1.0 - sig_right),
                    d_gate,
                ],
                axis=-1,
            )
        )
        dw_in = weight_grad(normed, d_proj)
        d_normed = to_half(input_grad(d_proj, w_tin[tri_index]))
        d_values, dg_in = norm_back(values, g_tin[tri_index], d_normed.astype(jnp.float32))
        return (d_values, dw_in, dg_in)

    def run_block(running, block_in):
        node_blk, pair_blk, dist_blk, length_blk, node_cot, pair_cot = block_in
        row_keep = (row_ids[None, :] < length_blk[:, None]).astype(jnp.float32)
        col_keep = (col_ids[None, :] < length_blk[:, None]).astype(jnp.float32)
        key_keep = (all_ids[None, :] < length_blk[:, None]).astype(jnp.float32)
        pair_keep = (row_keep[:, :, None] * col_keep[:, None, :])[..., None]
        node_full = node_blk.astype(jnp.float32)
        pair_full = pair_blk.astype(jnp.float32)
        qkv = to_half(matmul(node_blk, w_local))
        normed_node = to_half(layer_norm(node_full, g_node))
        pair_rows = to_half(matmul(normed_node, w_ab))
        left_node = pair_rows[..., :OP]
        kv_all, right_node_all = (
            lax.all_gather(qkv[..., head_width:], "row", axis=1, tiled=True),
            lax.all_gather(pair_rows[..., OP:], "row", axis=1, tiled=True),
        )
        bias_tile = to_half(
            jnp.einsum("gijc,ch->ghij", pair_blk, w_bias, preferred_element_type=jnp.float32)
            + w_dist[None, :, None, None] * dist_blk[:, None, :, :]
        )
        bias_rows = lax.all_to_all(bias_tile, "col", split_axis=1, concat_axis=3, tiled=True)
        query_heads = qkv[..., :head_width].reshape(blk_items, tile_rows, heads_here, HD)
        key_all = kv_all[..., :head_width].reshape(blk_items, residues, heads_here, HD)
        value_all = kv_all[..., head_width:].reshape(blk_items, residues, heads_here, HD)
        scores = (
            jnp.einsum("gihd,gjhd->ghij", query_heads, key_all, preferred_element_type=jnp.float32)
            * score_scale
            + bias_rows.astype(jnp.float32)
            + ((key_keep - 1.0) * 1000000000.0)[:, None, None, :]
        )
        attn_probs = jax.nn.softmax(scores, axis=-1)
        probs_half = to_half(attn_probs)
        attended = to_half(
            jnp.einsum(
                "ghij,gjhd->gihd", probs_half, value_all, preferred_element_type=jnp.float32
            ).reshape(blk_items, tile_rows, head_width)
        )
        node_out = node_full + lax.psum(
            matmul(attended, wo_local).astype(jnp.bfloat16), "col"
        ).astype(jnp.float32)
        right_cols = lax.dynamic_slice_in_dim(right_node_all, col_index * tile_cols, tile_cols, 1)
        middle = to_half(matmul(left_node, w_outer)).reshape(blk_items, tile_rows, OP, C)
        outer_term = (
            jnp.einsum("giqc,gjq->gijc", middle, right_cols, preferred_element_type=jnp.float32)
            + b_outer
        )
        pair_one = pair_full + pair_keep * outer_term
        normed_one, proj_one, left_one, right_one = tri_front(pair_one, pair_keep, 0)
        right_slab = lax.all_gather(right_one, "row", axis=1, tiled=True)
        slab_piece = right_slab
        product_one = jnp.transpose(
            lax.psum_scatter(
                jnp.einsum(
                    "gikc,gjkc->jgic", left_one, slab_piece, preferred_element_type=jnp.float32
                ).astype(jnp.bfloat16),
                "col",
                scatter_dimension=0,
                tiled=True,
            ).astype(jnp.float32),
            (1, 2, 0, 3),
        )
        pair_two, normed_yone, update_one = tri_rear(pair_one, proj_one, product_one, 0)
        normed_two, proj_two, left_two, right_two = tri_front(pair_two, pair_keep, 1)
        left_slab = lax.all_gather(left_two, "col", axis=2, tiled=True)
        slab_piece = left_slab
        product_two = jnp.transpose(
            lax.psum_scatter(
                jnp.einsum(
                    "gkic,gkjc->igjc", slab_piece, right_two, preferred_element_type=jnp.float32
                ).astype(jnp.bfloat16),
                "row",
                scatter_dimension=0,
                tiled=True,
            ).astype(jnp.float32),
            (1, 0, 2, 3),
        )
        pair_three, normed_ytwo, update_two = tri_rear(pair_two, proj_two, product_two, 1)
        normed_three = to_half(layer_norm(pair_three, g_trans))
        hidden = matmul(normed_three, w_up)
        active = to_half(jax.nn.silu(hidden))
        pair_four = pair_three + matmul(active, w_down)
        grad_pair = pair_cot.astype(jnp.float32)
        dw_down = weight_grad(active, pair_cot)
        d_active = to_half(input_grad(pair_cot, w_down))
        unused, silu_pull = jax.vjp(jax.nn.silu, hidden)
        d_hidden = to_half(silu_pull(d_active.astype(jnp.float32))[0])
        dw_up = weight_grad(normed_three, d_hidden)
        d_normed_three = to_half(input_grad(d_hidden, w_up))
        d_pair_norm, dg_trans = norm_back(pair_three, g_trans, d_normed_three.astype(jnp.float32))
        grad_pair = grad_pair + d_pair_norm
        d_prod_two, d_gate_two, dw_tout_two, dg_tout_two = rear_back(
            grad_pair, proj_two, product_two, normed_ytwo, update_two, 1
        )
        dprod_rows = lax.all_gather(d_prod_two, "row", axis=1, tiled=True)
        d_right_two = to_half(
            jnp.einsum("gkic,gijc->gkjc", left_slab, dprod_rows, preferred_element_type=jnp.float32)
        )
        slab_piece = dprod_rows
        d_left_two = to_half(
            jnp.transpose(
                lax.psum_scatter(
                    jnp.einsum(
                        "gkjc,gijc->igkc", right_two, slab_piece, preferred_element_type=jnp.float32
                    ).astype(jnp.bfloat16),
                    "col",
                    scatter_dimension=0,
                    tiled=True,
                ).astype(jnp.float32),
                (1, 2, 0, 3),
            )
        )
        d_front_two, dw_tin_two, dg_tin_two = front_back(
            pair_two, pair_keep, normed_two, proj_two, d_left_two, d_right_two, d_gate_two, 1
        )
        grad_pair = grad_pair + d_front_two
        d_prod_one, d_gate_one, dw_tout_one, dg_tout_one = rear_back(
            grad_pair, proj_one, product_one, normed_yone, update_one, 0
        )
        dprod_cols = lax.all_gather(d_prod_one, "col", axis=2, tiled=True)
        d_left_one = to_half(
            jnp.einsum(
                "gijc,gjkc->gikc", dprod_cols, right_slab, preferred_element_type=jnp.float32
            )
        )
        slab_piece = dprod_cols
        d_right_one = to_half(
            jnp.transpose(
                lax.psum_scatter(
                    jnp.einsum(
                        "gijc,gikc->jgkc", slab_piece, left_one, preferred_element_type=jnp.float32
                    ).astype(jnp.bfloat16),
                    "row",
                    scatter_dimension=0,
                    tiled=True,
                ).astype(jnp.float32),
                (1, 0, 2, 3),
            )
        )
        d_front_one, dw_tin_one, dg_tin_one = front_back(
            pair_one, pair_keep, normed_one, proj_one, d_left_one, d_right_one, d_gate_one, 0
        )
        grad_pair = grad_pair + d_front_one
        outer_grad = grad_pair * pair_keep
        db_outer = jnp.sum(outer_grad, axis=(0, 1, 2))
        d_outer = to_half(outer_grad)
        d_middle_part = jnp.einsum(
            "gijc,gjq->giqc", d_outer, right_cols, preferred_element_type=jnp.float32
        )
        d_right_part = jnp.einsum(
            "gijc,giqc->gjq", d_outer, middle, preferred_element_type=jnp.float32
        )
        right_scatter = lax.dynamic_update_slice_in_dim(
            jnp.zeros((blk_items, residues, OP), jnp.float32),
            d_right_part,
            col_index * tile_cols,
            1,
        )
        dwo_own = weight_grad(attended, node_cot)
        d_attended = to_half(input_grad(node_cot, wo_local)).reshape(
            blk_items, tile_rows, heads_here, HD
        )
        d_probs = jnp.einsum(
            "gihd,gjhd->ghij", d_attended, value_all, preferred_element_type=jnp.float32
        )
        d_value = jnp.einsum(
            "ghij,gihd->gjhd", probs_half, d_attended, preferred_element_type=jnp.float32
        ).reshape(blk_items, residues, head_width)
        d_scores = to_half(
            attn_probs * (d_probs - jnp.sum(attn_probs * d_probs, axis=-1, keepdims=True))
        )
        d_query = (
            jnp.einsum("ghij,gjhd->gihd", d_scores, key_all, preferred_element_type=jnp.float32)
            * score_scale
        ).reshape(blk_items, tile_rows, head_width)
        d_key = (
            jnp.einsum("ghij,gihd->gjhd", d_scores, query_heads, preferred_element_type=jnp.float32)
            * score_scale
        ).reshape(blk_items, residues, head_width)
        d_bias_tile = lax.all_to_all(d_scores, "col", split_axis=3, concat_axis=1, tiled=True)
        d_kv_own, d_right_rows = (
            lax.psum_scatter(
                jnp.concatenate([d_key, d_value], axis=-1).astype(jnp.bfloat16),
                "row",
                scatter_dimension=1,
                tiled=True,
            ).astype(jnp.float32),
            lax.psum_scatter(
                right_scatter.astype(jnp.bfloat16), "row", scatter_dimension=1, tiled=True
            ).astype(jnp.float32),
        )
        d_qkv = to_half(jnp.concatenate([d_query, d_kv_own], axis=-1))
        dw_qkv_own = weight_grad(node_blk, d_qkv)
        d_att_part = input_grad(d_qkv, w_local)
        d_att_node, d_middle, d_right_sum = (
            lax.psum(d_att_part.astype(jnp.bfloat16), "col").astype(jnp.float32),
            lax.psum(d_middle_part.astype(jnp.bfloat16), "col").astype(jnp.float32),
            lax.psum(d_right_rows.astype(jnp.bfloat16), "col").astype(jnp.float32),
        )
        d_middle_half = to_half(d_middle.reshape(blk_items, tile_rows, OP * C))
        dw_outer = weight_grad(left_node, d_middle_half) / col_count
        d_left_node = input_grad(d_middle_half, w_outer)
        d_pair_rows = to_half(jnp.concatenate([d_left_node, d_right_sum], axis=-1))
        dw_ab = weight_grad(normed_node, d_pair_rows) / col_count
        d_normed_node = to_half(input_grad(d_pair_rows, w_ab))
        d_node_norm, dg_node = norm_back(node_full, g_node, d_normed_node.astype(jnp.float32))
        dg_node = dg_node / col_count
        grad_node = node_cot.astype(jnp.float32) + d_att_node + d_node_norm
        d_bias_full = d_bias_tile.astype(jnp.float32)
        grad_pair = grad_pair + jnp.einsum(
            "ghij,ch->gijc", d_bias_tile, w_bias, preferred_element_type=jnp.float32
        )
        dw_bias = jnp.einsum(
            "gijc,ghij->ch", pair_blk, d_bias_tile, preferred_element_type=jnp.float32
        )
        grad_dist = jnp.sum(d_bias_full * w_dist[None, :, None, None], axis=1)
        dw_dist = jnp.sum(d_bias_full * dist_blk[:, None, :, :], axis=(0, 2, 3))
        dw_qkv = jnp.zeros((D, 3 * D), jnp.float32)
        for part_index in range(3):
            dw_qkv = lax.dynamic_update_slice_in_dim(
                dw_qkv,
                dw_qkv_own[:, part_index * head_width : (part_index + 1) * head_width],
                part_index * D + head_start,
                1,
            )
        dw_node_out = lax.dynamic_update_slice_in_dim(
            jnp.zeros((D, D), jnp.float32), dwo_own, head_start, 0
        )
        grad_list = (
            dw_qkv,
            dw_bias,
            dw_dist,
            dw_node_out,
            dg_node,
            dw_ab,
            dw_outer,
            db_outer,
            jnp.stack([dg_tin_one, dg_tin_two]),
            jnp.stack([dw_tin_one, dw_tin_two]),
            jnp.stack([dg_tout_one, dg_tout_two]),
            jnp.stack([dw_tout_one, dw_tout_two]),
            dg_trans,
            dw_up,
            dw_down,
        )
        running = tuple((accum_sum + new_grad for accum_sum, new_grad in zip(running, grad_list)))
        return (running, (node_out, pair_four, grad_node, grad_pair, grad_dist))

    initial = tuple(
        (
            jnp.zeros(weight.shape, jnp.float32)
            for weight in (
                w_qkv,
                w_bias,
                w_dist,
                w_node_out,
                g_node,
                w_ab,
                w_outer,
                b_outer,
                g_tin,
                w_tin,
                g_tout,
                w_tout,
                g_trans,
                w_up,
                w_down,
            )
        )
    )
    block_inputs = tuple(
        (
            array_in.reshape((step_count, blk_items) + array_in.shape[1:])
            for array_in in (node_feats, pair_feats, distances, lengths, node_cotan, pair_cotan)
        )
    )
    running, outputs = lax.scan(run_block, initial, block_inputs)
    running = sum_weights(running)
    node_out = outputs[0].reshape(node_feats.shape)
    pair_out = outputs[1].reshape(pair_feats.shape)
    grad_node = outputs[2].reshape(node_feats.shape)
    grad_pair = outputs[3].reshape(pair_feats.shape)
    grad_dist = outputs[4].reshape(distances.shape)
    return (
        node_out,
        pair_out,
        grad_node,
        grad_pair,
        grad_dist,
        running[0],
        running[1],
        running[2],
        running[3],
        running[4],
        running[5],
        running[6],
        running[7],
        running[8],
        running[9],
        running[10],
        running[11],
        running[12],
        running[13],
        running[14],
    )


def solution(mesh):
    return jax.shard_map(
        per_device,
        mesh=mesh,
        in_specs=(
            P(None, "row", None),
            P(None, "row", "col", None),
            P(None, "row", "col"),
            P(),
            P(None, "row", None),
            P(None, "row", "col", None),
            P(),
            P(),
            P(),
            P(),
            P(),
            P(),
            P(),
            P(),
            P(),
            P(),
            P(),
            P(),
            P(),
            P(),
            P(),
        ),
        out_specs=(
            P(None, "row", None),
            P(None, "row", "col", None),
            P(None, "row", None),
            P(None, "row", "col", None),
            P(None, "row", "col"),
            P(),
            P(),
            P(),
            P(),
            P(),
            P(),
            P(),
            P(),
            P(),
            P(),
            P(),
            P(),
            P(),
            P(),
            P(),
        ),
        check_vma=False,
    )
```

profile of v0, /device:TPU:1, one launch (start us, length us, event | category | flops | bytes accessed | tf_op | source)
XLA Modules:
  0.0 2475.2 jit_solution(18379274945243947148)
XLA Ops:
  12.2 2281.8 %while.51 = (s32[]{:T(128)}, f32[256,768]{0,1:T(8,128)}, f32[128,8]{0,1:T(8,128)}, f32[8]{0:T(128)}, f32[256,256]{1,0:T(8,128)}, /*index=5*/f32[256]{0:T(256)}, ...) while((s32[]{:T(128)}, f32[256,768]{0,1:T(8,128)}, ...), condition=%wide.region_47.48_spmd.clone, body=%wide.region_0.47_spmd.clone.sunk | while | flops 6161991680 | bytes 832969984 | solution.py:448
  15.3 26.2 %all_gather.49 = bf16[2,384,32]{2,1,0:T(8,128)(2,1)S(1)} all-gather(bf16[2,24,32]{2,1,0:T(8,128)(2,1)S(1)} %slice.476), channel_id=1, replica_groups=mesh['row'=16,'col'=8] {'row'}, dimensions={1}, use_global_device_ids=true | all-gather | bytes 52224 | tf_op jit(solution)/shard_map/while/body/eval_jaxpr/all_gather | solution.py:187
  50.3 72.8 %all-gather.5.cloned.1.call-done = bf16[2,384,48,128]{3,2,1,0:T(8,128)(2,1)} async-done(((bf16[2,24,48,128]{3,2,1,0:T(8,128)(2,1)}), bf16[2,384,48,128]{3,2,1,0:T(8,128)(2,1)}) %all-gather.5.cloned.1.call-update) | async-done | bytes 9437200 | tf_op jit(solution)/shard_map/while/body/eval_jaxpr/all_gather | solution.py:221
  123.1 33.7 %copy.369 = bf16[2,384,48,128]{2,1,3,0:T(8,128)(2,1)} copy(bf16[2,384,48,128]{3,2,1,0:T(8,128)(2,1)} %all-gather.5.cloned.1.call-done) | data formatting | bytes 18874368 | tf_op jit(solution)/shard_map/while/body/eval_jaxpr/all_gather | solution.py:221
  156.9 19.5 convert_bitcast_fusion.10
  184.5 55.2 %reduce-scatter.11.cloned.1.call-done = bf16[48,2,24,128]{3,2,1,0:T(8,128)(2,1)} async-done(((bf16[384,2,24,128]{3,2,1,0:T(8,128)(2,1)}), bf16[48,2,24,128]{3,2,1,0:T(8,128)(2,1)}) %reduce-scatter.11.cloned.1.call-update) | async-done | bytes 589840 | tf_op jit(solution)/shard_map/while/body/eval_jaxpr/reduce_scatter | solution.py:224
  252.6 54.8 %all-gather.7.cloned.1.call-done = bf16[2,24,384,128]{3,2,1,0:T(8,128)(2,1)} async-done(((bf16[2,24,48,128]{3,2,1,0:T(8,128)(2,1)}), bf16[2,24,384,128]{3,2,1,0:T(8,128)(2,1)}) %all-gather.7.cloned.1.call-update) | async-done | bytes 4718608 | tf_op jit(solution)/shard_map/while/body/eval_jaxpr/all_gather | solution.py:236
  323.4 13.9 copy.374
  338.6 103.6 %reduce-scatter.13.cloned.1.call-done = bf16[24,2,48,128]{3,2,1,0:T(8,128)(2,1)} async-done(((bf16[384,2,48,128]{3,2,1,0:T(8,128)(2,1)}), bf16[24,2,48,128]{3,2,1,0:T(8,128)(2,1)}) %reduce-scatter.13.cloned.1.call-update) | async-done | bytes 589840 | tf_op jit(solution)/shard_map/while/body/eval_jaxpr/reduce_scatter | solution.py:239
  467.4 77.6 %all-gather.9.cloned.1.call-done = bf16[2,384,48,128]{3,2,0,1:T(8,128)(2,1)} async-done(((bf16[2,24,48,128]{3,2,0,1:T(8,128)(2,1)}), bf16[2,384,48,128]{3,2,0,1:T(8,128)(2,1)}) %all-gather.9.cloned.1.call-update) | async-done | bytes 9437200 | tf_op jit(solution)/shard_map/while/body/eval_jaxpr/all_gather | solution.py:266
  545.0 33.8 %copy.376 = bf16[2,384,48,128]{2,1,3,0:T(8,128)(2,1)} copy(bf16[2,384,48,128]{3,2,0,1:T(8,128)(2,1)} %all-gather.9.cloned.1.call-done) | data formatting | bytes 18874368 | tf_op jit(solution)/shard_map/while/body/eval_jaxpr/all_gather | solution.py:266
  578.8 19.5 fusion.525
  605.6 13.4 fusion.528
  621.6 39.6 %reduce-scatter.15.cloned.1.call-done = bf16[48,2,24,128]{3,0,2,1:T(8,128)(2,1)} async-done(((bf16[384,2,24,128]{3,0,2,1:T(8,128)(2,1)}), bf16[48,2,24,128]{3,0,2,1:T(8,128)(2,1)}) %reduce-scatter.15.cloned.1.call-update) | async-done | bytes 589840 | tf_op jit(solution)/shard_map/while/body/eval_jaxpr/reduce_scatter | solution.py:273
  697.1 25.1 %all_gather.48 = bf16[2,384,64]{2,1,0:T(8,128)(2,1)S(1)} all-gather(bf16[2,24,64]{2,1,0:T(8,128)(2,1)S(1)} %slice.475), channel_id=1, replica_groups=mesh['row'=16,'col'=8] {'row'}, dimensions={1}, use_global_device_ids=true | all-gather | bytes 104448 | tf_op jit(solution)/shard_map/while/body/eval_jaxpr/all_gather | solution.py:186
  726.2 21.8 all-gather.11.cloned.1.call-done
  764.6 13.9 copy.382
  778.5 11.8 copy.383
  805.5 74.6 %all-reduce.17.cloned.1.call-done = bf16[2,384,64]{2,0,1:T(2,128)(2,1)} async-done(((bf16[2,384,64]{2,0,1:T(2,128)(2,1)}), bf16[2,384,64]{2,0,1:T(2,128)(2,1)}) %all-reduce.17.cloned.1.call-update) | async-done | bytes 98320 | tf_op jit(solution)/shard_map/while
  894.1 16.4 fusion.536
  918.0 72.4 %reduce-scatter.17.cloned.1.call-done = bf16[24,12288]{1,0:T(8,128)(2,1)} async-done(((bf16[384,12288]{1,0:T(8,128)(2,1)}), bf16[24,12288]{1,0:T(8,128)(2,1)}) %reduce-scatter.17.cloned.1.call-update) | async-done | bytes 589840 | tf_op jit(solution)/shard_map/while
  1011.3 63.3 %all-reduce.9 = bf16[2,384,32]{2,1,0:T(8,128)(2,1)} all-reduce(bf16[2,384,32]{2,1,0:T(8,128)(2,1)S(1)} %fusion.544), channel_id=7, replica_groups=mesh['row'=16,'col'=8] {'row'}, use_global_device_ids=true, to_apply=%region_33.33.clone | all-reduce | flops 24576 | bytes 98304 | tf_op jit(solution)/shard_map/while
  1077.0 28.4 %all-reduce.10 = (bf16[2,24,32]{2,1,0:T(8,128)(2,1)S(1)}, bf16[2,24,256]{2,1,0:T(8,128)(2,1)S(1)}, bf16[2,24,256]{2,1,0:T(8,128)(2,1)S(1)}) all-reduce(bf16[2,24,32]{2,1,0:T(8,128)(2,1)S(1)} %constant_dynamic-slice_fusion.18, bf16[2,24,256]{2,1,0:T(8,128)(2,1)S(1)} %copy-done.78, ...), channel_id=1, replica_groups=mesh['row'=16,'col'=8] {'col'}, use_global_device_ids=true, to_apply=%region_34.34 | all-reduce | flops 26112 | bytes 104448 | tf_op jit(solution)/shard_map/while/body/eval_jaxpr/psum | solution.py:369
  1107.0 40.9 %all-reduce.19.cloned.1.call-done = bf16[2,24,4096]{2,1,0:T(8,128)(2,1)} async-done(((bf16[2,24,4096]{2,1,0:T(8,128)(2,1)}), bf16[2,24,4096]{2,1,0:T(8,128)(2,1)}) %all-reduce.19.cloned.1.call-update) | async-done | bytes 393232 | tf_op jit(solution)/shard_map/while/body/eval_jaxpr/psum | solution.py:368
  1154.7 29.8 %all_gather.49 = bf16[2,384,32]{2,1,0:T(8,128)(2,1)S(1)} all-gather(bf16[2,24,32]{2,1,0:T(8,128)(2,1)S(1)} %slice.476), channel_id=1, replica_groups=mesh['row'=16,'col'=8] {'row'}, dimensions={1}, use_global_device_ids=true | all-gather | bytes 52224 | tf_op jit(solution)/shard_map/while/body/eval_jaxpr/all_gather | solution.py:187
  1193.4 70.3 %all-gather.5.cloned.1.call-done = bf16[2,384,48,128]{3,2,1,0:T(8,128)(2,1)} async-done(((bf16[2,24,48,128]{3,2,1,0:T(8,128)(2,1)}), bf16[2,384,48,128]{3,2,1,0:T(8,128)(2,1)}) %all-gather.5.cloned.1.call-update) | async-done | bytes 9437200 | tf_op jit(solution)/shard_map/while/body/eval_jaxpr/all_gather | solution.py:221
  1263.6 33.7 %copy.369 = bf16[2,384,48,128]{2,1,3,0:T(8,128)(2,1)} copy(bf16[2,384,48,128]{3,2,1,0:T(8,128)(2,1)} %all-gather.5.cloned.1.call-done) | data formatting | bytes 18874368 | tf_op jit(solution)/shard_map/while/body/eval_jaxpr/all_gather | solution.py:221
  1297.4 19.5 convert_bitcast_fusion.10
  1325.0 55.2 %reduce-scatter.11.cloned.1.call-done = bf16[48,2,24,128]{3,2,1,0:T(8,128)(2,1)} async-done(((bf16[384,2,24,128]{3,2,1,0:T(8,128)(2,1)}), bf16[48,2,24,128]{3,2,1,0:T(8,128)(2,1)}) %reduce-scatter.11.cloned.1.call-update) | async-done | bytes 589840 | tf_op jit(solution)/shard_map/while/body/eval_jaxpr/reduce_scatter | solution.py:224
  1393.1 54.8 %all-gather.7.cloned.1.call-done = bf16[2,24,384,128]{3,2,1,0:T(8,128)(2,1)} async-done(((bf16[2,24,48,128]{3,2,1,0:T(8,128)(2,1)}), bf16[2,24,384,128]{3,2,1,0:T(8,128)(2,1)}) %all-gather.7.cloned.1.call-update) | async-done | bytes 4718608 | tf_op jit(solution)/shard_map/while/body/eval_jaxpr/all_gather | solution.py:236
  1463.9 13.9 copy.374
  1479.1 103.6 %reduce-scatter.13.cloned.1.call-done = bf16[24,2,48,128]{3,2,1,0:T(8,128)(2,1)} async-done(((bf16[384,2,48,128]{3,2,1,0:T(8,128)(2,1)}), bf16[24,2,48,128]{3,2,1,0:T(8,128)(2,1)}) %reduce-scatter.13.cloned.1.call-update) | async-done | bytes 589840 | tf_op jit(solution)/shard_map/while/body/eval_jaxpr/reduce_scatter | solution.py:239
  1607.9 77.6 %all-gather.9.cloned.1.call-done = bf16[2,384,48,128]{3,2,0,1:T(8,128)(2,1)} async-done(((bf16[2,24,48,128]{3,2,0,1:T(8,128)(2,1)}), bf16[2,384,48,128]{3,2,0,1:T(8,128)(2,1)}) %all-gather.9.cloned.1.call-update) | async-done | bytes 9437200 | tf_op jit(solution)/shard_map/while/body/eval_jaxpr/all_gather | solution.py:266
  1685.5 33.8 %copy.376 = bf16[2,384,48,128]{2,1,3,0:T(8,128)(2,1)} copy(bf16[2,384,48,128]{3,2,0,1:T(8,128)(2,1)} %all-gather.9.cloned.1.call-done) | data formatting | bytes 18874368 | tf_op jit(solution)/shard_map/while/body/eval_jaxpr/all_gather | solution.py:266
  1719.3 19.5 fusion.525
  1746.1 13.4 fusion.528
  1762.2 39.6 %reduce-scatter.15.cloned.1.call-done = bf16[48,2,24,128]{3,0,2,1:T(8,128)(2,1)} async-done(((bf16[384,2,24,128]{3,0,2,1:T(8,128)(2,1)}), bf16[48,2,24,128]{3,0,2,1:T(8,128)(2,1)}) %reduce-scatter.15.cloned.1.call-update) | async-done | bytes 589840 | tf_op jit(solution)/shard_map/while/body/eval_jaxpr/reduce_scatter | solution.py:273
  1837.7 25.1 %all_gather.48 = bf16[2,384,64]{2,1,0:T(8,128)(2,1)S(1)} all-gather(bf16[2,24,64]{2,1,0:T(8,128)(2,1)S(1)} %slice.475), channel_id=1, replica_groups=mesh['row'=16,'col'=8] {'row'}, dimensions={1}, use_global_device_ids=true | all-gather | bytes 104448 | tf_op jit(solution)/shard_map/while/body/eval_jaxpr/all_gather | solution.py:186
  1866.7 21.8 all-gather.11.cloned.1.call-done
  1905.1 13.9 copy.382
  1947.0 73.6 %all-reduce.17.cloned.1.call-done = bf16[2,384,64]{2,0,1:T(2,128)(2,1)} async-done(((bf16[2,384,64]{2,0,1:T(2,128)(2,1)}), bf16[2,384,64]{2,0,1:T(2,128)(2,1)}) %all-reduce.17.cloned.1.call-update) | async-done | bytes 98320 | tf_op jit(solution)/shard_map/while
  2035.2 16.4 fusion.536
  2059.0 71.7 %reduce-scatter.17.cloned.1.call-done = bf16[24,12288]{1,0:T(8,128)(2,1)} async-done(((bf16[384,12288]{1,0:T(8,128)(2,1)}), bf16[24,12288]{1,0:T(8,128)(2,1)}) %reduce-scatter.17.cloned.1.call-update) | async-done | bytes 589840 | tf_op jit(solution)/shard_map/while
  2151.7 63.3 %all-reduce.9 = bf16[2,384,32]{2,1,0:T(8,128)(2,1)} all-reduce(bf16[2,384,32]{2,1,0:T(8,128)(2,1)S(1)} %fusion.544), channel_id=7, replica_groups=mesh['row'=16,'col'=8] {'row'}, use_global_device_ids=true, to_apply=%region_33.33.clone | all-reduce | flops 24576 | bytes 98304 | tf_op jit(solution)/shard_map/while
  2217.4 28.4 %all-reduce.10 = (bf16[2,24,32]{2,1,0:T(8,128)(2,1)S(1)}, bf16[2,24,256]{2,1,0:T(8,128)(2,1)S(1)}, bf16[2,24,256]{2,1,0:T(8,128)(2,1)S(1)}) all-reduce(bf16[2,24,32]{2,1,0:T(8,128)(2,1)S(1)} %constant_dynamic-slice_fusion.18, bf16[2,24,256]{2,1,0:T(8,128)(2,1)S(1)} %copy-done.78, ...), channel_id=1, replica_groups=mesh['row'=16,'col'=8] {'col'}, use_global_device_ids=true, to_apply=%region_34.34 | all-reduce | flops 26112 | bytes 104448 | tf_op jit(solution)/shard_map/while/body/eval_jaxpr/psum | solution.py:369
  2247.4 40.8 %all-reduce.19.cloned.1.call-done = bf16[2,24,4096]{2,1,0:T(8,128)(2,1)} async-done(((bf16[2,24,4096]{2,1,0:T(8,128)(2,1)}), bf16[2,24,4096]{2,1,0:T(8,128)(2,1)}) %all-reduce.19.cloned.1.call-update) | async-done | bytes 393232 | tf_op jit(solution)/shard_map/while/body/eval_jaxpr/psum | solution.py:368
  2297.1 69.4 %all-reduce.3 = (f32[128,8]{0,1:T(8,128)}, f32[8]{0:T(128)}, f32[256]{0:T(256)}, f32[128]{0:T(128)}, f32[2,128]{1,0:T(2,128)}, /*index=5*/f32[2,128]{1,0:T(2,128)}, f32[128]{0:T(128)}) all-reduce(f32[128,8]{0,1:T(8,128)S(1)} %copy-done.105, f32[8]{0:T(128)S(1)} %copy-done.137, ...), channel_id=1, replica_groups=mesh['row'=16,'col'=8] {'row','col'}, use_global_device_ids=true, to_apply=%region_49.50 | all-reduce | flops 2056 | bytes 16448 | tf_op jit(solution)/shard_map/psum | solution.py:55
  2366.5 93.7 %all-reduce.15.cloned.1.call-done = (f32[256,768]{1,0:T(8,128)}, f32[256,256]{1,0:T(8,128)}, f32[256,64]{0,1:T(8,128)}, f32[32,4096]{1,0:T(8,128)}, f32[2,128,64...) async-done(((f32[256,768]{1,0:T(8,128)}, f32[256,256]{1,0:T(8,128)}, f32[256,64]{0,1:T(8,128)}, f32[32,4096]{1,0:T(8,128)}, ...) | async-done | bytes 2949136 | tf_op jit(solution)/shard_map/psum | solution.py:55
  (979 shorter events, 436.1 us)
Async XLA Ops:
  12.2 110.9 %all-gather.5.cloned.1.call-start = ((), (), s32[]{:S(2)}) async-start(), calls=%async_computation.8 | async-start | bytes 10027008 | tf_op jit(solution)/shard_map/while/body/eval_jaxpr/all_gather | solution.py:221
  48.6 191.1 %reduce-scatter.11.cloned.1.call-start = ((), (), s32[]{:S(2)}) async-start(), calls=%async_computation.9 | async-start | bytes 5308416 | tf_op jit(solution)/shard_map/while/body/eval_jaxpr/reduce_scatter | solution.py:224
  183.8 59.3 %copy-start.145 = (bf16[2,128,128]{2,1,0:T(8,128)(2,1)S(1)}, bf16[2,128,128]{2,1,0:T(8,128)(2,1)}, u32[]{:S(2)}) copy-start(bf16[2,128,128]{2,1,0:T(8,128)(2,1)} %get-tuple-element.1572) | copy-start | bytes 196612 | tf_op jit(solution)/shard_map/while
  183.8 123.5 %all-gather.7.cloned.1.call-start = ((), (), s32[]{:S(2)}) async-start(), calls=%async_computation.10 | async-start | bytes 5308416 | tf_op jit(solution)/shard_map/while/body/eval_jaxpr/all_gather | solution.py:236
  184.5 280.3 %copy-start.109 = (f32[128]{0:T(128)}, f32[128]{0:T(128)S(1)}, u32[]{:S(2)}) copy-start(f32[128]{0:T(128)S(1)} %get-tuple-element.1371) | copy-start | bytes 1540 | tf_op jit(solution)/shard_map/while
  184.5 502.3 %copy-start.107 = (f32[128]{0:T(128)}, f32[128]{0:T(128)S(1)}, u32[]{:S(2)}) copy-start(f32[128]{0:T(128)S(1)} %get-tuple-element.1365) | copy-start | bytes 1540 | tf_op jit(solution)/shard_map/while
  241.3 445.5 %copy-start.47 = (f32[2,24,48]{2,1,0:T(8,128)}, f32[2,24,48]{2,1,0:T(8,128)S(1)}, u32[]{:S(2)}) copy-start(f32[2,24,48]{2,1,0:T(8,128)S(1)} %broadcast_multiply_fusion.17) | copy-start | bytes 27652 | tf_op jit(solution)/shard_map/while
  250.8 191.4 %reduce-scatter.13.cloned.1.call-start = ((), (), s32[]{:S(2)}) async-start(), calls=%async_computation.11 | async-start | bytes 10027008 | tf_op jit(solution)/shard_map/while/body/eval_jaxpr/reduce_scatter | solution.py:239
  337.3 207.7 %all-gather.9.cloned.1.call-start = ((), (), s32[]{:S(2)}) async-start(), calls=%async_computation.12 | async-start | bytes 10027008 | tf_op jit(solution)/shard_map/while/body/eval_jaxpr/all_gather | solution.py:266
  338.6 114.3 %copy-start.26 = (bf16[1,2,24,48,128]{4,3,2,1,0:T(8,128)(2,1)}, bf16[1,2,24,48,128]{4,3,2,1,0:T(8,128)(2,1)S(1)}, u32[]{:S(2)}) copy-start(bf16[1,2,24,48,128]{4,3,2,1,0:T(8,128)(2,1)S(1)} %constant_dynamic-slice_fusion.17) | copy-start | bytes 1769476 | tf_op jit(solution)/shard_map/while
  467.3 193.9 %reduce-scatter.15.cloned.1.call-start = ((), (), s32[]{:S(2)}) async-start(), calls=%async_computation.13 | async-start | bytes 5308416 | tf_op jit(solution)/shard_map/while/body/eval_jaxpr/reduce_scatter | solution.py:273
  605.3 142.6 %all-gather.11.cloned.1.call-start = ((), (), s32[]{:S(2)}) async-start(), calls=%async_computation.14 | async-start | bytes 5308416 | tf_op jit(solution)/shard_map/while/body/eval_jaxpr/all_gather | solution.py:291
  692.7 29.6 %all-to-all-start = ((bf16[8,2,1152]{2,1,0:T(2,128)(2,1)}), bf16[8,2,1152]{2,1,0:T(2,128)(2,1)S(1)}, u32[]{:S(2)}, u32[]{:S(2)}) async-start(bf16[8,2,1152]{2,1,0:T(2,128)(2,1)} %reshape.610), calls=%async_computation | async-start | bytes 73728 | tf_op jit(solution)/shard_map/while/body/eval_jaxpr/all_to_all | solution.py:193
  696.1 184.1 %all-reduce.17.cloned.1.call-start = ((), (), s32[]{:S(2)}) async-start(), calls=%async_computation.7 | async-start | bytes 393216 | tf_op jit(solution)/shard_map/while
  725.7 264.6 %reduce-scatter.17.cloned.1.call-start = ((), (), s32[]{:S(2)}) async-start(), calls=%async_computation.15 | async-start | bytes 10027008 | tf_op jit(solution)/shard_map/while
  793.2 8.6 all-to-all-start.1
  796.5 351.3 %all-reduce.19.cloned.1.call-start = ((), (), s32[]{:S(2)}) async-start(), calls=%async_computation.16 | async-start | bytes 786432 | tf_op jit(solution)/shard_map/while/body/eval_jaxpr/psum | solution.py:368
  802.0 79.3 %copy-start.57 = (bf16[256,96]{0,1:T(8,128)(2,1)S(1)}, bf16[256,96]{0,1:T(8,128)(2,1)}, u32[]{:S(2)}) copy-start(bf16[256,96]{0,1:T(8,128)(2,1)} %get-tuple-element.1550) | copy-start | bytes 147460 | tf_op jit(solution)/shard_map/while
  805.5 76.9 %copy-start.104 = (f32[128,8]{0,1:T(8,128)}, f32[128,8]{0,1:T(8,128)S(1)}, u32[]{:S(2)}) copy-start(f32[128,8]{0,1:T(8,128)S(1)} %fusion.502) | copy-start | bytes 12292 | tf_op jit(solution)/shard_map/while
  1011.3 64.3 %copy-start.37 = (f32[2,128,640]{2,1,0:T(8,128)S(1)}, f32[2,128,640]{2,1,0:T(8,128)}, u32[]{:S(2)}) copy-start(f32[2,128,640]{2,1,0:T(8,128)} %get-tuple-element.1483) | copy-start | bytes 1966084 | tf_op jit(solution)/shard_map/while
  1105.5 44.5 %copy-start.121 = (f32[256]{0:T(256)S(1)}, f32[256]{0:T(256)}, u32[]{:S(2)}) copy-start(f32[256]{0:T(256)} %get-tuple-element.1478) | copy-start | bytes 3076 | tf_op jit(solution)/shard_map/while
  1105.5 44.6 %copy-start.83 = (bf16[2,2,24,256]{3,2,1,0:T(8,128)(2,1)S(1)}, bf16[2,2,24,256]{3,2,1,0:T(8,128)(2,1)}, u32[]{:S(2)}) copy-start(bf16[2,2,24,256]{3,2,1,0:T(8,128)(2,1)} %get-tuple-element.1556) | copy-start | bytes 147460 | tf_op jit(solution)/shard_map/while
  1105.5 44.6 %copy-start.141 = (f32[2,2,24,256]{3,2,1,0:T(8,128)S(1)}, f32[2,2,24,256]{3,2,1,0:T(8,128)}, u32[]{:S(2)}) copy-start(f32[2,2,24,256]{3,2,1,0:T(8,128)} %get-tuple-element.1491) | copy-start | bytes 294916 | tf_op jit(solution)/shard_map/while
  1105.5 44.6 %copy-start.143 = (f32[2,2,24,256]{3,2,1,0:T(8,128)S(1)}, f32[2,2,24,256]{3,2,1,0:T(8,128)}, u32[]{:S(2)}) copy-start(f32[2,2,24,256]{3,2,1,0:T(8,128)} %get-tuple-element.1489) | copy-start | bytes 294916 | tf_op jit(solution)/shard_map/while
  1151.6 112.0 %all-gather.5.cloned.1.call-start = ((), (), s32[]{:S(2)}) async-start(), calls=%async_computation.8 | async-start | bytes 10027008 | tf_op jit(solution)/shard_map/while/body/eval_jaxpr/all_gather | solution.py:221
  1191.6 188.6 %reduce-scatter.11.cloned.1.call-start = ((), (), s32[]{:S(2)}) async-start(), calls=%async_computation.9 | async-start | bytes 5308416 | tf_op jit(solution)/shard_map/while/body/eval_jaxpr/reduce_scatter | solution.py:224
  1324.4 59.3 %copy-start.145 = (bf16[2,128,128]{2,1,0:T(8,128)(2,1)S(1)}, bf16[2,128,128]{2,1,0:T(8,128)(2,1)}, u32[]{:S(2)}) copy-start(bf16[2,128,128]{2,1,0:T(8,128)(2,1)} %get-tuple-element.1572) | copy-start | bytes 196612 | tf_op jit(solution)/shard_map/while
  1324.4 123.5 %all-gather.7.cloned.1.call-start = ((), (), s32[]{:S(2)}) async-start(), calls=%async_computation.10 | async-start | bytes 5308416 | tf_op jit(solution)/shard_map/while/body/eval_jaxpr/all_gather | solution.py:236
  1325.0 280.3 %copy-start.109 = (f32[128]{0:T(128)}, f32[128]{0:T(128)S(1)}, u32[]{:S(2)}) copy-start(f32[128]{0:T(128)S(1)} %get-tuple-element.1371) | copy-start | bytes 1540 | tf_op jit(solution)/shard_map/while
  1325.0 502.3 %copy-start.107 = (f32[128]{0:T(128)}, f32[128]{0:T(128)S(1)}, u32[]{:S(2)}) copy-start(f32[128]{0:T(128)S(1)} %get-tuple-element.1365) | copy-start | bytes 1540 | tf_op jit(solution)/shard_map/while
  1381.8 445.5 %copy-start.47 = (f32[2,24,48]{2,1,0:T(8,128)}, f32[2,24,48]{2,1,0:T(8,128)S(1)}, u32[]{:S(2)}) copy-start(f32[2,24,48]{2,1,0:T(8,128)S(1)} %broadcast_multiply_fusion.17) | copy-start | bytes 27652 | tf_op jit(solution)/shard_map/while
  1391.3 191.4 %reduce-scatter.13.cloned.1.call-start = ((), (), s32[]{:S(2)}) async-start(), calls=%async_computation.11 | async-start | bytes 10027008 | tf_op jit(solution)/shard_map/while/body/eval_jaxpr/reduce_scatter | solution.py:239
  1477.8 207.7 %all-gather.9.cloned.1.call-start = ((), (), s32[]{:S(2)}) async-start(), calls=%async_computation.12 | async-start | bytes 10027008 | tf_op jit(solution)/shard_map/while/body/eval_jaxpr/all_gather | solution.py:266
  1479.1 114.3 %copy-start.26 = (bf16[1,2,24,48,128]{4,3,2,1,0:T(8,128)(2,1)}, bf16[1,2,24,48,128]{4,3,2,1,0:T(8,128)(2,1)S(1)}, u32[]{:S(2)}) copy-start(bf16[1,2,24,48,128]{4,3,2,1,0:T(8,128)(2,1)S(1)} %constant_dynamic-slice_fusion.17) | copy-start | bytes 1769476 | tf_op jit(solution)/shard_map/while
  1607.8 193.9 %reduce-scatter.15.cloned.1.call-start = ((), (), s32[]{:S(2)}) async-start(), calls=%async_computation.13 | async-start | bytes 5308416 | tf_op jit(solution)/shard_map/while/body/eval_jaxpr/reduce_scatter | solution.py:273
  1745.9 142.6 %all-gather.11.cloned.1.call-start = ((), (), s32[]{:S(2)}) async-start(), calls=%async_computation.14 | async-start | bytes 5308416 | tf_op jit(solution)/shard_map/while/body/eval_jaxpr/all_gather | solution.py:291
  1833.2 29.6 %all-to-all-start = ((bf16[8,2,1152]{2,1,0:T(2,128)(2,1)}), bf16[8,2,1152]{2,1,0:T(2,128)(2,1)S(1)}, u32[]{:S(2)}, u32[]{:S(2)}) async-start(bf16[8,2,1152]{2,1,0:T(2,128)(2,1)} %reshape.610), calls=%async_computation | async-start | bytes 73728 | tf_op jit(solution)/shard_map/while/body/eval_jaxpr/all_to_all | solution.py:193
  1836.6 184.0 %all-reduce.17.cloned.1.call-start = ((), (), s32[]{:S(2)}) async-start(), calls=%async_computation.7 | async-start | bytes 393216 | tf_op jit(solution)/shard_map/while
  1866.3 264.5 %reduce-scatter.17.cloned.1.call-start = ((), (), s32[]{:S(2)}) async-start(), calls=%async_computation.15 | async-start | bytes 10027008 | tf_op jit(solution)/shard_map/while
  1933.7 8.8 all-to-all-start.1
  1937.0 351.2 %all-reduce.19.cloned.1.call-start = ((), (), s32[]{:S(2)}) async-start(), calls=%async_computation.16 | async-start | bytes 786432 | tf_op jit(solution)/shard_map/while/body/eval_jaxpr/psum | solution.py:368
  1942.8 79.0 %copy-start.57 = (bf16[256,96]{0,1:T(8,128)(2,1)S(1)}, bf16[256,96]{0,1:T(8,128)(2,1)}, u32[]{:S(2)}) copy-start(bf16[256,96]{0,1:T(8,128)(2,1)} %get-tuple-element.1550) | copy-start | bytes 147460 | tf_op jit(solution)/shard_map/while
  1946.9 75.9 %copy-start.104 = (f32[128,8]{0,1:T(8,128)}, f32[128,8]{0,1:T(8,128)S(1)}, u32[]{:S(2)}) copy-start(f32[128,8]{0,1:T(8,128)S(1)} %fusion.502) | copy-start | bytes 12292 | tf_op jit(solution)/shard_map/while
  2151.7 64.3 %copy-start.37 = (f32[2,128,640]{2,1,0:T(8,128)S(1)}, f32[2,128,640]{2,1,0:T(8,128)}, u32[]{:S(2)}) copy-start(f32[2,128,640]{2,1,0:T(8,128)} %get-tuple-element.1483) | copy-start | bytes 1966084 | tf_op jit(solution)/shard_map/while
  2245.9 44.5 %copy-start.83 = (bf16[2,2,24,256]{3,2,1,0:T(8,128)(2,1)S(1)}, bf16[2,2,24,256]{3,2,1,0:T(8,128)(2,1)}, u32[]{:S(2)}) copy-start(bf16[2,2,24,256]{3,2,1,0:T(8,128)(2,1)} %get-tuple-element.1556) | copy-start | bytes 147460 | tf_op jit(solution)/shard_map/while
  2246.0 44.5 %copy-start.141 = (f32[2,2,24,256]{3,2,1,0:T(8,128)S(1)}, f32[2,2,24,256]{3,2,1,0:T(8,128)}, u32[]{:S(2)}) copy-start(f32[2,2,24,256]{3,2,1,0:T(8,128)} %get-tuple-element.1491) | copy-start | bytes 294916 | tf_op jit(solution)/shard_map/while
  2246.0 44.5 %copy-start.143 = (f32[2,2,24,256]{3,2,1,0:T(8,128)S(1)}, f32[2,2,24,256]{3,2,1,0:T(8,128)}, u32[]{:S(2)}) copy-start(f32[2,2,24,256]{3,2,1,0:T(8,128)} %get-tuple-element.1489) | copy-start | bytes 294916 | tf_op jit(solution)/shard_map/while
  2294.0 166.2 %all-reduce.15.cloned.1.call-start = ((), (), s32[]{:S(2)}) async-start(), calls=%async_computation.6 | async-start | bytes 5898240 | tf_op jit(solution)/shard_map/psum | solution.py:55
  (263 other events, 2321.2 us)
Sparse Core Ops, SparseCore 0:
  48.7 74.3 all-gather.4
  184.0 55.7 reduce-scatter.10
  250.9 56.3 all-gather.6
  337.4 104.7 reduce-scatter.12
  467.4 77.4 all-gather.8
  605.5 55.7 reduce-scatter.14
  689.7 58.2 all-gather.10
  750.6 129.5 all-reduce.16
  884.5 105.7 reduce-scatter.16
  1075.7 72.1 all-reduce.18
  1191.7 71.8 all-gather.4
  1324.5 55.7 reduce-scatter.10
  1391.4 56.3 all-gather.6
  1478.0 104.7 reduce-scatter.12
  1608.0 77.4 all-gather.8
  1746.0 55.7 reduce-scatter.14
  1830.2 58.2 all-gather.10
  1891.0 129.5 all-reduce.16
  2025.0 105.7 reduce-scatter.16
  2216.1 72.0 all-reduce.18
Sparse Core Ops, SparseCore 1:
  2301.6 158.5 all-reduce.14
where the time goes:
time: 2480 us
  waiting for transfers between devices  1320 us (53%)
  blocking collectives  359 us (14%)
  local copies, waits for them, and re-layouts  347 us (14%)
  matrix products  269 us (11%)
  other arithmetic  139 us (6%)
    while x24, waiting for transfers between devices  293 us
    reduce_scatter x2, waiting for transfers between devices, run_block(): lax.psum_scatter(jnp.einsum('gkic,gkjc->igjc', slab_piece, right_two, pre...  207 us
    all_gather x2, waiting for transfers between devices, run_block(): dprod_rows = lax.all_gather(d_prod_two, 'row', axis=1, tiled=True)  155 us
    all_gather x2, waiting for transfers between devices, run_block(): right_slab = lax.all_gather(right_one, 'row', axis=1, tiled=True)  143 us
    while x2, blocking collectives  127 us
    reduce_scatter x2, waiting for transfers between devices, run_block(): lax.psum_scatter(jnp.einsum('gikc,gjkc->jgic', left_one, slab_piece, pref...  110 us
    all_gather x2, waiting for transfers between devices, run_block(): left_slab = lax.all_gather(left_two, 'col', axis=2, tiled=True)  110 us
    psum x1, waiting for transfers between devices, sum_weights(): lax.psum((grad_list[0], grad_list[1], grad_list[2], grad_list[3], grad_li...  93.7 us
  transfers between devices with their start and end apart: 25, of which 23 were waited for; matrix products, arithmetic and copies ran while one was open for 9% of the time, Pallas kernels for 0%

commit v1 on v0

v1 whole, which is shorter than its diff:
```python
import jax
import jax.numpy as jnp
from jax import lax
from jax.experimental import pallas as pl
from jax.experimental.pallas import tpu as pltpu
from jax.sharding import PartitionSpec as P

D = 256
C = 128
H = 8
HD = 32
CH = 128
OP = 32
FT = 512
ITEMS = 4
EPS = 1e-05
BOTH = ("row", "col")
F32 = jnp.float32
BF16 = jnp.bfloat16
HALF = 64
JH = 3
STEP_ROWS = 6
VMEM = 60 * 1024 * 1024


def half(values):
    return values.astype(BF16)


def dot(lhs, rhs, lhs_dim, rhs_dim):
    return lax.dot_general(
        lhs, rhs, (((lhs_dim,), (rhs_dim,)), ((), ())), preferred_element_type=F32
    )


def sigmoid(values):
    return 0.5 * jnp.tanh(0.5 * values) + 0.5


def norm_parts(values):
    scale = 1.0 / values.shape[0]
    centered = values - jnp.sum(values, axis=0, keepdims=True) * scale
    spread = jnp.sum(centered * centered, axis=0, keepdims=True) * scale
    inv = lax.rsqrt(spread + EPS)
    return centered * inv, inv


def norm_back(unit, inv, gain, grad):
    scale = 1.0 / unit.shape[0]
    scaled = grad * gain
    first = jnp.sum(scaled, axis=0, keepdims=True) * scale
    second = jnp.sum(scaled * unit, axis=0, keepdims=True) * scale
    return inv * (scaled - first - unit * second)


def fold(values):
    total = values[:, :128]
    for start in range(128, values.shape[1], 128):
        total = total + values[:, start : start + 128]
    return total


def tile_rows_of(ref):
    items, parts, rows = ref.shape[:3]
    return jnp.concatenate(
        [ref[b, h, m] for m in range(rows) for h in range(parts) for b in range(items)], axis=0
    )


def put_tile(ref, values):
    items, parts, rows, cols = ref.shape[:4]
    flipped = jnp.transpose(values)
    start = 0
    for m in range(rows):
        for h in range(parts):
            for b in range(items):
                ref[b, h, m] = flipped[start : start + cols]
                start += cols


def low_lanes(rows):
    return lax.broadcasted_iota(jnp.int32, (rows, 128), 1) < HALF


def swap(values):
    return pltpu.roll(values, HALF, 1)


def lane_row(values, m):
    return values[:, m * 128 : (m + 1) * 128]


def put_rows(ref, values):
    for m in range(ref.shape[0]):
        ref[m] = lane_row(values, m)


def get_rows(ref):
    return jnp.concatenate([ref[m] for m in range(ref.shape[0])], axis=1)


def put_double(ref, left, right):
    low = low_lanes(left.shape[0])
    for m in range(ref.shape[2]):
        one, two = lane_row(left, m), lane_row(right, m)
        ref[0, 0, m] = half(jnp.where(low, one, swap(two)))
        ref[0, 1, m] = half(jnp.where(low, swap(one), two))


def get_double(ref):
    low = low_lanes(ref.shape[3])
    left, right = [], []
    for m in range(ref.shape[2]):
        one, two = ref[0, 0, m].astype(F32), ref[0, 1, m].astype(F32)
        left.append(jnp.where(low, one, swap(two)))
        right.append(jnp.where(low, swap(one), two))
    return jnp.concatenate(left, axis=1), jnp.concatenate(right, axis=1)


def add_to(ref, values):
    @pl.when(pl.program_id(0) == 0)
    def _():
        ref[...] = values

    @pl.when(pl.program_id(0) != 0)
    def _():
        ref[...] += values


def enter_kernel(pair_ref, eye_ref, wb_ref, wd_ref, dist_ref, x_ref, bias_ref):
    rows = tile_rows_of(pair_ref)
    x_ref[...] = half(dot(eye_ref[...], rows, 1, 1))
    bias_ref[...] = half(dot(wb_ref[...], rows, 1, 1) + wd_ref[...] * dist_ref[...])


def front(values, gain, w_in, keep, sides_ref):
    unit, _ = norm_parts(values)
    proj = dot(w_in, half(unit * gain), 1, 0)
    put_double(
        sides_ref,
        sigmoid(proj[CH : 2 * CH]) * proj[:CH] * keep,
        sigmoid(proj[3 * CH :]) * proj[2 * CH : 3 * CH] * keep,
    )


def open_kernel(
    x_ref, mid_ref, bd_ref, bout_ref, keep_ref, gain_ref, w_ref, one_ref, sides_ref
):
    keep = keep_ref[...]
    outer = jnp.concatenate(
        [dot(mid_ref[p], bd_ref[0], 0, 0) for p in range(mid_ref.shape[0])], axis=1
    )
    pair_one = x_ref[...].astype(F32) + keep * (outer + bout_ref[...])
    one_ref[...] = pair_one
    front(pair_one, gain_ref[...], w_ref[: 4 * CH], keep, sides_ref)


def middle_kernel(
    one_ref,
    prod_ref,
    keep_ref,
    gin0_ref,
    wog_ref,
    gout_ref,
    wout_ref,
    gin1_ref,
    w1_ref,
    two_ref,
    sides_ref,
):
    pair_one = one_ref[...]
    unit, _ = norm_parts(pair_one)
    gate = sigmoid(dot(wog_ref[...], half(unit * gin0_ref[...]), 1, 0))
    prod_unit, _ = norm_parts(get_rows(prod_ref).astype(F32))
    update = dot(wout_ref[...], half(prod_unit * gout_ref[...]), 1, 0)
    pair_two = pair_one + gate * update
    two_ref[...] = pair_two
    front(pair_two, gin1_ref[...], w1_ref[: 4 * CH], keep_ref[...], sides_ref)


def rear_back(grad, gate, update, y_half, prod_unit, prod_inv, gout, wout_plain):
    d_update = half(grad * gate)
    dw_out = dot(d_update, y_half, 1, 1)
    d_y = half(dot(wout_plain, d_update, 1, 0)).astype(F32)
    d_prod = half(norm_back(prod_unit, prod_inv, gout, d_y))
    d_og = half(grad * update * gate * (1.0 - gate))
    return d_prod, d_og, dw_out, fold(d_y * prod_unit)


def turn_kernel(
    two_ref,
    prod_ref,
    cot_ref,
    eye_ref,
    gin_ref,
    wog_ref,
    gout_ref,
    wout_ref,
    wout_plain_ref,
    gtr_ref,
    wup_ref,
    wup_plain_ref,
    wdown_ref,
    wdown_plain_ref,
    out_ref,
    grad_ref,
    dprod_ref,
    dog_ref,
    dwdown_ref,
    dwup_ref,
    dgtr_ref,
    dwout_ref,
    dgout_ref,
):
    pair_two = two_ref[...]
    unit, _ = norm_parts(pair_two)
    gate = sigmoid(dot(wog_ref[...], half(unit * gin_ref[...]), 1, 0))
    prod_unit, prod_inv = norm_parts(get_rows(prod_ref).astype(F32))
    y_half = half(prod_unit * gout_ref[...])
    update = dot(wout_ref[...], y_half, 1, 0)
    pair_three = pair_two + gate * update
    tr_unit, tr_inv = norm_parts(pair_three)
    xt = half(tr_unit * gtr_ref[...])
    hidden = dot(wup_ref[...], xt, 1, 0)
    sig = sigmoid(hidden)
    act32 = hidden * sig
    active = half(act32)
    put_tile(out_ref, pair_three + dot(wdown_ref[...], active, 1, 0))
    cot32 = dot(eye_ref[...], tile_rows_of(cot_ref), 1, 1)
    cot = half(cot32)
    add_to(dwdown_ref, dot(active, cot, 1, 1))
    d_active = half(dot(wdown_plain_ref[...], cot, 1, 0)).astype(F32)
    d_hidden = half(d_active * (sig + act32 * (1.0 - sig)))
    add_to(dwup_ref, dot(d_hidden, xt, 1, 1))
    d_xt = half(dot(wup_plain_ref[...], d_hidden, 1, 0)).astype(F32)
    add_to(dgtr_ref, fold(d_xt * tr_unit))
    grad = cot32 + norm_back(tr_unit, tr_inv, gtr_ref[...], d_xt)
    grad_ref[...] = grad
    d_prod, d_og, dw_out, dg_out = rear_back(
        grad, gate, update, y_half, prod_unit, prod_inv, gout_ref[...], wout_plain_ref[...]
    )
    put_rows(dprod_ref, d_prod)
    dog_ref[...] = d_og
    add_to(dwout_ref, dw_out)
    add_to(dgout_ref, dg_out)


def front_back(values, keep, gain, w_in, w_plain, sides_ref, d_og, dw_ref, dg_ref):
    unit, inv = norm_parts(values)
    normed = half(unit * gain)
    proj = dot(w_in[: 4 * CH], normed, 1, 0)
    sig_left = sigmoid(proj[CH : 2 * CH])
    sig_right = sigmoid(proj[3 * CH :])
    d_left, d_right = get_double(sides_ref)
    left = d_left * keep * sig_left
    right = d_right * keep * sig_right
    d_proj = jnp.concatenate(
        [
            half(left),
            half(left * proj[:CH] * (1.0 - sig_left)),
            half(right),
            half(right * proj[2 * CH : 3 * CH] * (1.0 - sig_right)),
            d_og,
        ],
        axis=0,
    )
    add_to(dw_ref, dot(d_proj, normed, 1, 1))
    d_normed = half(dot(w_plain, d_proj, 1, 0)).astype(F32)
    add_to(dg_ref, fold(d_normed * unit))
    return norm_back(unit, inv, gain, d_normed)


def back_kernel(
    two_ref,
    one_ref,
    prod_ref,
    dsides_ref,
    dog_ref,
    grad_ref,
    keep_ref,
    gin1_ref,
    w1_ref,
    w1_plain_ref,
    gin0_ref,
    wog_ref,
    gout_ref,
    wout_ref,
    wout_plain_ref,
    grad_out_ref,
    dprod_ref,
    dog_out_ref,
    dwin_ref,
    dgin_ref,
    dwout_ref,
    dgout_ref,
):
    grad = grad_ref[...] + front_back(
        two_ref[...],
        keep_ref[...],
        gin1_ref[...],
        w1_ref,
        w1_plain_ref[...],
        dsides_ref,
        dog_ref[...],
        dwin_ref,
        dgin_ref,
    )
    grad_out_ref[...] = grad
    unit, _ = norm_parts(one_ref[...])
    gate = sigmoid(dot(wog_ref[...], half(unit * gin0_ref[...]), 1, 0))
    prod_unit, prod_inv = norm_parts(get_rows(prod_ref).astype(F32))
    y_half = half(prod_unit * gout_ref[...])
    update = dot(wout_ref[...], y_half, 1, 0)
    d_prod, d_og, dw_out, dg_out = rear_back(
        grad, gate, update, y_half, prod_unit, prod_inv, gout_ref[...], wout_plain_ref[...]
    )
    put_rows(dprod_ref, d_prod)
    dog_out_ref[...] = d_og
    add_to(dwout_ref, dw_out)
    add_to(dgout_ref, dg_out)


def close_kernel(
    one_ref,
    x_ref,
    dsides_ref,
    dog_ref,
    grad_ref,
    keep_ref,
    gin_ref,
    w_ref,
    w_plain_ref,
    mid_ref,
    bd_ref,
    dbias_ref,
    wb_ref,
    out_ref,
    dmid_ref,
    dwin_ref,
    dgin_ref,
    dright_out_ref,
    dbout_ref,
    dwb_ref,
):
    keep = keep_ref[...]
    grad = grad_ref[...] + front_back(
        one_ref[...],
        keep,
        gin_ref[...],
        w_ref,
        w_plain_ref[...],
        dsides_ref,
        dog_ref[...],
        dwin_ref,
        dgin_ref,
    )
    outer = grad * keep
    add_to(dbout_ref, fold(outer))
    outer = half(outer)
    at = pl.program_id(0)
    total = None
    for p in range(mid_ref.shape[0]):
        piece = lane_row(outer, p)
        part = dot(bd_ref[0], piece, 1, 1)

        @pl.when(at % JH == 0)
        def _(p=p, part=part):
            dmid_ref[p] = part

        @pl.when(at % JH != 0)
        def _(p=p, part=part):
            dmid_ref[p] += part

        part = dot(mid_ref[p], piece, 1, 0)
        total = part if total is None else total + part

    @pl.when(at < JH)
    def _():
        dright_out_ref[at % JH] = total

    @pl.when(at >= JH)
    def _():
        dright_out_ref[at % JH] += total

    d_bias = dbias_ref[...]
    add_to(dwb_ref, dot(d_bias, x_ref[...], 1, 1))
    put_tile(out_ref, grad + dot(wb_ref[...], d_bias, 1, 0))


def item_masks(items, dtype):
    lane = lax.broadcasted_iota(jnp.int32, (1, 256), 1)
    which = (lane // 16) % items
    return [((which == b) & (lane < JH * HALF)).astype(F32).astype(dtype) for b in range(items)]


def spread_items(piece, masks):
    parts = [piece[16 * j : 16 * j + 16] * mask for j in range(JH) for mask in masks]
    return jnp.concatenate(parts + [jnp.zeros((HALF, 256), piece.dtype)], axis=0)


def pick_items(values, masks):
    rows = []
    for j in range(JH):
        total = None
        for b, mask in enumerate(masks):
            start = HALF * j + 16 * b
            part = values[start : start + 16] * mask
            total = part if total is None else total + part
        rows.append(total)
    return jnp.concatenate(rows, axis=0)


def split_lanes(one, two, three):
    low = low_lanes(one.shape[0])
    return (
        jnp.concatenate([jnp.where(low, one, swap(two)), three], axis=1),
        jnp.concatenate([jnp.where(low, swap(one), two), swap(three)], axis=1),
    )


def join_lanes(left, right):
    low = low_lanes(left.shape[0])
    return (
        jnp.where(low, left[:, :128], swap(right[:, :128])),
        jnp.where(low, swap(left[:, :128]), right[:, :128]),
        jnp.where(low, left[:, 128:], swap(right[:, 128:])),
    )


def thirds(values):
    rows = values.shape[0] // JH
    return [values[rows * j : rows * (j + 1)] for j in range(JH)]


def load_double(ref, cols, l_ref, r_ref):
    def step(q, carry):
        left, right = [], []
        for r in range(ref.shape[0] // cols):
            one, two = split_lanes(*thirds(ref[r * cols + q].astype(F32)))
            left.append(one)
            right.append(two)
        l_ref[q] = half(jnp.concatenate(left, axis=0))
        r_ref[q] = half(jnp.concatenate(right, axis=0))
        return carry

    lax.fori_loop(0, cols, step, 0)


def load_single(ref, cols, x_ref):
    def step(q, carry):
        rows = []
        for r in range(ref.shape[0] // cols):
            rows += split_lanes(*thirds(ref[r * cols + q].astype(F32)))
        x_ref[q] = half(jnp.concatenate(rows, axis=0))
        return carry

    lax.fori_loop(0, cols, step, 0)


def put_slab(ref, at, left, right):
    ref[at] = half(jnp.concatenate(join_lanes(left, right), axis=0))


def block_rows(ref, block, at):
    return ref[block, pl.ds(pl.multiple_of(at * 48, 16), 48), :]


def out_product_kernel(s_ref, p_ref, l_ref, r_ref):
    cols, residues, _ = l_ref.shape
    masks = item_masks(ITEMS, BF16)
    load_double(s_ref, cols, l_ref, r_ref)

    def step(at, carry):
        total = None
        for q in range(cols):
            part = dot(l_ref[q], spread_items(block_rows(r_ref, q, at), masks), 1, 1)
            total = part if total is None else total + part
        for r in range(residues // 24):
            tile = total[24 * r : 24 * r + 24]
            put_slab(p_ref, r * cols + at, tile[:12], tile[12:])
        return carry

    lax.fori_loop(0, cols, step, 0)


def flip(values, eye):
    return half(dot(eye, values, 1, 1))


def in_product_kernel(s_ref, eye_ref, p_ref, l_ref, r_ref):
    cols = l_ref.shape[0]
    masks = item_masks(ITEMS, F32)
    load_double(s_ref, cols, l_ref, r_ref)

    def step(at, carry):
        left = flip(l_ref[at], eye_ref[...])
        for q in range(cols):
            rows = pick_items(dot(left, r_ref[q], 1, 0), masks)
            for h in range(2):
                tile = rows[24 * h : 24 * h + 24]
                put_slab(p_ref, (2 * at + h) * cols + q, tile[:12], tile[12:])
        return carry

    lax.fori_loop(0, cols, step, 0)


def in_back_kernel(s_ref, dp_ref, d_ref, l_ref, r_ref, x_ref):
    cols, residues, _ = l_ref.shape
    masks = item_masks(ITEMS, BF16)
    load_double(s_ref, cols, l_ref, r_ref)
    load_single(dp_ref, cols, x_ref)

    def step(at, carry):
        left = right = None
        for q in range(cols):
            part = dot(r_ref[q], spread_items(block_rows(x_ref, q, at), masks), 1, 1)
            left = part if left is None else left + part
            wide = spread_items(x_ref[at, 48 * q : 48 * q + 48, :], masks)
            part = dot(l_ref[q], wide, 1, 0)
            right = part if right is None else right + part
        for r in range(residues // 24):
            rows = slice(24 * r, 24 * r + 24)
            put_slab(d_ref, r * cols + at, left[rows], right[rows])
        return carry

    lax.fori_loop(0, cols, step, 0)


def out_back_kernel(s_ref, dp_ref, eye_ref, d_ref, l_ref, r_ref, x_ref, g_ref):
    cols, residues, _ = l_ref.shape
    masks = item_masks(ITEMS, BF16)
    wide_masks = item_masks(ITEMS, F32)
    load_double(s_ref, cols, l_ref, r_ref)
    load_single(dp_ref, cols, x_ref)

    def right_step(at, carry):
        flipped = flip(x_ref[at], eye_ref[...])
        for q in range(cols):
            rows = pick_items(dot(flipped, l_ref[q], 1, 0), wide_masks)
            g_ref[q, pl.ds(pl.multiple_of(at * 48, 16), 48), :] = rows
        return carry

    lax.fori_loop(0, cols, right_step, 0)

    def left_step(at, carry):
        left = None
        for q in range(cols):
            wide = spread_items(r_ref[at, 48 * q : 48 * q + 48, :], masks)
            part = dot(x_ref[q], wide, 1, 0)
            left = part if left is None else left + part
        for r in range(residues // 24):
            rows = slice(24 * r, 24 * r + 24)
            put_slab(d_ref, r * cols + at, left[rows], g_ref[at, rows, :])
        return carry

    lax.fori_loop(0, cols, left_step, 0)


def cost(flops, nbytes):
    return pl.CostEstimate(flops=int(flops), bytes_accessed=int(nbytes), transcendentals=0)


def call(kernel, steps, ins, outs, flops, scratch=()):
    nbytes = sum(a.size * a.dtype.itemsize for a, _, _ in ins)
    nbytes += sum(s.size * s.dtype.itemsize for s, _, _ in outs)
    return pl.pallas_call(
        kernel,
        grid=(steps,),
        in_specs=[pl.BlockSpec(block, index) for _, block, index in ins],
        out_specs=[pl.BlockSpec(block, index) for _, block, index in outs],
        out_shape=[shape for shape, _, _ in outs],
        scratch_shapes=list(scratch),
        compiler_params=pltpu.CompilerParams(vmem_limit_bytes=VMEM),
        cost_estimate=cost(flops, nbytes),
    )(*[a for a, _, _ in ins])


def whole(array):
    rank = len(array.shape)
    return (array, tuple(array.shape), lambda s: (0,) * rank)


def sds(shape, dtype):
    return jax.ShapeDtypeStruct(shape, dtype)


def per_device(
    node_feats,
    pair_feats,
    distances,
    lengths,
    node_cotan,
    pair_cotan,
    w_qkv,
    w_bias,
    w_dist,
    w_node_out,
    g_node,
    w_ab,
    w_outer,
    b_outer,
    g_tin,
    w_tin,
    g_tout,
    w_tout,
    g_trans,
    w_up,
    w_down,
):
    row_count = lax.axis_size("row")
    col_count = lax.axis_size("col")
    row_index = lax.axis_index("row")
    col_index = lax.axis_index("col")
    items, tile_rows, tile_cols = pair_feats.shape[:3]
    residues = tile_rows * row_count
    devices = row_count * col_count
    il, jl = tile_rows // 2, tile_cols // JH
    lane_rows = JH * il
    slots = lane_rows * 128
    steps = lane_rows // STEP_ROWS
    width = STEP_ROWS * 128
    score_scale = HD ** (-0.5)

    def slot_block(s):
        return (s % JH) * (il // STEP_ROWS) + s // JH

    def chan(array):
        return (array, (array.shape[0], width), lambda s: (0, slot_block(s)))

    def rows_of(array):
        return (array, (STEP_ROWS, C, 128), lambda s: (slot_block(s), 0, 0))

    def double(array):
        return (array, (1, 2, STEP_ROWS, C, 128), lambda s: (s % JH, 0, s // JH, 0, 0))

    def tile(array):
        return (array, (items, 2, STEP_ROWS, jl, C), lambda s: (0, 0, s // JH, s % JH, 0))

    def pairs_of(array):
        return (array, (STEP_ROWS, 2 * items * OP, C), lambda s: (s // JH, 0, 0))

    def f_chan():
        return chan(sds((C, slots), F32))

    def f_whole(*shape):
        return whole(sds(shape, F32))

    def column(vector):
        return whole(vector.reshape(-1, 1))

    def split_tile(array):
        return array.reshape((items, 2, il) + array.shape[2:])

    def to_slots(array):
        lead = array.shape[:-3]
        array = array.reshape(lead + (items, 2, il, JH, jl))
        at = len(lead)
        order = tuple(range(at)) + tuple(at + d for d in (3, 2, 1, 0, 4))
        return jnp.transpose(array, order).reshape(lead + (lane_rows, 128))

    def from_slots(array):
        lead = array.shape[:-2]
        array = array.reshape(lead + (JH, il, 2, items, jl))
        at = len(lead)
        order = tuple(range(at)) + tuple(at + d for d in (3, 2, 1, 0, 4))
        return jnp.transpose(array, order).reshape(lead + (items, tile_rows, tile_cols))

    row_ids = row_index * tile_rows + jnp.arange(tile_rows, dtype=jnp.int32)
    col_ids = col_index * tile_cols + jnp.arange(tile_cols, dtype=jnp.int32)
    row_keep = (row_ids[None, :] < lengths[:, None]).astype(F32)
    col_keep = (col_ids[None, :] < lengths[:, None]).astype(F32)
    keep = to_slots(row_keep[:, :, None] * col_keep[:, None, :]).reshape(1, slots)
    eye = jnp.eye(C, dtype=BF16)
    eye_lanes = jnp.eye(256, dtype=BF16)
    w_in_t = [jnp.transpose(w_tin[t]) for t in range(2)]
    w_out_t = [jnp.transpose(w_tout[t]) for t in range(2)]

    def spread(array, axis):
        count = lax.axis_size(axis) if isinstance(axis, str) else devices
        return swap_all(jnp.broadcast_to(array[None], (count,) + array.shape), axis)

    def swap_all(array, axis):
        return lax.all_to_all(array, axis, split_axis=0, concat_axis=0, tiled=True)

    def tie(*arrays):
        return lax.optimization_barrier(arrays)

    node_rows = jnp.transpose(node_feats, (1, 0, 2)).reshape(tile_rows * items, D)
    cot_rows = jnp.transpose(node_cotan, (1, 0, 2)).reshape(tile_rows * items, D)
    node_full = node_rows.astype(F32)
    parts = tile_cols // tile_rows
    group = row_count // parts
    fetched = []
    for turn in range(parts):
        moves = []
        for src in range(devices):
            src_row, src_col = divmod(src, col_count)
            dst_row = ((src_row + turn) % parts) * group + src_col
            moves.append((src, dst_row * col_count + src_row // parts))
        fetched.append(lax.ppermute(node_rows, BOTH, moves))
    first = row_index // group
    fetched = jnp.stack(fetched)
    col_rows = jnp.concatenate(
        [
            lax.dynamic_index_in_dim(fetched, (first - h) % parts, 0, keepdims=False)
            for h in range(parts)
        ],
        axis=0,
    )
    share = tile_rows * items // col_count

    def node_norm(values):
        centered = values - jnp.mean(values, axis=-1, keepdims=True)
        inv = lax.rsqrt(jnp.mean(centered * centered, axis=-1, keepdims=True) + EPS)
        return centered * inv, inv

    heads_here = H // col_count
    head_width = heads_here * HD
    head_start = col_index * head_width
    w_local = jnp.concatenate(
        [
            lax.dynamic_slice_in_dim(w_qkv, part * D + head_start, head_width, 1)
            for part in range(3)
        ],
        axis=1,
    )
    wo_local = lax.dynamic_slice_in_dim(w_node_out, head_start, head_width, 0)
    qkv = half(dot(node_rows, w_local, 1, 0))
    node_unit, _ = node_norm(node_full)
    normed_node = half(node_unit * g_node)
    pair_rows = half(dot(normed_node, w_ab[:, :OP], 1, 0))
    left_node = pair_rows
    col_unit, _ = node_norm(col_rows.astype(F32))
    right_cols = half(dot(half(col_unit * g_node), w_ab[:, OP:], 1, 0))
    right_cols = right_cols.reshape(tile_cols, items, OP)
    everyone = spread(qkv[:, head_width:].reshape(-1, 128), "row")
    everyone = everyone.reshape(residues, items, 2 * head_width)
    right_wide = jnp.einsum(
        "xy,zxqj->zxqyj",
        jnp.eye(2 * items, dtype=BF16),
        jnp.tile(
            jnp.transpose(right_cols.reshape(JH, jl, items, OP), (0, 2, 3, 1)), (1, 2, 1, 1)
        ),
    ).reshape(JH, 2 * items * OP, 128)
    middle = half(dot(left_node, w_outer, 1, 0)).reshape(2, il, items * OP, C)
    middle = jnp.transpose(middle, (1, 0, 2, 3)).reshape(il, 2 * items * OP, C)
    dist_slots = to_slots(distances)

    x_chan, bias = call(
        enter_kernel,
        steps,
        [
            tile(split_tile(pair_feats)),
            whole(eye),
            whole(jnp.transpose(w_bias)),
            column(w_dist),
            chan(dist_slots.reshape(1, slots)),
        ],
        [chan(sds((C, slots), BF16)), chan(sds((H, slots), BF16))],
        2 * slots * C * C,
    )

    def lane_sum(values):
        return jnp.sum(values, axis=1)[None]

    def padded(arrays):
        flat = jnp.concatenate(arrays, axis=0)
        rows = -(-flat.shape[0] // (devices * 8)) * 8
        flat = jnp.pad(flat, ((0, devices * rows - flat.shape[0]), (0, 0)))
        return flat.reshape(devices, rows, 128)

    def scatter_sum(array):
        return jnp.sum(swap_all(array, BOTH).astype(F32), axis=0)

    def to_channels(rows):
        rows = rows.reshape(-1, C, 128)
        return swap_all(jnp.transpose(rows, (1, 0, 2)), BOTH)

    def to_pairs(slabs):
        got = jnp.transpose(swap_all(slabs, BOTH), (1, 0, 2))
        return got if got.shape[0] == lane_rows else got.reshape(sides.shape)

    sides = sds((JH, 2, il, C, 128), BF16)
    single = sds((lane_rows, C, 128), BF16)
    slab1 = whole(sds((devices, lane_rows, 128), BF16))
    slab2 = whole(sds((devices, 2 * lane_rows, 128), BF16))
    block = pltpu.VMEM((col_count, residues, 256), BF16)
    block32 = pltpu.VMEM((col_count, residues, 256), F32)
    chan_flops = 2 * col_count * col_count * residues * 256 * 256

    g_in = [column(g_tin[t]) for t in range(2)]
    g_out = [column(g_tout[t]) for t in range(2)]
    keep_in = chan(keep)
    bd = (right_wide, (1,) + right_wide.shape[1:], lambda s: (s % JH, 0, 0))
    pos_flops = 2 * slots * C * C
    pair_one, sides0 = call(
        open_kernel,
        steps,
        [
            chan(x_chan),
            pairs_of(middle),
            bd,
            column(b_outer),
            keep_in,
            g_in[0],
            whole(w_in_t[0]),
        ],
        [f_chan(), double(sides)],
        6 * pos_flops,
    )
    everyone, bias = tie(everyone, bias)
    bias_rows = swap_all(bias.reshape(H, lane_rows, 128), "col")
    sides0, bias_rows = tie(sides0, bias_rows)
    slabs0 = to_channels(sides0)
    bias_rows = from_slots(bias_rows.reshape(col_count, heads_here, lane_rows, 128))
    bias_rows = jnp.transpose(bias_rows, (2, 1, 3, 0, 4)).reshape(
        items, heads_here, tile_rows, residues
    )
    key_all = everyone[..., :head_width].reshape(residues, items, heads_here, HD)
    value_all = everyone[..., head_width:].reshape(residues, items, heads_here, HD)
    query = qkv[:, :head_width].reshape(tile_rows, items, heads_here, HD)
    all_ids = jnp.arange(residues, dtype=jnp.int32)
    key_keep = (all_ids[None, :] < lengths[:, None]).astype(F32)

    def product(spec, *operands):
        return jnp.einsum(spec, *operands, preferred_element_type=F32)

    scores = (
        product("ighd,jghd->ghij", query, key_all) * score_scale
        + bias_rows.astype(F32)
        + ((key_keep - 1.0) * 1000000000.0)[:, None, None, :]
    )
    probs = jax.nn.softmax(scores, axis=-1)
    probs_half = half(probs)
    attended = half(
        product("ghij,jghd->ighd", probs_half, value_all).reshape(
            tile_rows * items, head_width
        )
    )
    node_part = half(dot(attended, wo_local, 1, 0))
    dwo_own = dot(attended, cot_rows, 0, 0)
    d_attended = half(dot(cot_rows, wo_local, 1, 1)).reshape(tile_rows, items, heads_here, HD)
    d_probs = product("ighd,jghd->ghij", d_attended, value_all)
    d_value = product("ghij,ighd->jghd", probs_half, d_attended)
    d_scores = half(probs * (d_probs - jnp.sum(probs * d_probs, axis=-1, keepdims=True)))
    d_query = product("ghij,jghd->ighd", d_scores, key_all) * score_scale
    d_key = product("ghij,ighd->jghd", d_scores, query) * score_scale
    d_bias = jnp.transpose(
        d_scores.reshape(items, heads_here, tile_rows, col_count, tile_cols), (3, 1, 0, 2, 4)
    )
    d_bias = to_slots(d_bias).reshape(col_count, heads_here * lane_rows, 128)
    sent = jnp.concatenate([d_bias, node_part.reshape(col_count, -1, 128)], axis=1)
    d_kv = jnp.concatenate(
        [d_key.reshape(-1, head_width), d_value.reshape(-1, head_width)], axis=1
    )
    slabs0, sent = tie(slabs0, sent)
    got = swap_all(sent, "col")
    bias_lanes = heads_here * lane_rows
    d_bias = got[:, :bias_lanes].reshape(H, lane_rows, 128)
    node_sum = jnp.sum(got[:, bias_lanes:].astype(F32), axis=0)
    (p0,) = call(
        out_product_kernel, 1, [whole(slabs0)], [slab1], chan_flops, [block, block]
    )
    p0, d_bias, node_sum = tie(p0, d_bias, node_sum)
    prod0 = to_pairs(p0)
    prod0, d_kv = tie(prod0, d_kv)
    d_kv = swap_all(half(d_kv).reshape(row_count, -1, 128), "row")
    d_kv = jnp.sum(d_kv.astype(F32), axis=0).reshape(tile_rows * items, 2 * head_width)
    d_qkv = half(jnp.concatenate([d_query.reshape(-1, head_width), d_kv], axis=1))
    dw_qkv_own = dot(d_qkv, node_rows, 0, 0)
    pair_two, sides1 = call(
        middle_kernel,
        steps,
        [
            chan(pair_one),
            rows_of(prod0),
            keep_in,
            g_in[0],
            whole(w_in_t[0][4 * CH :]),
            g_out[0],
            whole(w_out_t[0]),
            g_in[1],
            whole(w_in_t[1]),
        ],
        [f_chan(), double(sides)],
        7 * pos_flops,
    )
    sides1, d_qkv = tie(sides1, d_qkv)
    slabs1 = to_channels(sides1)
    slabs1, d_qkv = tie(slabs1, d_qkv)
    d_att = swap_all(half(dot(d_qkv, w_local, 1, 1)).reshape(col_count, -1, 128), "col")
    d_att = jnp.sum(d_att.astype(F32), axis=0).reshape(share, D)
    d_bias32 = d_bias.astype(F32)
    grad_dist = from_slots(jnp.sum(d_bias32 * w_dist[:, None, None], axis=0))
    dw_dist = jnp.sum(d_bias32 * dist_slots[None], axis=(1, 2))
    d_bias_chan = d_bias.reshape(H, slots)

    (p1,) = call(
        in_product_kernel,
        1,
        [whole(slabs1), whole(eye_lanes)],
        [slab1],
        chan_flops,
        [block, block],
    )
    p1, d_att = tie(p1, d_att)
    prod1 = to_pairs(p1)
    head_grads = jnp.concatenate([dw_qkv_own, dwo_own], axis=0)
    prod1, head_grads = tie(prod1, head_grads)
    head_grads = swap_all(head_grads.reshape(row_count, -1, 128), "row")
    head_grads = jnp.sum(head_grads, axis=0)
    (
        pair_out,
        grad2,
        dprod1,
        dog1,
        dw_down,
        dw_up_t,
        dg_trans,
        dw_out1_t,
        dg_out1,
    ) = call(
        turn_kernel,
        steps,
        [
            chan(pair_two),
            rows_of(prod1),
            tile(split_tile(pair_cotan)),
            whole(eye),
            g_in[1],
            whole(w_in_t[1][4 * CH :]),
            g_out[1],
            whole(w_out_t[1]),
            whole(w_tout[1]),
            column(g_trans),
            whole(jnp.transpose(w_up)),
            whole(w_up),
            whole(jnp.transpose(w_down)),
            whole(w_down),
        ],
        [
            tile(sds((items, 2, il, tile_cols, C), F32)),
            f_chan(),
            rows_of(single),
            chan(sds((C, slots), BF16)),
            f_whole(FT, C),
            f_whole(FT, C),
            f_whole(C, 128),
            f_whole(C, CH),
            f_whole(CH, 128),
        ],
        30 * pos_flops,
    )
    dprod1, head_grads = tie(dprod1, head_grads)
    dp1 = to_channels(dprod1)
    (d1,) = call(
        in_back_kernel,
        1,
        [whole(slabs1), whole(dp1)],
        [slab2],
        2 * chan_flops,
        [block, block, block],
    )
    dsides1 = to_pairs(d1)
    grad1, dprod0, dog0, dw_in1_t, dg_in1, dw_out0_t, dg_out0 = call(
        back_kernel,
        steps,
        [
            chan(pair_two),
            chan(pair_one),
            rows_of(prod0),
            double(dsides1),
            chan(dog1),
            chan(grad2),
            keep_in,
            g_in[1],
            whole(w_in_t[1]),
            whole(w_tin[1]),
            g_in[0],
            whole(w_in_t[0][4 * CH :]),
            g_out[0],
            whole(w_out_t[0]),
            whole(w_tout[0]),
        ],
        [
            f_chan(),
            rows_of(single),
            chan(sds((C, slots), BF16)),
            f_whole(5 * CH, C),
            f_whole(C, 128),
            f_whole(C, CH),
            f_whole(CH, 128),
        ],
        20 * pos_flops,
    )
    dp0 = to_channels(dprod0)
    mid_arrays = [
        dw_in1_t,
        dw_out0_t,
        lane_sum(dg_in1),
        lane_sum(dg_out0),
        dw_down,
        dw_up_t,
        dw_out1_t,
        jnp.pad(dw_dist, (0, 128 - H))[None],
        lane_sum(dg_trans),
        lane_sum(dg_out1),
    ]
    mid_sent = half(padded(mid_arrays))
    dp0, mid_sent = tie(dp0, mid_sent)
    mid_part = scatter_sum(mid_sent)
    (d0,) = call(
        out_back_kernel,
        1,
        [whole(slabs0), whole(dp0), whole(eye_lanes)],
        [slab2],
        2 * chan_flops,
        [block, block, block, block32],
    )
    d0, mid_part = tie(d0, mid_part)
    dsides0 = to_pairs(d0)
    mid_part = half(jnp.concatenate([mid_part, head_grads], axis=0))
    dsides0, mid_part = tie(dsides0, mid_part)
    mid_all = spread(mid_part, BOTH)
    grad_pair, d_middle, dw_in0_t, dg_in0, d_right_wide, db_outer, dw_bias_t = call(
        close_kernel,
        steps,
        [
            chan(pair_one),
            chan(x_chan),
            double(dsides0),
            chan(dog0),
            chan(grad1),
            keep_in,
            g_in[0],
            whole(w_in_t[0]),
            whole(w_tin[0]),
            pairs_of(middle),
            bd,
            chan(d_bias_chan),
            whole(w_bias),
        ],
        [
            tile(sds((items, 2, il, tile_cols, C), F32)),
            pairs_of(sds(middle.shape, F32)),
            f_whole(5 * CH, C),
            f_whole(C, 128),
            f_whole(*right_wide.shape),
            f_whole(C, 128),
            f_whole(H, C),
        ],
        18 * pos_flops,
    )

    grad_pair, mid_all, d_middle = tie(grad_pair, mid_all, d_middle)
    mid_rows = mid_all.shape[1] - head_grads.shape[0]
    d_middle = jnp.transpose(half(d_middle).reshape(il, 2, items * OP, C), (1, 0, 2, 3))
    d_middle = d_middle.reshape(tile_rows * items, OP * C)
    dw_outer = dot(left_node, d_middle, 0, 0)
    d_left = dot(d_middle, w_outer, 1, 1)
    d_right = jnp.einsum(
        "zxqxj->zxqj", d_right_wide.reshape(JH, 2 * items, OP, 2 * items, jl)
    )
    d_right = jnp.sum(d_right.reshape(JH, 2, items, OP, jl), axis=1)
    d_right = jnp.transpose(d_right, (0, 3, 1, 2))
    d_right = d_right.reshape(tile_cols * items, OP)
    unit_ab = jnp.concatenate(
        [dot(half(node_unit), half(d_left), 0, 0), dot(half(col_unit), half(d_right), 0, 0)],
        axis=1,
    )
    late_arrays = [
        dw_in0_t,
        dw_outer.reshape(-1, 128),
        unit_ab.reshape(-1, 128),
        dw_bias_t,
        lane_sum(dg_in0),
        lane_sum(db_outer),
    ]
    own_row = (jnp.arange(row_count) == row_index).astype(F32)
    own_col = (jnp.arange(row_count) // parts == col_index).astype(F32)
    send_left = own_row[:, None, None, None] * d_left.reshape(1, col_count, share, OP)
    send_right = own_col[:, None, None, None] * jnp.tile(
        d_right.reshape(parts, col_count, share, OP), (group, 1, 1, 1)
    )
    sent = half(jnp.concatenate([send_left, send_right], axis=-1)).reshape(devices, -1, 128)
    rows = sent.shape[1]
    sent = jnp.concatenate([sent, half(padded(late_arrays))], axis=1)
    got = scatter_sum(sent)
    late_part = got[rows:]
    d_pair_rows = half(got[:rows]).reshape(share, 2 * OP)
    node_share = lax.dynamic_slice_in_dim(node_full, col_index * share, share, 0)
    cot_share = lax.dynamic_slice_in_dim(cot_rows, col_index * share, share, 0)
    unit, inv = node_norm(node_share)
    d_normed = half(dot(d_pair_rows, w_ab, 1, 1)).astype(F32)
    scaled = d_normed * g_node
    d_norm = inv * (
        scaled
        - jnp.mean(scaled, axis=-1, keepdims=True)
        - unit * jnp.mean(scaled * unit, axis=-1, keepdims=True)
    )
    grad_share = cot_share.astype(F32) + d_att + d_norm
    out_share = node_share + node_sum.reshape(share, D)
    nodes = spread(jnp.stack([out_share, grad_share]).reshape(-1, 128), "col")
    nodes = nodes.reshape(col_count, 2, share, D)

    def node_result(which):
        array = nodes[:, which].reshape(tile_rows, items, D)
        return jnp.transpose(array, (1, 0, 2))

    head_grads = mid_all[:, mid_rows:].astype(F32).reshape(row_count, col_count, -1)
    head_grads = jnp.transpose(head_grads, (1, 0, 2)).reshape(col_count, 4, head_width, D)
    g_qkv = jnp.transpose(head_grads[:, :3], (3, 1, 0, 2)).reshape(D, 3 * D)
    g_node_out = head_grads[:, 3].reshape(D, D)

    def cut(flat, arrays):
        start, pieces = 0, []
        for array in arrays:
            pieces.append(flat[start : start + array.shape[0]])
            start += array.shape[0]
        return pieces

    (
        s_in1_t,
        s_out0_t,
        s_gin1,
        s_gout0,
        s_down,
        s_up_t,
        s_out1_t,
        s_dist,
        s_trans,
        s_gout1,
    ) = cut(mid_all[:, :mid_rows].reshape(-1, 128).astype(F32), mid_arrays)
    late_all = spread(half(late_part), BOTH).reshape(-1, 128).astype(F32)
    s_in0_t, s_outer, s_ab, s_bias_t, s_gin0, s_bout = cut(late_all, late_arrays)
    s_ab = s_ab.reshape(D, 2 * OP)
    s_gnode = jnp.sum(s_ab * w_ab.astype(F32), axis=1)
    s_ab = s_ab * g_node[:, None]
    return (
        node_result(0),
        pair_out.reshape(pair_feats.shape),
        node_result(1),
        grad_pair.reshape(pair_feats.shape),
        grad_dist,
        g_qkv,
        jnp.transpose(s_bias_t),
        s_dist[0, :H],
        g_node_out,
        s_gnode,
        s_ab,
        s_outer.reshape(OP, OP * C),
        s_bout.reshape(C),
        jnp.concatenate([s_gin0, s_gin1]),
        jnp.stack([jnp.transpose(s_in0_t), jnp.transpose(s_in1_t)]),
        jnp.concatenate([s_gout0, s_gout1]),
        jnp.stack([jnp.transpose(s_out0_t), jnp.transpose(s_out1_t)]),
        s_trans[0],
        jnp.transpose(s_up_t),
        s_down,
    )


def solution(mesh):
    pair = P(None, "row", "col", None)
    node = P(None, "row", None)
    dist = P(None, "row", "col")
    return jax.shard_map(
        per_device,
        mesh=mesh,
        in_specs=(node, pair, dist, P(), node, pair) + (P(),) * 15,
        out_specs=(node, pair, node, pair, dist) + (P(),) * 15,
        check_vma=False,
    )
```

time: 2480 us -> 598 us (0.24)
  waiting for transfers between devices: 1320 us -> 162 us
  blocking collectives: 359 us -> 66.8 us
  local copies, waits for them, and re-layouts: 347 us -> 76.5 us
  matrix products: 269 us -> 7.47 us
  Pallas kernels: 0 us -> 140 us
  other arithmetic: 139 us -> 22.2 us
  starting transfers between devices: 17.1 us -> 112 us
    all_gather x8 -> x0, waiting for transfers between devices: 451 us -> none  [the longest x2 155 us: run_block(): dprod_rows = lax.all_gather(d_prod_two, 'row', axis=1, tiled=True)]
    reduce_scatter x6 -> x0, waiting for transfers between devices: 397 us -> none  [the longest x2 207 us: run_block(): lax.psum_scatter(jnp.einsum('gkic,gkjc->igjc', slab_piece, right_two, pre...]
    while x24 -> x0, waiting for transfers between devices: 293 us -> none
    dot_general x96 -> x20, matrix products: 269 us -> 7.47 us  [the longest x14 6.14 us: dot(): lax.dot_general(lhs, rhs, (((lhs_dim,), (rhs_dim,)), ((), ())), preferred...]
    psum x3 -> x0, waiting for transfers between devices: 175 us -> none  [the longest x1 93.7 us: sum_weights(): lax.psum((grad_list[0], grad_list[1], grad_list[2], grad_list[3], grad_li...]
    all_gather x8 -> x0, local copies, waits for them, and re-layouts: 164 us -> none  [the longest x2 67.7 us: run_block(): dprod_rows = lax.all_gather(d_prod_two, 'row', axis=1, tiled=True)]
    all_to_all x4 -> x17, waiting for transfers between devices: 4.67 us -> 162 us  [swap_all(): return lax.all_to_all(array, axis, split_axis=0, concat_axis=0, tiled=True)]
    pallas_call x0 -> x10, Pallas kernels: none -> 140 us  [call(): pl.pallas_call(kernel, grid=(steps,), in_specs=[pl.BlockSpec(block, index...]
  transfers between devices with their start and end apart: 25 -> 19, of which waited for: 23 -> 9; matrix products, arithmetic and copies ran while one was open for 9% -> 10% of each run, Pallas kernels for 0% -> 18%
where the time goes in v1:
time: 598 us; the launch traced here: 590 us
  waiting for transfers between devices  162 us (27%)
  Pallas kernels  140 us (23%)
  starting transfers between devices  112 us (19%)
  local copies, waits for them, and re-layouts  76.5 us (13%)
  blocking collectives  66.8 us (11%)
  other arithmetic  22.2 us (4%)
  matrix products  7.47 us (1%)
    all_to_all x17, waiting for transfers between devices, swap_all(): return lax.all_to_all(array, axis, split_axis=0, concat_axis=0, tiled=True)  162 us
    pallas_call x10, Pallas kernels, call(): pl.pallas_call(kernel, grid=(steps,), in_specs=[pl.BlockSpec(block, index...  140 us
    all_to_all x17, starting transfers between devices, swap_all(): return lax.all_to_all(array, axis, split_axis=0, concat_axis=0, tiled=True)  104 us
    all_to_all x2, blocking collectives, swap_all(): return lax.all_to_all(array, axis, split_axis=0, concat_axis=0, tiled=True)  66.8 us
  transfers between devices with their start and end apart: 19, of which 9 were waited for; matrix products, arithmetic and copies ran while one was open for 10% of the time, Pallas kernels for 18%

profile of v1, /device:TPU:1, one launch (start us, length us, event | category | flops | bytes accessed | tf_op | source)
XLA Modules:
  0.0 589.7 jit_solution(13399636129727341258)
XLA Ops:
  1.7 1.5 collective-permute-start.1
  3.2 6.2 %collective-permute-start = (bf16[96,256]{1,0:T(8,128)(2,1)S(1)}, bf16[96,256]{1,0:T(8,128)(2,1)S(1)}, u32[]{:S(2)}, u32[]{:S(2)}) collective-permute-start(bf16[96,256]{1,0:T(8,128)(2,1)S(1)} %reshape.500), channel_id=1, source_target_pairs={{0,0},{1,8},{2,16},{3,24},{4,32},{5,40},{6,48},{7,56},{8,64},{9,72... | collective-permute-start | bytes 147464 | tf_op jit(solution)/shard_map/ppermute | solution.py:700
  12.2 8.8 %all-to-all-start = ((bf16[16,48,128]{2,1,0:T(8,128)(2,1)}), bf16[16,48,128]{2,1,0:T(8,128)(2,1)S(1)}, u32[]{:S(2)}, u32[]{:S(2)}) async-start(bf16[16,48,128]{2,1,0:T(8,128)(2,1)} %broadcast_in_dim.38), calls=%async_computation | async-start | bytes 393216 | tf_op jit(solution)/shard_map/all_to_all | solution.py:683
  30.3 5.1 shard_map.356
  38.5 4.0 all-to-all-start.1
  42.5 7.9 %shard_map.357 = (f32[128,4608]{1,0:T(8,128)}, bf16[3,2,12,128,128]{4,3,2,1,0:T(8,128)(2,1)}) custom-call(bf16[128,4608]{1,0:T(8,128)(2,1)} %get-tuple-element.79.x_ref, bf16[12,256,128]{2,1,0:T(8,128)(2,1)} %bitcast.256, bf16[3,256,128]{2,1,0:T(8,128)(2,1)} %copy.493.bd_ref, f32[128,1]{1,0:T(8,128)} %copy.494.bout_ref, f32[1,4608]{1,0:T(1,128)} %mul.228.keep_ref, ...), custom_call_target="tpu_custom_call" | custom-call | flops 905969664 | bytes 7064576 | tf_op jit(solution)/shard_map/pallas_call | solution.py:566
  50.5 4.6 copy.590
  55.1 11.4 %all-to-all-start.2 = ((bf16[128,72,128]{2,1,0:T(8,128)(2,1)}), bf16[128,72,128]{2,1,0:T(8,128)(2,1)}, u32[]{:S(2)}, u32[]{:S(2)}) async-start(bf16[128,72,128]{2,1,0:T(8,128)(2,1)} %bitcast.235), calls=%async_computation.2 | async-start | bytes 4718592 | tf_op jit(solution)/shard_map/all_to_all | solution.py:683
  76.2 22.7 %all-to-all-done.2.s_ref = bf16[128,72,128]{2,1,0:T(8,128)(2,1)} async-done(((bf16[128,72,128]{2,1,0:T(8,128)(2,1)}), bf16[128,72,128]{2,1,0:T(8,128)(2,1)}, u32[]{:S(2)}, u32[]{:S(2)}) %all-to-all-start.2) | async-done | bytes 2359328 | tf_op jit(solution)/shard_map/all_to_all | solution.py:683
  99.6 3.4 all-to-all-start.3
  103.0 9.2 %shard_map.358 = bf16[128,36,128]{2,1,0:T(8,128)(2,1)} custom-call(bf16[128,72,128]{2,1,0:T(8,128)(2,1)} %all-to-all-done.2.s_ref), custom_call_target="tpu_custom_call" | custom-call | flops 3221225472 | bytes 3538944 | tf_op jit(solution)/shard_map/pallas_call | solution.py:566
  112.9 7.1 %all-to-all-start.4 = ((bf16[128,36,128]{2,1,0:T(8,128)(2,1)}), bf16[128,36,128]{2,1,0:T(8,128)(2,1)S(1)}, u32[]{:S(2)}, u32[]{:S(2)}) async-start(bf16[128,36,128]{2,1,0:T(8,128)(2,1)} %shard_map.358), calls=%async_computation.4 | async-start | bytes 2621440 | tf_op jit(solution)/shard_map/all_to_all | solution.py:683
  125.8 16.4 %all-to-all-done.4 = bf16[128,36,128]{2,1,0:T(8,128)(2,1)S(1)} async-done(((bf16[128,36,128]{2,1,0:T(8,128)(2,1)}), bf16[128,36,128]{2,1,0:T(8,128)(2,1)S(1)}, u32[]{:S(2)}, u32[]{:S(2)}) %all-to-all-start.4) | async-done | bytes 1179680 | tf_op jit(solution)/shard_map/all_to_all | solution.py:683
  144.5 4.2 all-to-all-start.5
  148.9 8.8 %shard_map.359 = (f32[128,4608]{1,0:T(8,128)}, bf16[3,2,12,128,128]{4,3,2,1,0:T(8,128)(2,1)}) custom-call(f32[128,4608]{1,0:T(8,128)} %get-tuple-element.89.one_ref, bf16[36,128,128]{2,1,0:T(8,128)(2,1)} %bitcast.243, f32[1,4608]{1,0:T(1,128)} %mul.228.keep_ref, f32[128,1]{1,0:T(8,128)} %copy.495.gain_ref.gin0_ref.gin_ref, bf16[128,128]{1,0:T(8,128)(2,1)} %copy.522.wog_ref, ...), custom_call_target="tpu_custom_call" | custom-call | flops 1056964608 | bytes 8506880 | tf_op jit(solution)/shard_map/pallas_call | solution.py:566
  157.8 4.6 copy.589
  162.5 7.1 %all-to-all-start.6 = ((bf16[128,72,128]{2,1,0:T(8,128)(2,1)}), bf16[128,72,128]{2,1,0:T(8,128)(2,1)S(1)}, u32[]{:S(2)}, u32[]{:S(2)}) async-start(bf16[128,72,128]{2,1,0:T(8,128)(2,1)} %bitcast.234), calls=%async_computation.6 | async-start | bytes 4718592 | tf_op jit(solution)/shard_map/all_to_all | solution.py:683
  170.3 32.2 %all-to-all-done.6.s_ref = bf16[128,72,128]{2,1,0:T(8,128)(2,1)S(1)} async-done(((bf16[128,72,128]{2,1,0:T(8,128)(2,1)}), bf16[128,72,128]{2,1,0:T(8,128)(2,1)S(1)}, u32[]{:S(2)}, u32[]{:S(2)}) %all-to-all-start.6) | async-done | bytes 2359328 | tf_op jit(solution)/shard_map/all_to_all | solution.py:683
  203.7 3.8 all-to-all-start.7
  207.4 11.5 %shard_map.360 = bf16[128,36,128]{2,1,0:T(8,128)(2,1)} custom-call(bf16[128,72,128]{2,1,0:T(8,128)(2,1)} %copy-done.3, bf16[256,256]{1,0:T(8,128)(2,1)} %fusion.14.eye_ref), custom_call_target="tpu_custom_call" | custom-call | flops 3221225472 | bytes 3670016 | tf_op jit(solution)/shard_map/pallas_call | solution.py:566
  219.0 7.2 %all-to-all-start.8 = ((bf16[128,36,128]{2,1,0:T(8,128)(2,1)}), bf16[128,36,128]{2,1,0:T(8,128)(2,1)S(1)}, u32[]{:S(2)}, u32[]{:S(2)}) async-start(bf16[128,36,128]{2,1,0:T(8,128)(2,1)} %shard_map.360), calls=%async_computation.8 | async-start | bytes 2621440 | tf_op jit(solution)/shard_map/all_to_all | solution.py:683
  231.0 17.3 %all-to-all-done.8 = bf16[128,36,128]{2,1,0:T(8,128)(2,1)S(1)} async-done(((bf16[128,36,128]{2,1,0:T(8,128)(2,1)}), bf16[128,36,128]{2,1,0:T(8,128)(2,1)S(1)}, u32[]{:S(2)}, u32[]{:S(2)}) %all-to-all-start.8) | async-done | bytes 1179680 | tf_op jit(solution)/shard_map/all_to_all | solution.py:683
  250.2 4.2 all-to-all-start.9
  254.4 23.3 %shard_map.361 = (f32[4,2,12,48,128]{4,3,2,1,0:T(8,128)}, f32[128,4608]{1,0:T(8,128)}, bf16[36,128,128]{2,1,0:T(8,128)(2,1)}, bf16[128,4608]{1,0:T(8,128)(2,1)},...) custom-call(f32[128,4608]{1,0:T(8,128)} %get-tuple-element.99.two_re, ...), custom_call_target="tpu_custom_call" | custom-call | flops 4529848320 | bytes 13174272 | tf_op jit(solution)/shard_map/pallas_call | solution.py:566
  277.8 2.0 copy.592
  279.8 29.2 %all_to_all.95.dp_ref = bf16[128,36,128]{2,1,0:T(8,128)(2,1)} all-to-all(bf16[128,36,128]{2,1,0:T(8,128)(2,1)S(1)} %bitcast.249), channel_id=1, replica_groups=mesh['row'=16,'col'=8] {'row','col'}, dimensions={0} | all-to-all | bytes 2359296 | tf_op jit(solution)/shard_map/all_to_all | solution.py:683
  309.0 14.1 %shard_map.362 = bf16[128,72,128]{2,1,0:T(8,128)(2,1)} custom-call(bf16[128,72,128]{2,1,0:T(8,128)(2,1)} %copy-done.3, bf16[128,36,128]{2,1,0:T(8,128)(2,1)} %all_to_all.95.dp_ref), custom_call_target="tpu_custom_call" | custom-call | flops 6442450944 | bytes 5898240 | tf_op jit(solution)/shard_map/pallas_call | solution.py:566
  323.1 37.6 %all_to_all.96 = bf16[128,72,128]{2,1,0:T(8,128)(2,1)S(1)} all-to-all(bf16[128,72,128]{2,1,0:T(8,128)(2,1)} %shard_map.362), channel_id=1, replica_groups=mesh['row'=16,'col'=8] {'row','col'}, dimensions={0} | all-to-all | bytes 4718592 | tf_op jit(solution)/shard_map/all_to_all | solution.py:683
  360.7 2.0 copy.538
  362.7 16.8 %shard_map.363 = (f32[128,4608]{1,0:T(8,128)}, bf16[36,128,128]{2,1,0:T(8,128)(2,1)}, bf16[128,4608]{1,0:T(8,128)(2,1)}, f32[640,128]{1,0:T(8,128)}, f32[128,128...) custom-call(f32[128,4608]{1,0:T(8,128)} %get-tuple-element.99.two_ref, f32[128,4608]{1,0:T(8,128)} %get-tuple-element.89.one_ref, ...), custom_call_target="tpu_custom_call" | custom-call | flops 3019898880 | bytes 17485312 | tf_op jit(solution)/shard_map/pallas_call | solution.py:566
  379.5 3.1 copy.591
  382.7 5.1 all-to-all-start.12
  388.8 1.5 concatenate.54
  391.1 19.0 %all-to-all-done.12.dp_ref = bf16[128,36,128]{2,1,0:T(8,128)(2,1)S(1)} async-done(((bf16[128,36,128]{2,1,0:T(8,128)(2,1)}), bf16[128,36,128]{2,1,0:T(8,128)(2,1)S(1)}, u32[]{:S(2)}, u32[]{:S(2)}) %all-to-all-start.12) | async-done | bytes 1179680 | tf_op jit(solution)/shard_map/all_to_all | solution.py:683
  410.1 4.3 all-to-all-start.13
  414.4 17.9 %shard_map.364 = bf16[128,72,128]{2,1,0:T(8,128)(2,1)} custom-call(bf16[128,72,128]{2,1,0:T(8,128)(2,1)} %all-to-all-done.2.s_ref, bf16[128,36,128]{2,1,0:T(8,128)(2,1)} %copy-done.4, bf16[256,256]{1,0:T(8,128)(2,1)} %fusion.14.eye_ref), custom_call_target="tpu_custom_call" | custom-call | flops 6442450944 | bytes 6029312 | tf_op jit(solution)/shard_map/pallas_call | solution.py:566
  432.6 9.9 %all-to-all-start.14 = ((bf16[128,72,128]{2,1,0:T(8,128)(2,1)}), bf16[128,72,128]{2,1,0:T(8,128)(2,1)S(1)}, u32[]{:S(2)}, u32[]{:S(2)}) async-start(bf16[128,72,128]{2,1,0:T(8,128)(2,1)} %shard_map.364), calls=%async_computation.14 | async-start | bytes 4718592 | tf_op jit(solution)/shard_map/all_to_all | solution.py:683
  447.6 27.8 %all-to-all-done.14 = bf16[128,72,128]{2,1,0:T(8,128)(2,1)S(1)} async-done(((bf16[128,72,128]{2,1,0:T(8,128)(2,1)}), bf16[128,72,128]{2,1,0:T(8,128)(2,1)S(1)}, u32[]{:S(2)}, u32[]{:S(2)}) %all-to-all-start.14) | async-done | bytes 2359328 | tf_op jit(solution)/shard_map/all_to_all | solution.py:683
  475.4 2.1 copy.547
  478.6 4.8 all-to-all-start.15
  483.9 25.2 %shard_map.365 = (f32[4,2,12,48,128]{4,3,2,1,0:T(8,128)}, f32[12,256,128]{2,1,0:T(8,128)}, f32[640,128]{1,0:T(8,128)}, f32[128,128]{1,0:T(8,128)}, f32[3,256,128...) custom-call(f32[128,4608]{1,0:T(8,128)} %get-tuple-element.89.one_ref, ...), custom_call_target="tpu_custom_call" | custom-call | flops 2717908992 | bytes 15630848 | tf_op jit(solution)/shard_map/pallas_call | solution.py:566
  518.2 1.5 convert_element_type.256
  524.1 10.3 %all-to-all-start.16 = ((bf16[128,22,128]{2,1,0:T(8,128)(2,1)}), bf16[128,22,128]{2,1,0:T(8,128)(2,1)}, u32[]{:S(2)}, u32[]{:S(2)}) async-start(bf16[128,22,128]{2,1,0:T(8,128)(2,1)} %pad_maximum_fusion.1), calls=%async_computation.16 | async-start | bytes 1572864 | tf_op jit(solution)/shard_map/all_to_all | solution.py:683
  540.9 9.9 %all-to-all-done.16 = bf16[128,22,128]{2,1,0:T(8,128)(2,1)} async-done(((bf16[128,22,128]{2,1,0:T(8,128)(2,1)}), bf16[128,22,128]{2,1,0:T(8,128)(2,1)}, u32[]{:S(2)}, u32[]{:S(2)}) %all-to-all-start.16) | async-done | bytes 720928 | tf_op jit(solution)/shard_map/all_to_all | solution.py:683
  554.8 3.4 all-to-all-start.17
  558.7 5.3 all-to-all-done.17
  564.9 5.2 all-to-all-start.18
  572.6 11.6 %all-to-all-done.18 = bf16[128,16,128]{2,1,0:T(8,128)(2,1)S(1)} async-done(((bf16[128,16,128]{2,1,0:T(8,128)(2,1)}), bf16[128,16,128]{2,1,0:T(8,128)(2,1)S(1)}, u32[]{:S(2)}, u32[]{:S(2)}) %all-to-all-start.18) | async-done | bytes 524320 | tf_op jit(solution)/shard_map/all_to_all | solution.py:683
  (388 shorter events, 84.8 us)
Async XLA Ops:
  0.7 23.1 %copy-start = (bf16[32,4096]{1,0:T(8,128)(2,1)S(1)}, bf16[32,4096]{1,0:T(8,128)(2,1)}, u32[]{:S(2)}) copy-start(bf16[32,4096]{1,0:T(8,128)(2,1)} %param.33) | copy-start | bytes 786436
  0.7 20.4 %copy-start.14 = (bf16[4,24,256]{2,1,0:T(8,128)(2,1)S(1)}, bf16[4,24,256]{2,1,0:T(8,128)(2,1)}, u32[]{:S(2)}) copy-start(bf16[4,24,256]{2,1,0:T(8,128)(2,1)} %param.21) | copy-start | bytes 147460
  0.7 21.4 %copy-start.62 = (f32[2,128]{1,0:T(2,128)S(1)}, f32[2,128]{1,0:T(2,128)}, u32[]{:S(2)}) copy-start(f32[2,128]{1,0:T(2,128)} %param.35) | copy-start | bytes 3076
  0.7 21.4 %copy-start.52 = (s32[4]{0:T(128)S(1)}, s32[4]{0:T(128)}, u32[]{:S(2)}) copy-start(s32[4]{0:T(128)} %param.24) | copy-start | bytes 52
  0.7 21.9 %copy-start.22 = (bf16[2,128,640]{2,1,0:T(8,128)(2,1)S(1)}, bf16[2,128,640]{2,1,0:T(8,128)(2,1)}, u32[]{:S(2)}) copy-start(bf16[2,128,640]{2,1,0:T(8,128)(2,1)} %param.36) | copy-start | bytes 983044
  0.7 22.8 %copy-start.46 = (bf16[256,64]{0,1:T(8,128)(2,1)S(1)}, bf16[256,64]{0,1:T(8,128)(2,1)}, u32[]{:S(2)}) copy-start(bf16[256,64]{0,1:T(8,128)(2,1)} %param.32) | copy-start | bytes 98308
  0.7 22.8 %copy-start.60 = (f32[256]{0:T(256)S(1)}, f32[256]{0:T(256)}, u32[]{:S(2)}) copy-start(f32[256]{0:T(256)} %param.31) | copy-start | bytes 3076
  1.7 33.7 %collective-permute-start.1 = (bf16[96,256]{1,0:T(8,128)(2,1)S(1)}, bf16[96,256]{1,0:T(8,128)(2,1)S(1)}, u32[]{:S(2)}, u32[]{:S(2)}) collective-permute-start(bf16[96,256]{1,0:T(8,128)(2,1)S(1)} %reshape.500), channel_id=1, source_target_pairs={{0,64},{1,72},{2,80},{3,88},{4,96},{5,104},{6,112},{7,120},{8,0},{... | collective-permute-start | bytes 147464 | tf_op jit(solution)/shard_map/ppermute | solution.py:700
  3.2 32.2 %collective-permute-start = (bf16[96,256]{1,0:T(8,128)(2,1)S(1)}, bf16[96,256]{1,0:T(8,128)(2,1)S(1)}, u32[]{:S(2)}, u32[]{:S(2)}) collective-permute-start(bf16[96,256]{1,0:T(8,128)(2,1)S(1)} %reshape.500), channel_id=1, source_target_pairs={{0,0},{1,8},{2,16},{3,24},{4,32},{5,40},{6,48},{7,56},{8,64},{9,72... | collective-permute-start | bytes 147464 | tf_op jit(solution)/shard_map/ppermute | solution.py:700
  12.2 12.0 %copy-start.56 = (f32[8]{0:T(128)S(1)}, f32[8]{0:T(128)}, u32[]{:S(2)}) copy-start(f32[8]{0:T(128)} %param.29) | copy-start | bytes 100
  12.2 13.4 %copy-start.65 = (f32[128]{0:T(128)S(1)}, f32[128]{0:T(128)}, u32[]{:S(2)}) copy-start(f32[128]{0:T(128)} %param.34) | copy-start | bytes 1540
  12.2 25.4 %all-to-all-start = ((bf16[16,48,128]{2,1,0:T(8,128)(2,1)}), bf16[16,48,128]{2,1,0:T(8,128)(2,1)S(1)}, u32[]{:S(2)}, u32[]{:S(2)}) async-start(bf16[16,48,128]{2,1,0:T(8,128)(2,1)} %broadcast_in_dim.38), calls=%async_computation | async-start | bytes 393216 | tf_op jit(solution)/shard_map/all_to_all | solution.py:683
  38.5 11.9 %all-to-all-start.1 = ((bf16[8,36,128]{2,1,0:T(8,128)(2,1)}), bf16[8,36,128]{2,1,0:T(8,128)(2,1)S(1)}, u32[]{:S(2)}, u32[]{:S(2)}) async-start(bf16[8,36,128]{2,1,0:T(8,128)(2,1)} %copy.498), calls=%async_computation.1 | async-start | bytes 163840 | tf_op jit(solution)/shard_map/all_to_all | solution.py:683
  55.1 11.4 %copy-start.41 = (bf16[4,24,256]{2,1,0:T(8,128)(2,1)S(1)}, bf16[4,24,256]{2,1,0:T(8,128)(2,1)}, u32[]{:S(2)}) copy-start(bf16[4,24,256]{2,1,0:T(8,128)(2,1)} %param.25) | copy-start | bytes 147460
  55.1 43.9 %all-to-all-start.2 = ((bf16[128,72,128]{2,1,0:T(8,128)(2,1)}), bf16[128,72,128]{2,1,0:T(8,128)(2,1)}, u32[]{:S(2)}, u32[]{:S(2)}) async-start(bf16[128,72,128]{2,1,0:T(8,128)(2,1)} %bitcast.235), calls=%async_computation.2 | async-start | bytes 4718592 | tf_op jit(solution)/shard_map/all_to_all | solution.py:683
  99.6 12.6 %all-to-all-start.3 = ((bf16[8,60,128]{2,1,0:T(8,128)(2,1)}), bf16[8,60,128]{2,1,0:T(8,128)(2,1)S(1)}, u32[]{:S(2)}, u32[]{:S(2)}) async-start(bf16[8,60,128]{2,1,0:T(8,128)(2,1)} %copy.514), calls=%async_computation.3 | async-start | bytes 262144 | tf_op jit(solution)/shard_map/all_to_all | solution.py:683
  112.3 275.7 %copy-start.5 = (bf16[8,36,128]{2,0,1:T(8,128)(2,1)}, bf16[8,36,128]{2,0,1:T(8,128)(2,1)S(1)}, u32[]{:S(2)}) copy-start(bf16[8,36,128]{2,0,1:T(8,128)(2,1)S(1)} %copy.569) | copy-start | bytes 221188
  112.9 11.6 %copy-start.28 = (bf16[96,32]{1,0:T(8,128)(2,1)S(1)}, bf16[96,32]{1,0:T(8,128)(2,1)}, u32[]{:S(2)}) copy-start(bf16[96,32]{1,0:T(8,128)(2,1)} %copy.500) | copy-start | bytes 18436
  112.9 29.3 %all-to-all-start.4 = ((bf16[128,36,128]{2,1,0:T(8,128)(2,1)}), bf16[128,36,128]{2,1,0:T(8,128)(2,1)S(1)}, u32[]{:S(2)}, u32[]{:S(2)}) async-start(bf16[128,36,128]{2,1,0:T(8,128)(2,1)} %shard_map.358), calls=%async_computation.4 | async-start | bytes 2621440 | tf_op jit(solution)/shard_map/all_to_all | solution.py:683
  125.8 22.9 %copy-start.20 = (bf16[384,4,64]{0,2,1:T(8,128)(2,1)S(1)}, bf16[384,4,64]{0,2,1:T(8,128)(2,1)}, u32[]{:S(2)}) copy-start(bf16[384,4,64]{0,2,1:T(8,128)(2,1)} %copy.501) | copy-start | bytes 589828
  144.5 13.2 %all-to-all-start.5 = ((bf16[16,48,128]{2,1,0:T(8,128)(2,1)}), bf16[16,48,128]{2,1,0:T(8,128)(2,1)S(1)}, u32[]{:S(2)}, u32[]{:S(2)}) async-start(bf16[16,48,128]{2,1,0:T(8,128)(2,1)} %reshape.521), calls=%async_computation.5 | async-start | bytes 393216 | tf_op jit(solution)/shard_map/all_to_all | solution.py:683
  162.4 40.1 %copy-start.7 = (bf16[256,32]{1,0:T(8,128)(2,1)S(1)}, bf16[256,32]{1,0:T(8,128)(2,1)}, u32[]{:S(2)}) copy-start(bf16[256,32]{1,0:T(8,128)(2,1)} %copy-done.6) | copy-start | bytes 49156
  162.4 40.1 %copy-start.9 = (bf16[256,32]{1,0:T(8,128)(2,1)S(1)}, bf16[256,32]{1,0:T(8,128)(2,1)}, u32[]{:S(2)}) copy-start(bf16[256,32]{1,0:T(8,128)(2,1)} %copy-done.8) | copy-start | bytes 49156
  162.4 40.1 %copy-start.11 = (bf16[256,32]{1,0:T(8,128)(2,1)S(1)}, bf16[256,32]{1,0:T(8,128)(2,1)}, u32[]{:S(2)}) copy-start(bf16[256,32]{1,0:T(8,128)(2,1)} %copy-done.10) | copy-start | bytes 49156
  162.5 40.1 %all-to-all-start.6 = ((bf16[128,72,128]{2,1,0:T(8,128)(2,1)}), bf16[128,72,128]{2,1,0:T(8,128)(2,1)S(1)}, u32[]{:S(2)}, u32[]{:S(2)}) async-start(bf16[128,72,128]{2,1,0:T(8,128)(2,1)} %bitcast.234), calls=%async_computation.6 | async-start | bytes 4718592 | tf_op jit(solution)/shard_map/all_to_all | solution.py:683
  203.7 15.2 %all-to-all-start.7 = ((bf16[8,24,128]{2,1,0:T(8,128)(2,1)}), bf16[8,24,128]{2,1,0:T(8,128)(2,1)S(1)}, u32[]{:S(2)}, u32[]{:S(2)}) async-start(bf16[8,24,128]{2,1,0:T(8,128)(2,1)} %reshape.524), calls=%async_computation.7 | async-start | bytes 98304 | tf_op jit(solution)/shard_map/all_to_all | solution.py:683
  218.9 10.2 %copy-start.31 = (bf16[128,128]{0,1:T(8,128)(2,1)S(1)}, bf16[128,128]{0,1:T(8,128)(2,1)}, u32[]{:S(2)}) copy-start(bf16[128,128]{0,1:T(8,128)(2,1)} %get-tuple-element.309) | copy-start | bytes 98308
  218.9 11.7 %copy-start.13 = (bf16[96,256]{1,0:T(8,128)(2,1)S(1)}, bf16[96,256]{1,0:T(8,128)(2,1)}, u32[]{:S(2)}) copy-start(bf16[96,256]{1,0:T(8,128)(2,1)} %copy-done.12) | copy-start | bytes 147460
  219.0 29.3 %all-to-all-start.8 = ((bf16[128,36,128]{2,1,0:T(8,128)(2,1)}), bf16[128,36,128]{2,1,0:T(8,128)(2,1)S(1)}, u32[]{:S(2)}, u32[]{:S(2)}) async-start(bf16[128,36,128]{2,1,0:T(8,128)(2,1)} %shard_map.360), calls=%async_computation.8 | async-start | bytes 2621440 | tf_op jit(solution)/shard_map/all_to_all | solution.py:683
  250.2 27.5 %all-to-all-start.9 = ((f32[16,16,128]{2,1,0:T(8,128)}), f32[16,16,128]{2,1,0:T(8,128)S(1)}, u32[]{:S(2)}, u32[]{:S(2)}) async-start(f32[16,16,128]{2,1,0:T(8,128)} %reshape.528), calls=%async_computation.9 | async-start | bytes 262144 | tf_op jit(solution)/shard_map/all_to_all | solution.py:683
  382.7 27.4 %all-to-all-start.12 = ((bf16[128,36,128]{2,1,0:T(8,128)(2,1)}), bf16[128,36,128]{2,1,0:T(8,128)(2,1)S(1)}, u32[]{:S(2)}, u32[]{:S(2)}) async-start(bf16[128,36,128]{2,1,0:T(8,128)(2,1)} %bitcast.236), calls=%async_computation.12 | async-start | bytes 2621440 | tf_op jit(solution)/shard_map/all_to_all | solution.py:683
  410.1 22.3 %all-to-all-start.13 = ((bf16[128,16,128]{2,1,0:T(8,128)(2,1)}), bf16[128,16,128]{2,1,0:T(8,128)(2,1)S(1)}, u32[]{:S(2)}, u32[]{:S(2)}) async-start(bf16[128,16,128]{2,1,0:T(8,128)(2,1)} %bitcast.74), calls=%async_computation.13 | async-start | bytes 1048576 | tf_op jit(solution)/shard_map/all_to_all | solution.py:683
  432.5 10.0 %copy-start.50 = (bf16[128,8]{0,1:T(8,128)(2,1)S(1)}, bf16[128,8]{0,1:T(8,128)(2,1)}, u32[]{:S(2)}) copy-start(bf16[128,8]{0,1:T(8,128)(2,1)} %param.28) | copy-start | bytes 6148
  432.6 10.7 %copy-start.47 = (bf16[256,64]{0,1:T(8,128)(2,1)S(1)}, bf16[256,64]{0,1:T(8,128)(2,1)}, u32[]{:S(2)}) copy-start(bf16[256,64]{0,1:T(8,128)(2,1)} %param.32) | copy-start | bytes 98308
  432.6 13.1 %copy-start.42 = (f32[24,128]{1,0:T(8,128)S(1)}, f32[24,128]{1,0:T(8,128)}, u32[]{:S(2)}) copy-start(f32[24,128]{1,0:T(8,128)} %convert_reduce_fusion.4) | copy-start | bytes 36868
  432.6 42.8 %all-to-all-start.14 = ((bf16[128,72,128]{2,1,0:T(8,128)(2,1)}), bf16[128,72,128]{2,1,0:T(8,128)(2,1)S(1)}, u32[]{:S(2)}, u32[]{:S(2)}) async-start(bf16[128,72,128]{2,1,0:T(8,128)(2,1)} %shard_map.364), calls=%async_computation.14 | async-start | bytes 4718592 | tf_op jit(solution)/shard_map/all_to_all | solution.py:683
  444.0 33.5 %copy-start.26 = (f32[96,256]{1,0:T(8,128)}, f32[96,256]{1,0:T(8,128)S(1)}, u32[]{:S(2)}) copy-start(f32[96,256]{1,0:T(8,128)S(1)} %convert_element_type.217) | copy-start | bytes 294916
  447.4 30.1 %copy-start.58 = (f32[12]{0:T(128)}, f32[12]{0:T(128)S(1)}, u32[]{:S(2)}) copy-start(f32[12]{0:T(128)S(1)} %broadcast_multiply_fusion.6) | copy-start | bytes 148
  478.6 39.6 %all-to-all-start.15 = ((bf16[128,32,128]{2,1,0:T(8,128)(2,1)}), bf16[128,32,128]{2,1,0:T(8,128)(2,1)S(1)}, u32[]{:S(2)}, u32[]{:S(2)}) async-start(bf16[128,32,128]{2,1,0:T(8,128)(2,1)} %broadcast_in_dim.44), calls=%async_computation.15 | async-start | bytes 2097152 | tf_op jit(solution)/shard_map/all_to_all | solution.py:683
  524.1 26.8 %all-to-all-start.16 = ((bf16[128,22,128]{2,1,0:T(8,128)(2,1)}), bf16[128,22,128]{2,1,0:T(8,128)(2,1)}, u32[]{:S(2)}, u32[]{:S(2)}) async-start(bf16[128,22,128]{2,1,0:T(8,128)(2,1)} %pad_maximum_fusion.1), calls=%async_computation.16 | async-start | bytes 1572864 | tf_op jit(solution)/shard_map/all_to_all | solution.py:683
  539.3 12.9 %copy-start.48 = (bf16[256,64]{0,1:T(8,128)(2,1)S(1)}, bf16[256,64]{0,1:T(8,128)(2,1)}, u32[]{:S(2)}) copy-start(bf16[256,64]{0,1:T(8,128)(2,1)} %param.32) | copy-start | bytes 98308
  539.3 12.9 %copy-start.59 = (f32[12]{0:T(128)S(1)}, f32[12]{0:T(128)}, u32[]{:S(2)}) copy-start(f32[12]{0:T(128)} %copy-done.58) | copy-start | bytes 148
  539.3 12.9 %copy-start.61 = (f32[256]{0:T(256)S(1)}, f32[256]{0:T(256)}, u32[]{:S(2)}) copy-start(f32[256]{0:T(256)} %param.31) | copy-start | bytes 3076
  539.3 12.9 %copy-start.67 = (f32[12]{0:T(128)S(1)}, f32[12]{0:T(128)}, u32[]{:S(2)}) copy-start(f32[12]{0:T(128)} %add_rsqrt_fusion.2) | copy-start | bytes 148
  539.3 14.8 %copy-start.40 = (f32[1,12,256]{2,1,0:T(8,128)S(1)}, f32[1,12,256]{2,1,0:T(8,128)}, u32[]{:S(2)}) copy-start(f32[1,12,256]{2,1,0:T(8,128)} %get-tuple-element.303) | copy-start | bytes 36868
  554.8 9.2 %all-to-all-start.17 = ((f32[8,48,128]{2,1,0:T(8,128)}), f32[8,48,128]{2,1,0:T(8,128)S(1)}, u32[]{:S(2)}, u32[]{:S(2)}) async-start(f32[8,48,128]{2,1,0:T(8,128)} %broadcast_in_dim.100), calls=%async_computation.17 | async-start | bytes 393216 | tf_op jit(solution)/shard_map/all_to_all | solution.py:683
  564.9 19.3 %all-to-all-start.18 = ((bf16[128,16,128]{2,1,0:T(8,128)(2,1)}), bf16[128,16,128]{2,1,0:T(8,128)(2,1)S(1)}, u32[]{:S(2)}, u32[]{:S(2)}) async-start(bf16[128,16,128]{2,1,0:T(8,128)(2,1)} %broadcast_in_dim.101), calls=%async_computation.18 | async-start | bytes 1048576 | tf_op jit(solution)/shard_map/all_to_all | solution.py:683
  571.2 14.3 %copy-start.23 = (bf16[256,64]{1,0:T(8,128)(2,1)S(1)}, bf16[256,64]{1,0:T(8,128)(2,1)}, u32[]{:S(2)}) copy-start(bf16[256,64]{1,0:T(8,128)(2,1)} %copy.561) | copy-start | bytes 98308
  (45 other events, 164.9 us)

commit v2 on v1

v2 whole, which is shorter than its diff:
```python
import functools

import jax
import jax.numpy as jnp
import ml_dtypes
import numpy as np
from jax import lax
from jax.experimental import pallas as pl
from jax.experimental.pallas import tpu as pltpu
from jax.sharding import PartitionSpec as P

D = 256
C = 128
H = 8
HD = 32
CH = 128
OP = 32
FT = 512
ITEMS = 4
EPS = 1e-05
BOTH = ("row", "col")
F32 = jnp.float32
BF16 = jnp.bfloat16
HALF = 64
JH = 3
VMEM = 60 * 1024 * 1024
SMALL_VMEM = 28 * 1024 * 1024


def half(values):
    return values.astype(BF16)


def dot(lhs, rhs, lhs_dim, rhs_dim):
    return lax.dot_general(
        lhs, rhs, (((lhs_dim,), (rhs_dim,)), ((), ())), preferred_element_type=F32
    )


def sigmoid(values):
    return 0.5 * jnp.tanh(0.5 * values) + 0.5


def norm_parts(values):
    scale = 1.0 / values.shape[0]
    centered = values - jnp.sum(values, axis=0, keepdims=True) * scale
    spread = jnp.sum(centered * centered, axis=0, keepdims=True) * scale
    inv = lax.rsqrt(spread + EPS)
    return centered * inv, inv


def norm_back(unit, inv, gain, grad):
    scale = 1.0 / unit.shape[0]
    scaled = grad * gain
    first = jnp.sum(scaled, axis=0, keepdims=True) * scale
    second = jnp.sum(scaled * unit, axis=0, keepdims=True) * scale
    return inv * (scaled - first - unit * second)


def lane_rows_of(width):
    return [(m, slice(128 * m, 128 * m + 128)) for m in range(width // 128)]


def tile_rows_of(ref):
    items, parts, rows = ref.shape[:3]
    return jnp.concatenate(
        [ref[b, h, m] for m in range(rows) for h in range(parts) for b in range(items)],
        axis=0,
    )


def put_tile(ref, m, values):
    items, parts, _, cols = ref.shape[:4]
    flipped = jnp.transpose(values)
    start = 0
    for h in range(parts):
        for b in range(items):
            ref[b, h, m] = flipped[start : start + cols]
            start += cols


def low_lanes(rows):
    return lax.broadcasted_iota(jnp.int32, (rows, 128), 1) < HALF


def swap(values):
    return pltpu.roll(values, HALF, 1)


def put_double(ref, m, left, right):
    low = low_lanes(left.shape[0])
    ref[0, 0, m] = half(jnp.where(low, left, swap(right)))
    ref[0, 1, m] = half(jnp.where(low, swap(left), right))


def get_double(ref, m):
    low = low_lanes(ref.shape[3])
    one, two = ref[0, 0, m].astype(F32), ref[0, 1, m].astype(F32)
    return jnp.where(low, one, swap(two)), jnp.where(low, swap(one), two)


def add_to(ref, values):
    @pl.when(pl.program_id(0) == 0)
    def _():
        ref[...] = values

    @pl.when(pl.program_id(0) != 0)
    def _():
        ref[...] += values


def add_diagonal(ref, total_ref, grad_ref, unit_ref):
    add_to(total_ref, dot(grad_ref[...], unit_ref[...], 1, 1))

    @pl.when(pl.program_id(0) == pl.num_programs(0) - 1)
    def _():
        rows = lax.broadcasted_iota(jnp.int32, total_ref.shape, 0)
        cols = lax.broadcasted_iota(jnp.int32, total_ref.shape, 1)
        picked = jnp.where(rows == cols, total_ref[...], 0.0)
        ref[...] = jnp.broadcast_to(jnp.sum(picked, axis=0, keepdims=True), ref.shape)


def bias_kernel(pair_ref, eye_ref, wb_ref, wd_ref, dist_ref, x_ref, bias_ref):
    x_chan = half(dot(eye_ref[...], tile_rows_of(pair_ref), 1, 1))
    x_ref[...] = x_chan
    bias_ref[...] = half(dot(wb_ref[...], x_chan, 0, 0) + wd_ref[...] * dist_ref[...])


def cotangent_kernel(cot_ref, eye_ref, wdown_plain_ref, out_ref, dact_ref):
    cot = half(dot(eye_ref[...], tile_rows_of(cot_ref), 1, 1))
    out_ref[...] = cot
    dact_ref[...] = half(dot(wdown_plain_ref[...], cot, 1, 0))


def put_sides(proj_ref, keep_ref, sides_ref, wide_ref):
    count = keep_ref.shape[1]
    for m, here in lane_rows_of(proj_ref.shape[1]):
        keep = keep_ref[0, m : m + 1, :]
        left = sigmoid(proj_ref[CH : 2 * CH, here]) * proj_ref[:CH, here] * keep
        right = (
            sigmoid(proj_ref[3 * CH : 4 * CH, here]) * proj_ref[2 * CH : 3 * CH, here] * keep
        )
        low = low_lanes(left.shape[0])
        wide_ref[:, m, :] = jnp.where(low, left, swap(right))
        wide_ref[:, m + count, :] = jnp.where(low, swap(left), right)
    sides_ref[...] = half(wide_ref[...])


def diagonal_blocks(right):
    which = lax.broadcasted_iota(jnp.int32, (8, 128), 0)
    lane = lax.broadcasted_iota(jnp.int32, (8, 128), 1) // 16
    same = (which == lane).astype(F32)
    return half(jnp.concatenate([same * right[q : q + 1] for q in range(OP)], axis=0))


def node_kernel(node_ref, col_ref, gain_ref, wab_ref, wout_ref, perm_ref, mid_ref, right_ref):
    def normed(ref):
        values = ref[...].astype(F32)
        scale = 1.0 / values.shape[1]
        centered = values - jnp.sum(values, axis=1, keepdims=True) * scale
        spread = jnp.sum(centered * centered, axis=1, keepdims=True) * scale
        return half(centered * lax.rsqrt(spread + EPS) * gain_ref[...])

    left = half(dot(wab_ref[...], normed(node_ref), 0, 1))
    mid_ref[...] = dot(left[:OP], wout_ref[...], 0, 0)
    right = half(dot(wab_ref[...], normed(col_ref), 0, 1))
    right = dot(right[OP:], perm_ref[...], 1, 0)
    for j in range(JH):
        right_ref[j] = right[:, 128 * j : 128 * j + 128]


def open_kernel(
    pair_ref,
    eye_ref,
    mid_ref,
    bd_ref,
    bout_ref,
    keep_ref,
    gain_ref,
    w_ref,
    one_ref,
    sides_ref,
    mids_ref,
    mid_t_ref,
    outer_ref,
    normed_ref,
    proj_ref,
    x_ref,
    wide_ref,
):
    @pl.when(pl.program_id(0) == 0)
    def _():
        for m in range(mids_ref.shape[1] // 128):
            rows = [
                mid_ref[8 * m : 8 * m + 8, 128 * q : 128 * q + 128] for q in range(OP)
            ]
            stack = jnp.concatenate(rows, axis=0)
            mids_ref[:, 128 * m : 128 * m + 128] = half(stack)
            mid_t_ref[128 * m : 128 * m + 128, :] = half(jnp.transpose(stack))

    x_ref[...] = half(dot(eye_ref[...], tile_rows_of(pair_ref), 1, 1))
    outer_ref[...] = dot(mid_t_ref[...], diagonal_blocks(bd_ref[0]), 1, 0)
    for m, here in lane_rows_of(x_ref.shape[1]):
        outer = outer_ref[128 * m : 128 * m + 128, :]
        keep = keep_ref[0, m : m + 1, :]
        pair_one = x_ref[:, here].astype(F32) + keep * (outer + bout_ref[0])
        one_ref[:, here] = pair_one
        unit, _ = norm_parts(pair_one)
        normed_ref[:, here] = half(unit * gain_ref[0])
    proj_ref[...] = dot(w_ref[0, :, : 4 * CH], normed_ref[...], 0, 0)
    put_sides(proj_ref, keep_ref, sides_ref, wide_ref)


def factor_kernel(
    in_ref, keep_ref, gain_ref, w_ref, unit_ref, inv_ref, normed_ref, factor_ref, *rest
):
    proj_ref = rest[-1]
    for _, here in lane_rows_of(in_ref.shape[1]):
        unit, inv = norm_parts(in_ref[:, here])
        unit_ref[:, here] = half(unit)
        inv_ref[:, here] = inv
        normed_ref[:, here] = half(unit * gain_ref[0])
    proj_ref[...] = dot(w_ref[0], normed_ref[...], 0, 0)
    for m, here in lane_rows_of(in_ref.shape[1]):
        keep = keep_ref[0, m : m + 1, :]
        for side in range(2):
            start = 2 * CH * side
            sig = sigmoid(proj_ref[start + CH : start + 2 * CH, here])
            first = keep * sig
            factor_ref[start : start + CH, here] = half(first)
            factor_ref[start + CH : start + 2 * CH, here] = half(
                first * proj_ref[start : start + CH, here] * (1.0 - sig)
            )
        if len(rest) > 1:
            rest[0][:, here] = half(sigmoid(proj_ref[4 * CH :, here]))


def rear_kernel(
    prod_ref, gate_ref, gout_ref, wout_ref, unit_ref, inv_ref, slope_ref, y_ref, update_ref
):
    for m, here in lane_rows_of(gate_ref.shape[1]):
        unit, inv = norm_parts(prod_ref[m].astype(F32))
        unit_ref[:, here] = half(unit)
        inv_ref[:, here] = inv
        y_ref[:, here] = half(unit * gout_ref[0])
    update_ref[...] = dot(wout_ref[0], y_ref[...], 0, 0)
    for _, here in lane_rows_of(gate_ref.shape[1]):
        gate = gate_ref[:, here].astype(F32)
        slope_ref[:, here] = half(update_ref[:, here] * gate * (1.0 - gate))


def middle_kernel(
    one_ref,
    gate_ref,
    prod_ref,
    keep_ref,
    gout_ref,
    wout_ref,
    gin_ref,
    w_ref,
    two_ref,
    sides_ref,
    gate_out_ref,
    y_ref,
    update_ref,
    proj_ref,
    wide_ref,
):
    for m, here in lane_rows_of(one_ref.shape[1]):
        unit, _ = norm_parts(prod_ref[m].astype(F32))
        y_ref[:, here] = half(unit * gout_ref[0])
    update_ref[...] = dot(wout_ref[0], y_ref[...], 0, 0)
    for _, here in lane_rows_of(one_ref.shape[1]):
        pair_two = one_ref[:, here] + gate_ref[:, here].astype(F32) * update_ref[:, here]
        two_ref[:, here] = pair_two
        unit, _ = norm_parts(pair_two)
        y_ref[:, here] = half(unit * gin_ref[0])
    proj_ref[...] = dot(w_ref[0], y_ref[...], 0, 0)
    put_sides(proj_ref, keep_ref, sides_ref, wide_ref)
    for _, here in lane_rows_of(one_ref.shape[1]):
        gate_out_ref[:, here] = half(sigmoid(proj_ref[4 * CH :, here]))


def transition(two_ref, gate_ref, prod_ref, gout_ref, wout_ref, gtr_ref, wup_ref, refs):
    y_ref, prod_unit_ref, prod_inv_ref, update_ref = refs[:4]
    three_ref, xt_ref, tr_unit_ref, tr_inv_ref, hidden_ref = refs[4:]
    rows = lane_rows_of(two_ref.shape[1])
    for m, here in rows:
        unit, inv = norm_parts(prod_ref[m].astype(F32))
        if prod_unit_ref is not None:
            prod_inv_ref[:, here] = inv
            prod_unit_ref[:, here] = half(unit)
        y_ref[:, here] = half(unit * gout_ref[0])
    update_ref[...] = dot(wout_ref[0], y_ref[...], 0, 0)
    for _, here in rows:
        pair_three = (
            two_ref[:, here] + gate_ref[:, here].astype(F32) * update_ref[:, here]
        )
        if three_ref is not None:
            three_ref[:, here] = pair_three
        unit, inv = norm_parts(pair_three)
        if tr_unit_ref is not None:
            tr_inv_ref[:, here] = inv
            tr_unit_ref[:, here] = half(unit)
        xt_ref[:, here] = half(unit * gtr_ref[0])
    hidden_ref[...] = dot(wup_ref[...], xt_ref[...], 0, 0)


def put_hidden_back(hidden_ref, dact_ref, dhid_ref, active_ref=None):
    for _, here in lane_rows_of(hidden_ref.shape[1]):
        for start in range(0, FT, CH):
            part = slice(start, start + CH)
            hidden = hidden_ref[part, here]
            sig = sigmoid(hidden)
            act32 = hidden * sig
            if active_ref is not None:
                active_ref[part, here] = half(act32)
            dhid_ref[part, here] = half(
                dact_ref[part, here].astype(F32) * (sig + act32 * (1.0 - sig))
            )


def turn_kernel(
    two_ref,
    gate_ref,
    prod_ref,
    cot_ref,
    dact_ref,
    gout_ref,
    wout_ref,
    gtr_ref,
    wup_ref,
    grad_ref,
    dprod_ref,
    dgtr_ref,
    dgout_ref,
    small_ref,
    xt_ref,
    tr_unit_ref,
    tr_inv_ref,
    prod_unit_ref,
    prod_inv_ref,
    update_ref,
    hidden_ref,
    dhid_ref,
    tr_total_ref,
    out_total_ref,
):
    rows = lane_rows_of(two_ref.shape[1])
    refs = (small_ref, prod_unit_ref, prod_inv_ref, update_ref)
    refs += (None, xt_ref, tr_unit_ref, tr_inv_ref, hidden_ref)
    transition(two_ref, gate_ref, prod_ref, gout_ref, wout_ref, gtr_ref, wup_ref, refs)
    put_hidden_back(hidden_ref, dact_ref, dhid_ref)
    small_ref[...] = half(dot(wup_ref[...], dhid_ref[...], 1, 0))
    for _, here in rows:
        grad = cot_ref[:, here].astype(F32) + norm_back(
            tr_unit_ref[:, here].astype(F32),
            tr_inv_ref[:, here],
            gtr_ref[0],
            small_ref[:, here].astype(F32),
        )
        grad_ref[:, here] = grad
        xt_ref[:, here] = half(grad * gate_ref[:, here].astype(F32))
    add_diagonal(dgtr_ref, tr_total_ref, small_ref, tr_unit_ref)
    small_ref[...] = half(dot(wout_ref[0], xt_ref[...], 1, 0))
    put_product_back(dprod_ref, prod_unit_ref, prod_inv_ref, gout_ref, small_ref)
    add_diagonal(dgout_ref, out_total_ref, small_ref, prod_unit_ref)


def put_product_back(dprod_ref, unit_ref, inv_ref, gain_ref, dy_ref):
    for m, here in lane_rows_of(unit_ref.shape[1]):
        dprod_ref[m] = half(
            norm_back(
                unit_ref[:, here].astype(F32),
                inv_ref[:, here],
                gain_ref[0],
                dy_ref[:, here].astype(F32),
            )
        )


def finish_kernel(
    two_ref,
    gate_ref,
    prod_ref,
    cot_ref,
    dact_ref,
    grad_ref,
    gout_ref,
    wout_ref,
    gtr_ref,
    wup_ref,
    wdown_ref,
    out_ref,
    dwdown_ref,
    dwup_ref,
    dwout_ref,
    y_ref,
    xt_ref,
    update_ref,
    three_ref,
    hidden_ref,
    dhid_ref,
    active_ref,
    dwup_t_ref,
):
    refs = (y_ref, None, None, update_ref, three_ref, xt_ref, None, None, hidden_ref)
    transition(two_ref, gate_ref, prod_ref, gout_ref, wout_ref, gtr_ref, wup_ref, refs)
    put_hidden_back(hidden_ref, dact_ref, dhid_ref, active_ref)
    update_ref[...] = dot(wdown_ref[...], active_ref[...], 0, 0)
    for m, here in lane_rows_of(two_ref.shape[1]):
        put_tile(out_ref, m, three_ref[:, here] + update_ref[:, here])
    add_to(dwdown_ref, dot(active_ref[...], cot_ref[...], 1, 1))
    add_to(dwup_t_ref, dot(dhid_ref[...], xt_ref[...], 1, 1))
    d_update = half(grad_ref[...] * gate_ref[...].astype(F32))
    add_to(dwout_ref, dot(y_ref[...], d_update, 1, 1))

    @pl.when(pl.program_id(0) == pl.num_programs(0) - 1)
    def _():
        put_flipped(dwup_ref, dwup_t_ref)


def put_front_grads(sides_ref, factor_ref, slope_ref, grad_ref, dproj_ref):
    for m, here in lane_rows_of(grad_ref.shape[1]):
        sides = get_double(sides_ref, m)
        for at in range(4):
            part = slice(CH * at, CH * at + CH)
            dproj_ref[part, here] = half(sides[at // 2] * factor_ref[part, here].astype(F32))
        dproj_ref[4 * CH :, here] = half(grad_ref[:, here] * slope_ref[:, here].astype(F32))


def front_back(unit_ref, inv_ref, gain_ref, dn_ref, here):
    return norm_back(
        unit_ref[:, here].astype(F32),
        inv_ref[:, here],
        gain_ref[0],
        dn_ref[:, here].astype(F32),
    )


def back_kernel(
    dsides_ref,
    factor_ref,
    slope_ref,
    unit_ref,
    inv_ref,
    grad_ref,
    gin_ref,
    w_ref,
    gate_ref,
    prod_unit_ref,
    prod_inv_ref,
    gout_ref,
    wout_ref,
    grad_out_ref,
    dprod_ref,
    dgin_ref,
    dgout_ref,
    dproj_ref,
    dupd_ref,
    small_ref,
    in_total_ref,
    out_total_ref,
):
    put_front_grads(dsides_ref, factor_ref, slope_ref, grad_ref, dproj_ref)
    small_ref[...] = half(dot(w_ref[0], dproj_ref[...], 1, 0))
    for _, here in lane_rows_of(grad_ref.shape[1]):
        grad = grad_ref[:, here] + front_back(unit_ref, inv_ref, gin_ref, small_ref, here)
        grad_out_ref[:, here] = grad
        dupd_ref[:, here] = half(grad * gate_ref[:, here].astype(F32))
    add_diagonal(dgin_ref, in_total_ref, small_ref, unit_ref)
    small_ref[...] = half(dot(wout_ref[0], dupd_ref[...], 1, 0))
    put_product_back(dprod_ref, prod_unit_ref, prod_inv_ref, gout_ref, small_ref)
    add_diagonal(dgout_ref, out_total_ref, small_ref, prod_unit_ref)


def put_flipped(out_ref, total_ref):
    for start in range(0, total_ref.shape[0], 128):
        out_ref[start : start + 128, :] = jnp.transpose(total_ref[start : start + 128, :])


def weights_kernel(
    dsides_ref,
    factor_ref,
    slope_ref,
    grad_ref,
    normed_ref,
    next_grad_ref,
    gate_ref,
    prod_unit_ref,
    gout_ref,
    dbias_ref,
    x_ref,
    dwin_ref,
    dwout_ref,
    dwb_ref,
    dproj_ref,
    dwin_t_ref,
):
    put_front_grads(dsides_ref, factor_ref, slope_ref, grad_ref, dproj_ref)
    add_to(dwin_t_ref, dot(dproj_ref[...], normed_ref[...], 1, 1))

    @pl.when(pl.program_id(0) == pl.num_programs(0) - 1)
    def _():
        put_flipped(dwin_ref, dwin_t_ref)

    d_update = half(next_grad_ref[...] * gate_ref[...].astype(F32))
    y_half = half(prod_unit_ref[...].astype(F32) * gout_ref[0])
    add_to(dwout_ref, dot(y_half, d_update, 1, 1))
    add_to(dwb_ref, dot(dbias_ref[...], x_ref[...], 1, 1))


def close_kernel(
    dsides_ref,
    factor_ref,
    slope_ref,
    unit_ref,
    inv_ref,
    grad_ref,
    keep_ref,
    gin_ref,
    w_ref,
    mids_ref,
    bd_ref,
    dbias_ref,
    wb_ref,
    out_ref,
    dmid_ref,
    dwin_ref,
    dgin_ref,
    dright_ref,
    dbout_ref,
    dproj_ref,
    small_ref,
    outer_ref,
    in_total_ref,
    dmid_t_ref,
    bias_ref,
    dwin_t_ref,
):
    put_front_grads(dsides_ref, factor_ref, slope_ref, grad_ref, dproj_ref)
    small_ref[...] = half(dot(w_ref[0], dproj_ref[...], 1, 0))
    bias_ref[...] = dot(wb_ref[...], dbias_ref[...], 1, 0)
    total = None
    for m, here in lane_rows_of(grad_ref.shape[1]):
        grad = grad_ref[:, here] + front_back(unit_ref, inv_ref, gin_ref, small_ref, here)
        put_tile(out_ref, m, grad + bias_ref[:, here])
        outer = grad * keep_ref[0, m : m + 1, :]
        outer_ref[128 * m : 128 * m + 128, :] = half(outer)
        total = outer if total is None else total + outer
    normed = half(unit_ref[...].astype(F32) * gin_ref[0])
    add_to(dmid_t_ref, dot(outer_ref[...], diagonal_blocks(bd_ref[0]), 1, 1))
    right = dot(mids_ref[...], outer_ref[...], 1, 0)
    which = lax.broadcasted_iota(jnp.int32, (8, 128), 0)
    lane = lax.broadcasted_iota(jnp.int32, (8, 128), 1) // 16
    for q in range(OP):
        picked = jnp.where(which == lane, right[8 * q : 8 * q + 8], 0.0)
        dright_ref[0, q : q + 1, :] = jnp.sum(picked, axis=0, keepdims=True)
    add_to(dwin_t_ref, dot(dproj_ref[...], normed, 1, 1))
    ones = jnp.ones((8, 128), F32)
    add_to(
        dbout_ref,
        lax.dot_general(
            ones,
            total,
            (((1,), (1,)), ((), ())),
            preferred_element_type=F32,
            precision=lax.Precision.HIGHEST,
        ),
    )
    add_diagonal(dgin_ref, in_total_ref, small_ref, unit_ref)

    @pl.when(pl.program_id(0) == pl.num_programs(0) - 1)
    def _():
        for m in range(dmid_t_ref.shape[0] // 128):
            stack = jnp.transpose(dmid_t_ref[128 * m : 128 * m + 128, :])
            for q in range(OP):
                dmid_ref[8 * m : 8 * m + 8, 128 * q : 128 * q + 128] = stack[
                    8 * q : 8 * q + 8
                ]
        put_flipped(dwin_ref, dwin_t_ref)


def tail_kernel(count, *refs):
    weight_refs, refs = refs[:count], refs[count:]
    dmid_ref, left_ref, wouter_ref, unit_ref, dright_ref, col_unit_ref = refs[:6]
    wouter_pad_ref, pick_left_ref, pick_right_ref, mask_ref = refs[6:10]
    out_ref, outer_ref, small_ref = refs[10:]
    d_mid = half(dmid_ref[...])
    outer = dot(left_ref[...], d_mid, 0, 0)
    for q in range(OP):
        outer_ref[OP * q : OP * q + OP, :] = outer[:, 128 * q : 128 * q + 128]
    d_left = dot(d_mid, wouter_ref[...], 1, 1)
    sums = [dot(half(d_left), unit_ref[...], 0, 0)]
    total = None
    for j in range(JH):
        part = dot(half(dright_ref[j]), col_unit_ref[j], 1, 0)
        total = part if total is None else total + part
    sums = jnp.concatenate(sums + [total], axis=0)
    small_ref[: 2 * OP, :] = sums[:, :128]
    small_ref[2 * OP :, :] = sums[:, 128:]
    lefts, rights = None, [None, None]
    for s in range(2):
        part = half(dot(d_mid, wouter_pad_ref[s], 1, 1))
        part = dot(pick_left_ref[s], part, 1, 0)
        lefts = part if lefts is None else lefts + part
        for j in range(JH):
            above = jnp.zeros((HALF * s + OP, 128), F32)
            spread = [above, dright_ref[j]]
            if s == 0:
                spread.append(jnp.zeros((HALF, 128), F32))
            spread = jnp.concatenate(spread, axis=0)
            spread = half(jnp.transpose(spread))
            for h in range(2):
                part = dot(pick_right_ref[h, s, j], spread, 1, 0)
                rights[h] = part if rights[h] is None else rights[h] + part
    sources = list(weight_refs) + [outer_ref, small_ref]
    pieces = [(ref, at) for ref in sources for at in range(0, ref.shape[0], 8)]
    rows = mask_ref.shape[0] // 2
    cols = out_ref.shape[0] // rows
    for r in range(rows):
        nodes = mask_ref[r : r + 1] * lefts + mask_ref[rows + r : rows + r + 1] * rights[r % 2]
        for c in range(cols):
            at = 3 * (r * cols + c)
            parts = [ref[k : k + 8, :] for ref, k in pieces[at : at + 3]]
            parts += [jnp.zeros((8, 128), F32)] * (3 - len(parts))
            out_ref[r * cols + c] = half(
                jnp.concatenate(parts + [nodes[8 * c : 8 * c + 8]], axis=0)
            )


def item_masks(items, cols, dtype):
    lane = lax.broadcasted_iota(jnp.int32, (1, 256 * cols), 1) % 256
    which = (lane // 16) % items
    return [((which == b) & (lane < JH * HALF)).astype(F32).astype(dtype) for b in range(items)]


def spread_items(piece, masks):
    parts = [piece[16 * j : 16 * j + 16] * mask for j in range(JH) for mask in masks]
    return jnp.concatenate(
        parts + [jnp.zeros((HALF, piece.shape[1]), piece.dtype)], axis=0
    )


def pick_items(values, masks):
    rows = []
    for j in range(JH):
        total = None
        for b, mask in enumerate(masks):
            start = HALF * j + 16 * b
            part = values[start : start + 16] * mask
            total = part if total is None else total + part
        rows.append(total)
    return jnp.concatenate(rows, axis=0)


def split_lanes(one, two, three):
    low = low_lanes(one.shape[0])
    return (
        jnp.concatenate([jnp.where(low, one, swap(two)), three], axis=1),
        jnp.concatenate([jnp.where(low, swap(one), two), swap(three)], axis=1),
    )


def join_lanes(left, right):
    low = low_lanes(left.shape[0])
    return (
        jnp.where(low, left[:, :128], swap(right[:, :128])),
        jnp.where(low, swap(left[:, :128]), right[:, :128]),
        jnp.where(low, left[:, 128:], swap(right[:, 128:])),
    )


def thirds(values):
    rows = values.shape[0] // JH
    return [values[rows * j : rows * (j + 1)] for j in range(JH)]


def block_lanes(q):
    return pl.ds(pl.multiple_of(q * 256, 256), 256)


def load_double(ref, cols, l_ref, r_ref):
    def step(q, carry):
        for r in range(0, ref.shape[0] // cols, 2):
            left, right = [], []
            for h in range(2):
                one, two = split_lanes(*thirds(ref[(r + h) * cols + q].astype(F32)))
                left.append(one)
                right.append(two)
            rows = slice(24 * r, 24 * r + 48)
            l_ref[rows, block_lanes(q)] = half(jnp.concatenate(left, axis=0))
            r_ref[rows, block_lanes(q)] = half(jnp.concatenate(right, axis=0))
        return carry

    lax.fori_loop(0, cols, step, 0)


def load_single(ref, cols, x_ref):
    def step(q, carry):
        for r in range(0, ref.shape[0] // cols, 2):
            parts = []
            for h in range(2):
                parts += split_lanes(*thirds(ref[(r + h) * cols + q].astype(F32)))
            rows = slice(24 * r, 24 * r + 48)
            x_ref[rows, block_lanes(q)] = half(jnp.concatenate(parts, axis=0))
        return carry

    lax.fori_loop(0, cols, step, 0)


def put_slab(ref, at, left, right):
    ref[at] = half(jnp.concatenate(join_lanes(left, right), axis=0))


def rows_at(at):
    return pl.ds(pl.multiple_of(at * 48, 16), 48)


def stack_blocks(piece_of, cols, masks):
    return jnp.concatenate([spread_items(piece_of(q), masks) for q in range(cols)], axis=0)


def unpack_kernel(s_ref, l_ref, r_ref):
    load_double(s_ref, l_ref.shape[1] // 256, l_ref, r_ref)


def out_product_kernel(s_ref, p_ref, l_ref, r_ref):
    residues, cols = l_ref.shape[0], l_ref.shape[1] // 256
    masks = item_masks(ITEMS, cols, BF16)
    load_double(s_ref, cols, l_ref, r_ref)

    def step(at, carry):
        total = dot(l_ref[...], spread_items(r_ref[rows_at(at), :], masks), 1, 1)
        for r in range(residues // 24):
            tile = total[24 * r : 24 * r + 24]
            put_slab(p_ref, r * cols + at, tile[:12], tile[12:])
        return carry

    lax.fori_loop(0, cols, step, 0)


def flip(values, eye):
    return half(dot(eye, values, 1, 1))


def flip_all(ref, eye_ref, out_ref):
    for q in range(ref.shape[1] // 256):
        part = slice(256 * q, 256 * q + 256)
        out_ref[part, :] = flip(ref[:, part], eye_ref[...])


def in_product_kernel(s_ref, eye_ref, p_ref, l_ref, r_ref, f_ref):
    cols = l_ref.shape[1] // 256
    masks = item_masks(ITEMS, 1, F32)
    load_double(s_ref, cols, l_ref, r_ref)
    flip_all(l_ref, eye_ref, f_ref)

    def step(q, carry):
        total = dot(f_ref[...], r_ref[:, block_lanes(q)], 1, 0)
        for at in range(cols):
            rows = pick_items(total[256 * at : 256 * at + 256], masks)
            for h in range(2):
                tile = rows[24 * h : 24 * h + 24]
                put_slab(p_ref, (2 * at + h) * cols + q, tile[:12], tile[12:])
        return carry

    lax.fori_loop(0, cols, step, 0)


def in_back_kernel(l_ref, r_ref, dp_ref, d_ref, x_ref):
    residues, cols = l_ref.shape[0], l_ref.shape[1] // 256
    masks = item_masks(ITEMS, cols, BF16)
    one_masks = item_masks(ITEMS, 1, BF16)
    load_single(dp_ref, cols, x_ref)

    def step(at, carry):
        left = dot(r_ref[...], spread_items(x_ref[rows_at(at), :], masks), 1, 1)
        wide = stack_blocks(
            lambda q: x_ref[48 * q : 48 * q + 48, block_lanes(at)], cols, one_masks
        )
        right = dot(l_ref[...], wide, 1, 0)
        for r in range(residues // 24):
            rows = slice(24 * r, 24 * r + 24)
            put_slab(d_ref, r * cols + at, left[rows], right[rows])
        return carry

    lax.fori_loop(0, cols, step, 0)


def out_back_kernel(l_ref, r_ref, dp_ref, eye_ref, d_ref, x_ref, g_ref, f_ref):
    residues, cols = l_ref.shape[0], l_ref.shape[1] // 256
    masks = item_masks(ITEMS, 1, F32)
    one_masks = item_masks(ITEMS, 1, BF16)
    load_single(dp_ref, cols, x_ref)
    flip_all(x_ref, eye_ref, f_ref)

    def right_step(q, carry):
        total = dot(f_ref[...], l_ref[:, block_lanes(q)], 1, 0)
        for at in range(cols):
            g_ref[48 * at : 48 * at + 48, block_lanes(q)] = pick_items(
                total[256 * at : 256 * at + 256], masks
            )
        return carry

    lax.fori_loop(0, cols, right_step, 0)

    def left_step(at, carry):
        wide = stack_blocks(
            lambda q: r_ref[48 * q : 48 * q + 48, block_lanes(at)], cols, one_masks
        )
        left = dot(x_ref[...], wide, 1, 0)
        for r in range(residues // 24):
            rows = slice(24 * r, 24 * r + 24)
            put_slab(d_ref, r * cols + at, left[rows], g_ref[rows, block_lanes(at)])
        return carry

    lax.fori_loop(0, cols, left_step, 0)


def cost(flops, nbytes):
    return pl.CostEstimate(flops=int(flops), bytes_accessed=int(nbytes), transcendentals=0)


def call(kernel, steps, ins, outs, flops, scratch=(), vmem=VMEM):
    nbytes = sum(a.size * a.dtype.itemsize for a, _, _ in ins)
    nbytes += sum(s.size * s.dtype.itemsize for s, _, _ in outs)
    return pl.pallas_call(
        kernel,
        grid=(steps,),
        in_specs=[pl.BlockSpec(block, index) for _, block, index in ins],
        out_specs=[pl.BlockSpec(block, index) for _, block, index in outs],
        out_shape=[shape for shape, _, _ in outs],
        scratch_shapes=list(scratch),
        compiler_params=pltpu.CompilerParams(vmem_limit_bytes=vmem),
        cost_estimate=cost(flops, nbytes),
        name=getattr(kernel, "__name__", "tail_kernel"),
    )(*[a for a, _, _ in ins])


def whole(array):
    rank = len(array.shape)
    return (array, tuple(array.shape), lambda s: (0,) * rank)


def sds(shape, dtype):
    return jax.ShapeDtypeStruct(shape, dtype)


def per_device(
    node_feats,
    pair_feats,
    distances,
    lengths,
    node_cotan,
    pair_cotan,
    w_qkv,
    w_bias,
    w_dist,
    w_node_out,
    g_node,
    w_ab,
    w_outer,
    b_outer,
    g_tin,
    w_tin,
    g_tout,
    w_tout,
    g_trans,
    w_up,
    w_down,
):
    row_count = lax.axis_size("row")
    col_count = lax.axis_size("col")
    row_index = lax.axis_index("row")
    col_index = lax.axis_index("col")
    items, tile_rows, tile_cols = pair_feats.shape[:3]
    residues = tile_rows * row_count
    devices = row_count * col_count
    il, jl = tile_rows // 2, tile_cols // JH
    lane_rows = JH * il
    slots = lane_rows * 128
    steps = JH
    width = il * 128
    score_scale = HD ** (-0.5)

    def chan(array):
        return (array, (array.shape[0], width), lambda s: (0, s))

    def rows_of(array):
        return (array, (il, C, 128), lambda s: (s, 0, 0))

    def double(array):
        return (array, (1, 2, il, C, 128), lambda s: (s, 0, 0, 0, 0))

    def tile(array):
        return (array, (items, 2, il, jl, C), lambda s: (0, 0, 0, s, 0))

    def f_chan():
        return chan(sds((C, slots), F32))

    def f_whole(*shape):
        return whole(sds(shape, F32))

    columns = jnp.concatenate([b_outer[None], g_tin, g_tout, g_trans[None]], axis=0)
    columns = columns[:, :, None]

    def column(which):
        return (columns, (1, C, 1), lambda s: (which, 0, 0))

    def layer_of(array):
        return (array, (1,) + array.shape[1:], lambda s: (s, 0, 0))

    def layer(array, which):
        return (array, (1,) + array.shape[1:], lambda s: (which, 0, 0))

    def split_tile(array):
        return array.reshape((items, 2, il) + array.shape[2:])

    def to_slots(array):
        lead = array.shape[:-3]
        array = array.reshape(lead + (items, 2, il, JH, jl))
        at = len(lead)
        order = tuple(range(at)) + tuple(at + d for d in (3, 2, 1, 0, 4))
        return jnp.transpose(array, order).reshape(lead + (lane_rows, 128))

    def from_slots(array):
        lead = array.shape[:-2]
        array = array.reshape(lead + (JH, il, 2, items, jl))
        at = len(lead)
        order = tuple(range(at)) + tuple(at + d for d in (3, 2, 1, 0, 4))
        return jnp.transpose(array, order).reshape(lead + (items, tile_rows, tile_cols))

    def slot_index(dim):
        return lax.broadcasted_iota(jnp.int32, (JH, il, 128), dim)

    lane = slot_index(2)
    row_ids = row_index * tile_rows + (lane // HALF) * il + slot_index(1)
    col_ids = col_index * tile_cols + slot_index(0) * jl + lane % jl
    limit = jnp.tile(jnp.repeat(lengths, jl), 2)[None, None, :]
    keep = ((row_ids < limit) & (col_ids < limit)).astype(F32)
    eye = np.eye(C, dtype=ml_dtypes.bfloat16)
    eye_lanes = np.eye(256, dtype=ml_dtypes.bfloat16)

    def spread(array, axis):
        count = lax.axis_size(axis) if isinstance(axis, str) else devices
        return swap_all(jnp.broadcast_to(array[None], (count,) + array.shape), axis)

    def swap_all(array, axis):
        return lax.all_to_all(array, axis, split_axis=0, concat_axis=0, tiled=True)

    def tie(*arrays):
        return lax.optimization_barrier(arrays)

    node_rows = jnp.transpose(node_feats, (1, 0, 2)).reshape(tile_rows * items, D)
    cot_rows = jnp.transpose(node_cotan, (1, 0, 2)).reshape(tile_rows * items, D)
    node_full = node_rows.astype(F32)
    parts = tile_cols // tile_rows
    group = row_count // parts
    fetched = []
    for turn in range(parts):
        moves = []
        for src in range(devices):
            src_row, src_col = divmod(src, col_count)
            dst_row = ((src_row + turn) % parts) * group + src_col
            moves.append((src, dst_row * col_count + src_row // parts))
        fetched.append(lax.ppermute(node_rows, BOTH, moves))
    first = row_index // group
    fetched = jnp.stack(fetched)
    col_rows = jnp.concatenate(
        [
            lax.dynamic_index_in_dim(fetched, (first - h) % parts, 0, keepdims=False)
            for h in range(parts)
        ],
        axis=0,
    )
    share = tile_rows * items // col_count

    def node_norm(values):
        centered = values - jnp.mean(values, axis=-1, keepdims=True)
        inv = lax.rsqrt(jnp.mean(centered * centered, axis=-1, keepdims=True) + EPS)
        return centered * inv, inv

    heads_here = H // col_count
    head_width = heads_here * HD
    head_start = col_index * head_width
    w_local = jnp.concatenate(
        [
            lax.dynamic_slice_in_dim(w_qkv, part * D + head_start, head_width, 1)
            for part in range(3)
        ],
        axis=1,
    )
    wo_local = lax.dynamic_slice_in_dim(w_node_out, head_start, head_width, 0)
    node_unit, _ = node_norm(node_full)
    normed_node = half(node_unit * g_node)
    left_node = half(dot(normed_node, w_ab[:, :OP], 1, 0))
    col_unit, _ = node_norm(col_rows.astype(F32))
    def il_first(rows):
        rows = rows.reshape(2, il, items, rows.shape[1])
        return jnp.transpose(rows, (1, 0, 2, 3)).reshape(-1, rows.shape[3])

    left_node = il_first(left_node)
    perm = np.zeros((JH, jl, items, JH, 2, items, jl), ml_dtypes.bfloat16)
    for j in range(JH):
        for n in range(jl):
            for b in range(items):
                perm[j, n, b, j, :, b, n] = 1
    middle, right_wide = call(
        node_kernel,
        1,
        [
            whole(il_first(node_rows)),
            whole(col_rows),
            whole(g_node[None]),
            whole(w_ab),
            whole(w_outer),
            whole(perm.reshape(tile_cols * items, JH * 128)),
        ],
        [
            whole(sds((tile_rows * items, OP * C), F32)),
            whole(sds((JH, OP, 128), F32)),
        ],
        1000,
    )
    dist_slots = to_slots(distances)

    def padded(arrays):
        flat = jnp.concatenate(arrays, axis=0)
        rows = -(-flat.shape[0] // (devices * 8)) * 8
        flat = jnp.pad(flat, ((0, devices * rows - flat.shape[0]), (0, 0)))
        return flat.reshape(devices, rows, 128)

    def scatter_sum(array):
        return jnp.sum(swap_all(array, BOTH).astype(F32), axis=0)

    def to_channels(rows):
        return swap_all(jnp.transpose(rows, (1, 0, 2)), BOTH)

    def to_pairs(slabs):
        got = jnp.transpose(swap_all(slabs, BOTH), (1, 0, 2))
        return got if got.shape[0] == lane_rows else got.reshape(sides.shape)

    sides = sds((JH, 2, il, C, 128), BF16)
    single = sds((lane_rows, C, 128), BF16)
    slab1 = whole(sds((devices, lane_rows, 128), BF16))
    slab2 = whole(sds((devices, 2 * lane_rows, 128), BF16))
    blocks = whole(sds((residues, col_count * 256), BF16))
    block = pltpu.VMEM((residues, col_count * 256), BF16)
    flips = pltpu.VMEM((col_count * 256, residues), BF16)
    block32 = pltpu.VMEM((residues, col_count * 256), F32)
    chan_flops = 2 * col_count * col_count * residues * 256 * 256
    sums = f_whole(8, C)
    sides_out = (
        sds((C, 2 * lane_rows, 128), BF16),
        (C, 2 * il, 128),
        lambda s: (0, s, 0),
    )
    part = pltpu.VMEM((C, width), BF16)
    square = pltpu.VMEM((C, C), F32)
    wide = pltpu.VMEM((C, 2 * il, 128), F32)
    line = pltpu.VMEM((1, width), F32)

    def part32(rows=C):
        return pltpu.VMEM((rows, width), F32)


    def b_chan(rows=C):
        return chan(sds((rows, slots), BF16))

    g_in = [column(1 + t) for t in range(2)]
    g_out = [column(3 + t) for t in range(2)]
    keep_in = layer_of(keep)
    bd = (right_wide, (1,) + right_wide.shape[1:], lambda s: (s, 0, 0))
    pos_flops = 2 * slots * C * C

    def factors(values, t, more=()):
        return call(
            factor_kernel,
            steps,
            [chan(values), keep_in, g_in[t], layer(w_tin, t)],
            [b_chan(), chan(sds((1, slots), F32)), b_chan(), b_chan(4 * CH), *more],
            5 * pos_flops,
            [part32(5 * CH)],
        )

    pair_one, sides0, mids = call(
        open_kernel,
        steps,
        [
            tile(split_tile(pair_feats)),
            whole(eye),
            whole(middle),
            bd,
            column(0),
            keep_in,
            g_in[0],
            layer(w_tin, 0),
        ],
        [f_chan(), sides_out, whole(sds((2 * items * OP, width), BF16))],
        6 * pos_flops,
        [
            pltpu.VMEM((width, 2 * items * OP), BF16),
            pltpu.VMEM((width, 128), F32),
            part,
            part32(4 * CH),
            part,
            wide,
        ],
    )
    slabs0 = swap_all(sides0, BOTH)
    unit0, inv0, _, factor0, gate0 = factors(pair_one, 0, [b_chan()])
    x_chan, bias = call(
        bias_kernel,
        steps,
        [
            tile(split_tile(pair_feats)),
            whole(eye),
            whole(w_bias),
            (w_dist.reshape(-1, 1), (H, 1), lambda s: (0, 0)),
            chan(dist_slots.reshape(1, slots)),
        ],
        [b_chan(), b_chan(H)],
        pos_flops // 10,
    )

    qkv = half(dot(node_rows, w_local, 1, 0))
    slabs0, own = tie(slabs0, qkv[:, head_width:].reshape(-1, 128))
    everyone = spread(own, "row").reshape(residues, items, 2 * head_width)
    (p0,) = call(
        out_product_kernel,
        1,
        [whole(slabs0)],
        [slab1],
        chan_flops,
        [block, block],
        SMALL_VMEM,
    )
    p0, everyone = tie(p0, everyone)
    prod0 = to_pairs(p0)
    cot, d_active = call(
        cotangent_kernel,
        steps,
        [tile(split_tile(pair_cotan)), whole(eye), whole(w_down)],
        [b_chan(), b_chan(FT)],
        5 * pos_flops,
    )

    prod0, bias = tie(prod0, bias)
    bias_rows = swap_all(bias.reshape(H, lane_rows, 128), "col")
    pair_two, sides1, gate1 = call(
        middle_kernel,
        steps,
        [
            chan(pair_one),
            chan(gate0),
            rows_of(prod0),
            keep_in,
            g_out[0],
            layer(w_tout, 0),
            g_in[1],
            layer(w_tin, 1),
        ],
        [f_chan(), sides_out, b_chan()],
        6 * pos_flops,
        [part, part32(), part32(5 * CH), wide],
    )
    sides1, bias_rows = tie(sides1, bias_rows)
    slabs1 = swap_all(sides1, BOTH)
    unit1, inv1, normed1, factor1 = factors(pair_two, 1)

    def rear(product, gate, t):
        return call(
            rear_kernel,
            steps,
            [rows_of(product), chan(gate), g_out[t], layer(w_tout, t)],
            [b_chan(), chan(sds((1, slots), F32)), b_chan()],
            pos_flops,
            [part, part32()],
        )

    prod_unit0, prod_inv0, slope0 = rear(prod0, gate0, 0)

    bias_rows = from_slots(bias_rows.reshape(col_count, heads_here, lane_rows, 128))
    bias_rows = jnp.transpose(bias_rows, (2, 1, 3, 0, 4)).reshape(
        items, heads_here, tile_rows, residues
    )
    key_all = everyone[..., :head_width].reshape(residues, items, heads_here, HD)
    value_all = everyone[..., head_width:].reshape(residues, items, heads_here, HD)
    query = qkv[:, :head_width].reshape(tile_rows, items, heads_here, HD)
    all_ids = jnp.arange(residues, dtype=jnp.int32)
    key_keep = (all_ids[None, :] < lengths[:, None]).astype(F32)

    def product(spec, *operands):
        return jnp.einsum(spec, *operands, preferred_element_type=F32)

    scores = (
        product("ighd,jghd->ghij", query, key_all) * score_scale
        + bias_rows.astype(F32)
        + ((key_keep - 1.0) * 1000000000.0)[:, None, None, :]
    )
    probs = jax.nn.softmax(scores, axis=-1)
    probs_half = half(probs)
    attended = half(
        product("ghij,jghd->ighd", probs_half, value_all).reshape(
            tile_rows * items, head_width
        )
    )
    node_part = half(dot(attended, wo_local, 1, 0))
    d_attended = half(dot(cot_rows, wo_local, 1, 1)).reshape(tile_rows, items, heads_here, HD)
    d_probs = product("ighd,jghd->ghij", d_attended, value_all)
    d_value = product("ghij,ighd->jghd", probs_half, d_attended)
    d_scores = half(probs * (d_probs - jnp.sum(probs * d_probs, axis=-1, keepdims=True)))
    d_query = product("ghij,jghd->ighd", d_scores, key_all) * score_scale
    d_key = product("ghij,ighd->jghd", d_scores, query) * score_scale
    d_bias = jnp.transpose(
        d_scores.reshape(items, heads_here, tile_rows, col_count, tile_cols), (3, 1, 0, 2, 4)
    )
    d_bias = to_slots(d_bias).reshape(col_count, heads_here * lane_rows, 128)
    sent = jnp.concatenate([d_bias, node_part.reshape(col_count, -1, 128)], axis=1)
    d_kv = jnp.concatenate(
        [d_key.reshape(-1, head_width), d_value.reshape(-1, head_width)], axis=1
    )
    slabs1, sent = tie(slabs1, sent)
    got = swap_all(sent, "col")
    bias_lanes = heads_here * lane_rows
    d_bias = got[:, :bias_lanes].reshape(H, lane_rows, 128)
    node_sum = jnp.sum(got[:, bias_lanes:].astype(F32), axis=0)
    (p1,) = call(
        in_product_kernel,
        1,
        [whole(slabs1), whole(eye_lanes)],
        [slab1],
        chan_flops,
        [block, block, flips],
        SMALL_VMEM,
    )
    p1, d_bias, node_sum = tie(p1, d_bias, node_sum)
    prod1 = to_pairs(p1)
    d_bias32 = d_bias.astype(F32)
    grad_dist = from_slots(jnp.sum(d_bias32 * w_dist[:, None, None], axis=0))
    dw_dist = jnp.sum(d_bias32 * dist_slots[None], axis=(1, 2))
    d_bias_chan = d_bias.reshape(H, slots)

    prod1, d_kv, cot, d_active = tie(prod1, half(d_kv), cot, d_active)
    d_kv = swap_all(d_kv.reshape(row_count, -1, 128), "row")
    grad2, dprod1, dg_trans, dg_out1 = call(
        turn_kernel,
        steps,
        [
            chan(pair_two),
            chan(gate1),
            rows_of(prod1),
            chan(cot),
            chan(d_active),
            g_out[1],
            layer(w_tout, 1),
            column(5),
            whole(w_up),
        ],
        [f_chan(), rows_of(single), sums, sums],
        10 * pos_flops,
        [
            part,
            part,
            part,
            line,
            part,
            line,
            part32(),
            part32(FT),
            pltpu.VMEM((FT, width), BF16),
            square,
            square,
        ],
    )
    dprod1, d_kv = tie(dprod1, d_kv)
    dp1 = to_channels(dprod1)
    _, _, slope1 = rear(prod1, gate1, 1)
    pair_out, dw_down, dw_up, dw_out1 = call(
        finish_kernel,
        steps,
        [
            chan(pair_two),
            chan(gate1),
            rows_of(prod1),
            chan(cot),
            chan(d_active),
            chan(grad2),
            g_out[1],
            layer(w_tout, 1),
            column(5),
            whole(w_up),
            whole(w_down),
        ],
        [
            tile(sds((items, 2, il, tile_cols, C), F32)),
            f_whole(FT, C),
            f_whole(FT, C),
            f_whole(C, CH),
        ],
        13 * pos_flops,
        [
            part,
            part,
            part32(),
            part32(),
            part32(FT),
            pltpu.VMEM((FT, width), BF16),
            pltpu.VMEM((FT, width), BF16),
            pltpu.VMEM((FT, C), F32),
        ],
    )
    d_kv = jnp.sum(d_kv.astype(F32), axis=0).reshape(tile_rows * items, 2 * head_width)
    d_qkv = half(jnp.concatenate([d_query.reshape(-1, head_width), d_kv], axis=1))
    d_att = half(dot(d_qkv, w_local, 1, 1)).reshape(col_count, -1, 128)

    dp1, d_att, dw_down, dw_up, dw_out1 = tie(
        dp1, d_att, dw_down, dw_up, dw_out1
    )
    d_att = swap_all(d_att, "col")
    l1, r1 = call(unpack_kernel, 1, [whole(slabs1)], [blocks, blocks], pos_flops)
    (d1,) = call(
        in_back_kernel,
        1,
        [whole(l1), whole(r1), whole(dp1)],
        [slab2],
        2 * chan_flops,
        [block],
    )
    d1, d_att = tie(d1, d_att)
    dsides1 = to_pairs(d1)
    d_att = jnp.sum(d_att.astype(F32), axis=0).reshape(share, D)
    head_grads = jnp.concatenate(
        [dot(d_qkv, node_rows, 0, 0), dot(attended, cot_rows, 0, 0)], axis=0
    )

    mid_arrays = [
        dw_down,
        dw_up,
        dw_out1,
        jnp.pad(dw_dist[None], ((0, 7), (0, 128 - H))),
        dg_trans,
        dg_out1,
    ]
    dsides1, mid_sent, factor1, unit1, slope1, prod_unit0 = tie(
        dsides1, half(padded(mid_arrays)), factor1, unit1, slope1, prod_unit0
    )
    mid_part = swap_all(mid_sent, BOTH)
    grad1, dprod0, dg_in1, dg_out0 = call(
        back_kernel,
        steps,
        [
            double(dsides1),
            chan(factor1),
            chan(slope1),
            chan(unit1),
            chan(inv1),
            chan(grad2),
            g_in[1],
            layer(w_tin, 1),
            chan(gate0),
            chan(prod_unit0),
            chan(prod_inv0),
            g_out[0],
            layer(w_tout, 0),
        ],
        [f_chan(), rows_of(single), sums, sums],
        8 * pos_flops,
        [pltpu.VMEM((5 * CH, width), BF16), part, part, square, square],
    )
    dprod0, mid_part = tie(dprod0, mid_part)
    dp0 = to_channels(dprod0)
    mid_part = jnp.sum(mid_part.astype(F32), axis=0)

    dp0, head_grads = tie(dp0, head_grads)
    head_grads = swap_all(head_grads.reshape(row_count, -1, 128), "row")
    l0, r0 = call(unpack_kernel, 1, [whole(slabs0)], [blocks, blocks], pos_flops)
    (d0,) = call(
        out_back_kernel,
        1,
        [whole(l0), whole(r0), whole(dp0), whole(eye_lanes)],
        [slab2],
        2 * chan_flops,
        [block, block32, flips],
    )
    d0, head_grads = tie(d0, head_grads)
    dsides0 = to_pairs(d0)
    head_grads = jnp.sum(head_grads, axis=0)
    dw_in1, dw_out0, dw_bias_t = call(
        weights_kernel,
        steps,
        [
            double(dsides1),
            chan(factor1),
            chan(slope1),
            chan(grad2),
            chan(normed1),
            chan(grad1),
            chan(gate0),
            chan(prod_unit0),
            g_out[0],
            chan(d_bias_chan),
            chan(x_chan),
        ],
        [f_whole(5 * CH, C), f_whole(C, CH), f_whole(H, C)],
        6 * pos_flops,
        [pltpu.VMEM((5 * CH, width), BF16), pltpu.VMEM((5 * CH, C), F32)],
    )
    mid_part = half(jnp.concatenate([mid_part, head_grads], axis=0))

    dsides0, mid_part, dw_in1, dw_out0, dw_bias_t = tie(
        dsides0, mid_part, dw_in1, dw_out0, dw_bias_t
    )
    mid_all = spread(mid_part, BOTH)
    grad_pair, d_middle, dw_in0, dg_in0, d_right_wide, db_outer = call(
        close_kernel,
        steps,
        [
            double(dsides0),
            chan(factor0),
            chan(slope0),
            chan(unit0),
            chan(inv0),
            chan(grad1),
            keep_in,
            g_in[0],
            layer(w_tin, 0),
            whole(mids),
            bd,
            chan(d_bias_chan),
            whole(w_bias),
        ],
        [
            tile(sds((items, 2, il, tile_cols, C), F32)),
            whole(sds(middle.shape, F32)),
            f_whole(5 * CH, C),
            sums,
            (sds((JH, OP, 128), F32), (1, OP, 128), lambda s: (s, 0, 0)),
            sums,
        ],
        14 * pos_flops,
        [
            pltpu.VMEM((5 * CH, width), BF16),
            part,
            pltpu.VMEM((width, 128), BF16),
            square,
            pltpu.VMEM((width, 2 * items * OP), F32),
            part32(),
            pltpu.VMEM((5 * CH, C), F32),
        ],
    )
    grad_pair, mid_all, d_middle = tie(grad_pair, mid_all, d_middle)
    mid_rows = mid_all.shape[1] - head_grads.shape[0]
    pick_left = np.zeros((2, col_count, 8, il, 2, items), ml_dtypes.bfloat16)
    pick_right = np.zeros((parts, 2, JH, col_count, 8, 2, items, jl), ml_dtypes.bfloat16)
    for c in range(col_count):
        for n in range(share):
            i, b = divmod(c * share + n, items)
            pick_left[n % 2, c, n // 2, i % il, i // il, b] = 1
            for h in range(parts):
                j = h * tile_rows + i
                pick_right[h, n % 2, j // jl, c, n // 2, :, b, j % jl] = 1
    pick_left = pick_left.reshape(2, 8 * col_count, tile_rows * items)
    pick_right = pick_right.reshape(parts, 2, JH, 8 * col_count, 128)
    places = jnp.zeros((2, 128, OP * C), BF16)
    places = places.at[0, :OP].set(w_outer).at[1, HALF : HALF + OP].set(w_outer)
    own_row = (jnp.arange(row_count) == row_index).astype(F32)
    own_col = (jnp.arange(row_count) // parts == col_index).astype(F32)
    masks = jnp.broadcast_to(
        jnp.concatenate([own_row, own_col])[:, None], (2 * row_count, 128)
    )
    col_units = jnp.transpose(half(col_unit).reshape(JH, jl, items, D), (0, 2, 1, 3))
    col_units = jnp.tile(col_units.reshape(JH, items * jl, D), (1, 2, 1))
    late_arrays = [dw_in0, dg_in0, db_outer, dw_in1, dw_out0, dg_in1, dg_out0, dw_bias_t]
    late_rows = [a.shape[0] for a in late_arrays] + [OP * OP, 4 * OP]
    (sent,) = call(
        functools.partial(tail_kernel, len(late_arrays)),
        1,
        [whole(a) for a in late_arrays]
        + [
            whole(d_middle),
            whole(left_node),
            whole(w_outer),
            whole(il_first(half(node_unit))),
            whole(d_right_wide),
            whole(col_units),
            whole(places),
            whole(pick_left),
            whole(pick_right),
            whole(masks),
        ],
        [whole(sds((devices, 32, 128), BF16))],
        1000,
        [pltpu.VMEM((OP * OP, 128), F32), pltpu.VMEM((4 * OP, 128), F32)],
    )
    got = scatter_sum(sent)
    late_part = got[:24]
    d_pair_rows = half(got[24 : 24 + share // 2]).reshape(share, 2 * OP)
    node_share = lax.dynamic_slice_in_dim(node_full, col_index * share, share, 0)
    cot_share = lax.dynamic_slice_in_dim(cot_rows, col_index * share, share, 0)
    unit, inv = node_norm(node_share)
    d_normed = half(dot(d_pair_rows, w_ab, 1, 1)).astype(F32)
    scaled = d_normed * g_node
    d_norm = inv * (
        scaled
        - jnp.mean(scaled, axis=-1, keepdims=True)
        - unit * jnp.mean(scaled * unit, axis=-1, keepdims=True)
    )
    grad_share = cot_share.astype(F32) + d_att + d_norm
    out_share = node_share + node_sum.reshape(share, D)
    late_all = spread(half(late_part), BOTH)
    mine = jnp.stack([out_share, grad_share]).reshape(-1, 128)
    late_all, mine = tie(late_all, mine)
    nodes = spread(mine, "col").reshape(col_count, 2, share, D)

    def node_result(which):
        array = nodes[:, which].reshape(tile_rows, items, D)
        return jnp.transpose(array, (1, 0, 2))

    head_grads = mid_all[:, mid_rows:].astype(F32).reshape(row_count, col_count, -1)
    head_grads = jnp.transpose(head_grads, (1, 0, 2)).reshape(col_count, 4, head_width, D)
    g_qkv = jnp.transpose(head_grads[:, :3], (3, 1, 0, 2)).reshape(D, 3 * D)
    g_node_out = head_grads[:, 3].reshape(D, D)

    def widen(blocks):
        count = blocks.shape[0] // 128
        return jnp.concatenate([blocks[128 * n : 128 * n + 128] for n in range(count)], axis=1)

    def cut(flat, counts):
        start, pieces = 0, []
        for rows in counts:
            pieces.append(flat[start : start + rows])
            start += rows
        return pieces

    (
        s_down,
        s_up,
        s_out1,
        s_dist,
        s_trans,
        s_gout1,
    ) = cut(mid_all[:, :mid_rows].reshape(-1, 128).astype(F32), [a.shape[0] for a in mid_arrays])
    late_all = late_all.reshape(-1, 128).astype(F32)
    s_in0, s_gin0, s_bout, s_in1, s_out0, s_gin1, s_gout0, s_bias_t, s_outer, s_ab = cut(
        late_all, late_rows
    )
    s_outer = jnp.transpose(s_outer.reshape(OP, OP, C), (1, 0, 2))
    s_ab = jnp.transpose(s_ab.reshape(2, 2 * OP, 128), (0, 2, 1))
    s_ab = s_ab.reshape(D, 2 * OP)
    s_gnode = jnp.sum(s_ab * w_ab.astype(F32), axis=1)
    s_ab = s_ab * g_node[:, None]
    return (
        node_result(0),
        pair_out.reshape(pair_feats.shape),
        node_result(1),
        grad_pair.reshape(pair_feats.shape),
        grad_dist,
        g_qkv,
        jnp.transpose(s_bias_t),
        s_dist[0, :H],
        g_node_out,
        s_gnode,
        s_ab,
        s_outer.reshape(OP, OP * C),
        s_bout[0],
        jnp.stack([s_gin0[0], s_gin1[0]]),
        jnp.stack([widen(s_in0), widen(s_in1)]),
        jnp.stack([s_gout0[0], s_gout1[0]]),
        jnp.stack([s_out0, s_out1]),
        s_trans[0],
        widen(s_up),
        s_down,
    )


def solution(mesh):
    pair = P(None, "row", "col", None)
    node = P(None, "row", None)
    dist = P(None, "row", "col")
    return jax.shard_map(
        per_device,
        mesh=mesh,
        in_specs=(node, pair, dist, P(), node, pair) + (P(),) * 15,
        out_specs=(node, pair, node, pair, dist) + (P(),) * 15,
        check_vma=False,
    )
```

time: 598 us -> 554 us (0.926)
  blocking collectives: 66.8 us -> 0 us
  Pallas kernels: 140 us -> 179 us
  local copies, waits for them, and re-layouts: 76.5 us -> 66.3 us
  starting transfers between devices: 112 us -> 122 us
  waiting for transfers between devices: 162 us -> 152 us
  other arithmetic: 22.2 us -> 14.3 us
    all_to_all x2 -> x0, blocking collectives: 66.8 us -> none  [swap_all(): return lax.all_to_all(array, axis, split_axis=0, concat_axis=0, tiled=True)]
    pallas_call x10 -> x21, Pallas kernels: 140 us -> 179 us  [call(): pl.pallas_call(kernel, grid=(steps,), in_specs=[pl.BlockSpec(block, index...]
    reshape x20 -> x10, local copies, waits for them, and re-layouts: 17.1 us -> 3.88 us  [the longest x2 1.27 us: il_first(): return jnp.transpose(rows, (1, 0, 2, 3)).reshape(-1, rows.shape[3])]
    all_to_all x17 -> x19, starting transfers between devices: 104 us -> 116 us  [swap_all(): return lax.all_to_all(array, axis, split_axis=0, concat_axis=0, tiled=True)]
    all_to_all x17 -> x19, waiting for transfers between devices: 162 us -> 152 us  [swap_all(): return lax.all_to_all(array, axis, split_axis=0, concat_axis=0, tiled=True)]
  transfers between devices with their start and end apart: 19 -> 21, of which waited for: 9 -> 13; matrix products, arithmetic and copies ran while one was open for 10% -> 10% of each run, Pallas kernels for 18% -> 30%
where the time goes in v2:
time: 554 us; the launch traced here: 543 us
  Pallas kernels  179 us (32%)
  waiting for transfers between devices  152 us (27%)
  starting transfers between devices  122 us (22%)
  local copies, waits for them, and re-layouts  66.3 us (12%)
  other arithmetic  14.3 us (3%)
  matrix products  6.8 us (1%)
    pallas_call x21, Pallas kernels, call(): pl.pallas_call(kernel, grid=(steps,), in_specs=[pl.BlockSpec(block, index...  179 us
    all_to_all x19, waiting for transfers between devices, swap_all(): return lax.all_to_all(array, axis, split_axis=0, concat_axis=0, tiled=True)  152 us
    all_to_all x19, starting transfers between devices, swap_all(): return lax.all_to_all(array, axis, split_axis=0, concat_axis=0, tiled=True)  116 us
  transfers between devices with their start and end apart: 21, of which 13 were waited for; matrix products, arithmetic and copies ran while one was open for 10% of the time, Pallas kernels for 30%

profile of v2, /device:TPU:1, one launch (start us, length us, event | category | flops | bytes accessed | tf_op | source)
XLA Modules:
  0.0 542.8 jit_solution(16657886693739698193)
XLA Ops:
  1.6 6.0 %collective-permute-start = (bf16[96,256]{1,0:T(8,128)(2,1)S(1)}, bf16[96,256]{1,0:T(8,128)(2,1)S(1)}, u32[]{:S(2)}, u32[]{:S(2)}) collective-permute-start(bf16[96,256]{1,0:T(8,128)(2,1)S(1)} %reshape.490), channel_id=1, source_target_pairs={{0,0},{1,8},{2,16},{3,24},{4,32},{5,40},{6,48},{7,56},{8,64},{9,72... | collective-permute-start | bytes 147464 | tf_op jit(solution)/shard_map/ppermute | solution.py:967
  17.7 9.3 %open_kernel.1 = (f32[128,4608]{1,0:T(8,128)}, bf16[128,72,128]{2,1,0:T(8,128)(2,1)}, bf16[256,1536]{1,0:T(8,128)(2,1)}) custom-call(bf16[4,2,12,48,128]{4,3,2,1,0:T(8,128)(2,1)} %bitcast.181, bf16[128,128]{1,0:T(8,128)(2,1)} %constant.220.clone.eye_ref, f32[96,4096]{1,0:T(8,128)} %get-tuple-element.141.mid_ref, f32[3,32,128]{2,1,0:T(8,128)} %get-tuple-element.142.bd_ref, ...), custom_call_target="tpu_custom_call" | custom-call | flops 905969664 | bytes 8691712 | tf_op jit(solution)/shard_map/open_kernel/pallas_call | solution.py:828
  27.0 13.1 %all-to-all-start = ((bf16[128,72,128]{2,1,0:T(8,128)(2,1)}), bf16[128,72,128]{2,1,0:T(8,128)(2,1)S(1)}, u32[]{:S(2)}, u32[]{:S(2)}) async-start(bf16[128,72,128]{2,1,0:T(8,128)(2,1)} %get-tuple-element.143), calls=%async_computation | async-start | bytes 4718592 | tf_op jit(solution)/shard_map/all_to_all | solution.py:950
  40.8 32.2 %all-to-all-done.s_ref = bf16[128,72,128]{2,1,0:T(8,128)(2,1)S(1)} async-done(((bf16[128,72,128]{2,1,0:T(8,128)(2,1)}), bf16[128,72,128]{2,1,0:T(8,128)(2,1)S(1)}, u32[]{:S(2)}, u32[]{:S(2)}) %all-to-all-start) | async-done | bytes 2359328 | tf_op jit(solution)/shard_map/all_to_all | solution.py:950
  73.8 4.7 all-to-all-start.1
  78.4 6.6 %out_product_kernel.1 = bf16[128,36,128]{2,1,0:T(8,128)(2,1)S(1)} custom-call(bf16[128,72,128]{2,1,0:T(8,128)(2,1)S(1)} %all-to-all-done.s_ref), custom_call_target="tpu_custom_call" | custom-call | flops 3221225472 | bytes 3538944 | tf_op jit(solution)/shard_map/out_product_kernel/pallas_call | solution.py:828
  87.0 6.5 %all-to-all-start.2 = ((bf16[128,36,128]{2,1,0:T(8,128)(2,1)}), bf16[128,36,128]{2,1,0:T(8,128)(2,1)S(1)}, u32[]{:S(2)}, u32[]{:S(2)}) async-start(bf16[128,36,128]{2,1,0:T(8,128)(2,1)} %copy-done.5), calls=%async_computation.2 | async-start | bytes 2621440 | tf_op jit(solution)/shard_map/all_to_all | solution.py:950
  95.9 3.5 bias_kernel.1
  99.4 6.6 %factor_kernel.2 = (bf16[128,4608]{1,0:T(8,128)(2,1)}, f32[1,4608]{1,0:T(1,128)}, bf16[128,4608]{1,0:T(8,128)(2,1)}, bf16[512,4608]{1,0:T(8,128)(2,1)}, bf16[128,4608]{1,0:T(8,128)(2,1)}) custom-call(f32[128,4608]{1,0:T(8,128)} %get-tuple-element.147.in_ref.one_ref, f32[3,12,128]{2,1,0:T(8,128)} %fusion.39.keep_ref, ...), custom_call_target="tpu_custom_call" | custom-call | flops 754974720 | bytes 10984448 | tf_op jit(solution)/shard_map/factor_kernel/pallas_call | solution.py:828
  106.1 9.6 %all-to-all-done.2 = bf16[128,36,128]{2,1,0:T(8,128)(2,1)S(1)} async-done(((bf16[128,36,128]{2,1,0:T(8,128)(2,1)}), bf16[128,36,128]{2,1,0:T(8,128)(2,1)S(1)}, u32[]{:S(2)}, u32[]{:S(2)}) %all-to-all-start.2) | async-done | bytes 1179680 | tf_op jit(solution)/shard_map/all_to_all | solution.py:950
  121.0 9.2 %middle_kernel.1 = (f32[128,4608]{1,0:T(8,128)}, bf16[128,72,128]{2,1,0:T(8,128)(2,1)}, bf16[128,4608]{1,0:T(8,128)(2,1)}) custom-call(f32[128,4608]{1,0:T(8,128)} %get-tuple-element.147.in_ref.one_ref, bf16[128,4608]{1,0:T(8,128)(2,1)} %get-tuple-element.148.gate_ref, bf16[36,128,128]{2,1,0:T(8,128)(2,1)} %bitcast.176, f32[3,12,128]{2,1,0:T(8,128)} %fusion.39.keep_ref, ...), custom_call_target="tpu_custom_call" | custom-call | flops 905969664 | bytes 11034624 | tf_op jit(solution)/shard_map/middle_kernel/pallas_call | solution.py:828
  130.2 7.3 %all-to-all-start.4 = ((bf16[128,72,128]{2,1,0:T(8,128)(2,1)}), bf16[128,72,128]{2,1,0:T(8,128)(2,1)S(1)}, u32[]{:S(2)}, u32[]{:S(2)}) async-start(bf16[128,72,128]{2,1,0:T(8,128)(2,1)} %get-tuple-element.155), calls=%async_computation.4 | async-start | bytes 4718592 | tf_op jit(solution)/shard_map/all_to_all | solution.py:950
  156.7 13.5 %all-to-all-done.4.s_ref = bf16[128,72,128]{2,1,0:T(8,128)(2,1)S(1)} async-done(((bf16[128,72,128]{2,1,0:T(8,128)(2,1)}), bf16[128,72,128]{2,1,0:T(8,128)(2,1)S(1)}, u32[]{:S(2)}, u32[]{:S(2)}) %all-to-all-start.4) | async-done | bytes 2359328 | tf_op jit(solution)/shard_map/all_to_all | solution.py:950
  171.0 3.4 all-to-all-start.5
  174.4 8.0 %in_product_kernel.1 = bf16[128,36,128]{2,1,0:T(8,128)(2,1)S(1)} custom-call(bf16[128,72,128]{2,1,0:T(8,128)(2,1)S(1)} %all-to-all-done.4.s_ref, bf16[256,256]{1,0:T(8,128)(2,1)S(1)} %copy-done.6), custom_call_target="tpu_custom_call" | custom-call | flops 3221225472 | bytes 3670016 | tf_op jit(solution)/shard_map/in_product_kernel/pallas_call | solution.py:828
  184.2 7.1 %all-to-all-start.6 = ((bf16[128,36,128]{2,1,0:T(8,128)(2,1)}), bf16[128,36,128]{2,1,0:T(8,128)(2,1)S(1)}, u32[]{:S(2)}, u32[]{:S(2)}) async-start(bf16[128,36,128]{2,1,0:T(8,128)(2,1)} %copy-done.4), calls=%async_computation.6 | async-start | bytes 2621440 | tf_op jit(solution)/shard_map/all_to_all | solution.py:950
  191.4 5.1 cotangent_kernel.1
  198.8 14.7 %all-to-all-done.6 = bf16[128,36,128]{2,1,0:T(8,128)(2,1)S(1)} async-done(((bf16[128,36,128]{2,1,0:T(8,128)(2,1)}), bf16[128,36,128]{2,1,0:T(8,128)(2,1)S(1)}, u32[]{:S(2)}, u32[]{:S(2)}) %all-to-all-start.6) | async-done | bytes 1179680 | tf_op jit(solution)/shard_map/all_to_all | solution.py:950
  215.7 4.5 all-to-all-start.7
  220.2 13.7 %turn_kernel.1 = (f32[128,4608]{1,0:T(8,128)}, bf16[36,128,128]{2,1,0:T(8,128)(2,1)}, f32[8,128]{1,0:T(8,128)}, f32[8,128]{1,0:T(8,128)}) custom-call(f32[128,4608]{1,0:T(8,128)} %get-tuple-element.161.two_ref.in_ref, bf16[128,4608]{1,0:T(8,128)(2,1)} %get-tuple-element.162.gate_ref, bf16[36,128,128]{2,1,0:T(8,128)(2,1)} %bitcast.173, ...), custom_call_target="tpu_custom_call" | custom-call | flops 1509949440 | bytes 14366720 | tf_op jit(solution)/shard_map/turn_kernel/pallas_call | solution.py:828
  237.0 7.1 %all-to-all-start.8 = ((bf16[128,36,128]{2,1,0:T(8,128)(2,1)}), bf16[128,36,128]{2,1,0:T(8,128)(2,1)S(1)}, u32[]{:S(2)}, u32[]{:S(2)}) async-start(bf16[128,36,128]{2,1,0:T(8,128)(2,1)} %bitcast.166), calls=%async_computation.8 | async-start | bytes 2621440 | tf_op jit(solution)/shard_map/all_to_all | solution.py:950
  244.4 4.5 unpack_kernel.3
  248.9 16.4 %finish_kernel.1 = (f32[4,2,12,48,128]{4,3,2,1,0:T(8,128)}, f32[512,128]{1,0:T(8,128)}, f32[512,128]{1,0:T(8,128)}, f32[128,128]{1,0:T(8,128)}) custom-call(f32[128,4608]{1,0:T(8,128)} %get-tuple-element.161.two_ref.in_ref, bf16[128,4608]{1,0:T(8,128)(2,1)} %get-tuple-element.162.gate_ref, bf16[36,128,128]{2,1,0:T(8,128)(2,1)} %bitcast.174, ...), custom_call_target="tpu_custom_call" | custom-call | flops 1962934272 | bytes 16259072 | tf_op jit(solution)/shard_map/finish_kernel/pallas_call | solution.py:828
  266.3 5.5 %all-to-all-start.9 = ((bf16[8,24,128]{2,1,0:T(8,128)(2,1)}), bf16[8,24,128]{2,1,0:T(8,128)(2,1)S(1)}, u32[]{:S(2)}, u32[]{:S(2)}) async-start(bf16[8,24,128]{2,1,0:T(8,128)(2,1)} %reshape.508), calls=%async_computation.9 | async-start | bytes 98304 | tf_op jit(solution)/shard_map/all_to_all | solution.py:950
  271.8 13.2 %in_back_kernel.1 = bf16[128,72,128]{2,1,0:T(8,128)(2,1)} custom-call(bf16[384,2048]{1,0:T(8,128)(2,1)} %get-tuple-element.159.l_ref, bf16[384,2048]{1,0:T(8,128)(2,1)} %get-tuple-element.160.r_ref, bf16[128,36,128]{2,1,0:T(8,128)(2,1)} %copy-done.10), custom_call_target="tpu_custom_call" | custom-call | flops 6442450944 | bytes 6684672 | tf_op jit(solution)/shard_map/in_back_kernel/pallas_call | solution.py:828
  285.7 10.0 %all-to-all-start.10 = ((bf16[128,72,128]{2,1,0:T(8,128)(2,1)}), bf16[128,72,128]{2,1,0:T(8,128)(2,1)S(1)}, u32[]{:S(2)}, u32[]{:S(2)}) async-start(bf16[128,72,128]{2,1,0:T(8,128)(2,1)} %in_back_kernel.1), calls=%async_computation.10 | async-start | bytes 4718592 | tf_op jit(solution)/shard_map/all_to_all | solution.py:950
  295.9 4.3 rear_kernel.3
  300.2 6.2 %factor_kernel.3 = (bf16[128,4608]{1,0:T(8,128)(2,1)}, f32[1,4608]{1,0:T(1,128)}, bf16[128,4608]{1,0:T(8,128)(2,1)}, bf16[512,4608]{1,0:T(8,128)(2,1)}) custom-call(f32[128,4608]{1,0:T(8,128)} %get-tuple-element.161.two_ref.in_ref, f32[3,12,128]{2,1,0:T(8,128)} %fusion.39.keep_ref, f32[6,128,1]{2,1,0:T(8,128)} %copy.283.bout_ref.gain_ref.gout_ref.gin_ref.gtr_ref, ...), custom_call_target="tpu_custom_call" | custom-call | flops 754974720 | bytes 9804800 | tf_op jit(solution)/shard_map/factor_kernel/pallas_call | solution.py:828
  307.2 4.4 rear_kernel.2
  312.6 15.9 %all-to-all-done.10 = bf16[128,72,128]{2,1,0:T(8,128)(2,1)S(1)} async-done(((bf16[128,72,128]{2,1,0:T(8,128)(2,1)}), bf16[128,72,128]{2,1,0:T(8,128)(2,1)S(1)}, u32[]{:S(2)}, u32[]{:S(2)}) %all-to-all-start.10) | async-done | bytes 2359328 | tf_op jit(solution)/shard_map/all_to_all | solution.py:950
  330.5 4.8 all-to-all-start.11
  335.4 11.3 %back_kernel.1 = (f32[128,4608]{1,0:T(8,128)}, bf16[36,128,128]{2,1,0:T(8,128)(2,1)}, f32[8,128]{1,0:T(8,128)}, f32[8,128]{1,0:T(8,128)}) custom-call(bf16[3,2,12,128,128]{4,3,2,1,0:T(8,128)(2,1)} %bitcast.171, bf16[512,4608]{1,0:T(8,128)(2,1)} %get-tuple-element.192.factor_ref, bf16[128,4608]{1,0:T(8,128)(2,1)} %get-tuple-element.193.slope_ref, ...), custom_call_target="tpu_custom_call" | custom-call | flops 1207959552 | bytes 18139136 | tf_op jit(solution)/shard_map/back_kernel/pallas_call | solution.py:828
  352.5 7.1 %all-to-all-start.12 = ((bf16[128,36,128]{2,1,0:T(8,128)(2,1)}), bf16[128,36,128]{2,1,0:T(8,128)(2,1)S(1)}, u32[]{:S(2)}, u32[]{:S(2)}) async-start(bf16[128,36,128]{2,1,0:T(8,128)(2,1)} %bitcast.165), calls=%async_computation.12 | async-start | bytes 2621440 | tf_op jit(solution)/shard_map/all_to_all | solution.py:950
  362.8 4.5 unpack_kernel.2
  367.8 14.1 %all-to-all-done.12.dp_ref = bf16[128,36,128]{2,1,0:T(8,128)(2,1)S(1)} async-done(((bf16[128,36,128]{2,1,0:T(8,128)(2,1)}), bf16[128,36,128]{2,1,0:T(8,128)(2,1)S(1)}, u32[]{:S(2)}, u32[]{:S(2)}) %all-to-all-start.12) | async-done | bytes 1179680 | tf_op jit(solution)/shard_map/all_to_all | solution.py:950
  382.5 4.2 all-to-all-start.13
  386.7 16.2 %out_back_kernel.1 = bf16[128,72,128]{2,1,0:T(8,128)(2,1)} custom-call(bf16[384,2048]{1,0:T(8,128)(2,1)} %get-tuple-element.145.l_ref, bf16[384,2048]{1,0:T(8,128)(2,1)} %get-tuple-element.146.r_ref, bf16[128,36,128]{2,1,0:T(8,128)(2,1)} %copy-done.9, bf16[256,256]{1,0:T(8,128)(2,1)} %constant.221.clone.eye_ref), custom_call_target="tpu_custom_call" | custom-call | flops 6442450944 | bytes 6815744 | tf_op jit(solution)/shard_map/out_back_kernel/pallas_call | solution.py:828
  403.6 7.5 %all-to-all-start.14 = ((bf16[128,72,128]{2,1,0:T(8,128)(2,1)}), bf16[128,72,128]{2,1,0:T(8,128)(2,1)S(1)}, u32[]{:S(2)}, u32[]{:S(2)}) async-start(bf16[128,72,128]{2,1,0:T(8,128)(2,1)} %out_back_kernel.1), calls=%async_computation.14 | async-start | bytes 4718592 | tf_op jit(solution)/shard_map/all_to_all | solution.py:950
  416.8 10.8 %weights_kernel.1 = (f32[640,128]{1,0:T(8,128)}, f32[128,128]{1,0:T(8,128)}, f32[8,128]{1,0:T(8,128)}) custom-call(bf16[3,2,12,128,128]{4,3,2,1,0:T(8,128)(2,1)} %bitcast.172, bf16[512,4608]{1,0:T(8,128)(2,1)} %get-tuple-element.192.factor_ref, bf16[128,4608]{1,0:T(8,128)(2,1)} %get-tuple-element.193.slope_ref, f32[128,4608]{1,0:T(8,128)} %get-tuple-element.174.grad_ref, ...), custom_call_target="tpu_custom_call" | custom-call | flops 905969664 | bytes 18168832 | tf_op jit(solution)/shard_map/weights_kernel/pallas_call | solution.py:828
  427.8 16.1 %all-to-all-done.14 = bf16[128,72,128]{2,1,0:T(8,128)(2,1)S(1)} async-done(((bf16[128,72,128]{2,1,0:T(8,128)(2,1)}), bf16[128,72,128]{2,1,0:T(8,128)(2,1)S(1)}, u32[]{:S(2)}, u32[]{:S(2)}) %all-to-all-start.14) | async-done | bytes 2359328 | tf_op jit(solution)/shard_map/all_to_all | solution.py:950
  447.1 4.8 all-to-all-start.15
  452.2 16.3 %close_kernel.1 = (f32[4,2,12,48,128]{4,3,2,1,0:T(8,128)}, f32[96,4096]{1,0:T(8,128)}, f32[640,128]{1,0:T(8,128)}, f32[8,128]{1,0:T(8,128)}, f32[3,32,128]{2,1,0:T(8,128)}, /*index=5*/f32[8,128]{1,0:T(8,128)}) custom-call(bf16[3,2,12,128,128]{4,3,2,1,0:T(8,128)(2,1)} %bitcast.180, bf16[512,4608]{1,0:T(8,128)(2,1)} %get-tuple-element.213.factor_ref, ...), custom_call_target="tpu_custom_call" | custom-call | flops 2113929216 | bytes 17392640 | tf_op jit(solution)/shard_map/close_kernel/pallas_call | solution.py:828
  473.9 5.6 %tail_kernel.1 = bf16[128,32,128]{2,1,0:T(8,128)(2,1)} custom-call(f32[640,128]{1,0:T(8,128)} %get-tuple-element.218.refs_0_, f32[8,128]{1,0:T(8,128)} %get-tuple-element.219.refs_1_, f32[8,128]{1,0:T(8,128)} %get-tuple-element.220.refs_2_, f32[640,128]{1,0:T(8,128)} %get-tuple-element.221.refs_3_, f32[128,128]{1,0:T(8,128)} %get-tuple-element.222.refs_4_, ...), custom_call_target="tpu_custom_call" | custom-call | flops 1000 | bytes 6260736 | tf_op jit(solution)/shard_map/tail_kernel/pallas_call | solution.py:828
  479.5 7.1 %all-to-all-start.16 = ((bf16[128,32,128]{2,1,0:T(8,128)(2,1)}), bf16[128,32,128]{2,1,0:T(8,128)(2,1)S(1)}, u32[]{:S(2)}, u32[]{:S(2)}) async-start(bf16[128,32,128]{2,1,0:T(8,128)(2,1)} %tail_kernel.1), calls=%async_computation.16 | async-start | bytes 2097152 | tf_op jit(solution)/shard_map/all_to_all | solution.py:950
  494.2 11.8 %all-to-all-done.16 = bf16[128,32,128]{2,1,0:T(8,128)(2,1)S(1)} async-done(((bf16[128,32,128]{2,1,0:T(8,128)(2,1)}), bf16[128,32,128]{2,1,0:T(8,128)(2,1)S(1)}, u32[]{:S(2)}, u32[]{:S(2)}) %all-to-all-start.16) | async-done | bytes 1048608 | tf_op jit(solution)/shard_map/all_to_all | solution.py:950
  507.3 4.2 all-to-all-start.17
  512.6 15.8 %all-to-all-done.17 = bf16[128,24,128]{2,1,0:T(8,128)(2,1)S(1)} async-done(((bf16[128,24,128]{2,1,0:T(8,128)(2,1)}), bf16[128,24,128]{2,1,0:T(8,128)(2,1)S(1)}, u32[]{:S(2)}, u32[]{:S(2)}) %all-to-all-start.17) | async-done | bytes 786464 | tf_op jit(solution)/shard_map/all_to_all | solution.py:950
  531.6 3.4 all-to-all-start.18
  (321 shorter events, 102.5 us)
Async XLA Ops:
  0.7 137.0 %copy-start = (bf16[256,256]{1,0:T(8,128)(2,1)S(1)}, bf16[256,256]{1,0:T(8,128)(2,1)}, u32[]{:S(2)}) copy-start(bf16[256,256]{1,0:T(8,128)(2,1)} %param.39) | copy-start | bytes 393220
  1.6 38.7 %copy-start.15 = (bf16[96,256]{1,0:T(8,128)(2,1)}, bf16[96,256]{1,0:T(8,128)(2,1)S(1)}, u32[]{:S(2)}) copy-start(bf16[96,256]{1,0:T(8,128)(2,1)S(1)} %reshape.490) | copy-start | bytes 147460
  1.6 11.7 %collective-permute-start = (bf16[96,256]{1,0:T(8,128)(2,1)S(1)}, bf16[96,256]{1,0:T(8,128)(2,1)S(1)}, u32[]{:S(2)}, u32[]{:S(2)}) collective-permute-start(bf16[96,256]{1,0:T(8,128)(2,1)S(1)} %reshape.490), channel_id=1, source_target_pairs={{0,0},{1,8},{2,16},{3,24},{4,32},{5,40},{6,48},{7,56},{8,64},{9,72... | collective-permute-start | bytes 147464 | tf_op jit(solution)/shard_map/ppermute | solution.py:967
  7.6 5.6 %collective-permute-start.1 = (bf16[96,256]{1,0:T(8,128)(2,1)S(1)}, bf16[96,256]{1,0:T(8,128)(2,1)S(1)}, u32[]{:S(2)}, u32[]{:S(2)}) collective-permute-start(bf16[96,256]{1,0:T(8,128)(2,1)S(1)} %reshape.490), channel_id=1, source_target_pairs={{0,64},{1,72},{2,80},{3,88},{4,96},{5,104},{6,112},{7,120},{8,0},{... | collective-permute-start | bytes 147464 | tf_op jit(solution)/shard_map/ppermute | solution.py:967
  27.0 13.1 %copy-start.41 = (bf16[256,768]{1,0:T(8,128)(2,1)S(1)}, bf16[256,768]{1,0:T(8,128)(2,1)}, u32[]{:S(2)}) copy-start(bf16[256,768]{1,0:T(8,128)(2,1)} %param.36) | copy-start | bytes 1179652
  27.0 46.1 %all-to-all-start = ((bf16[128,72,128]{2,1,0:T(8,128)(2,1)}), bf16[128,72,128]{2,1,0:T(8,128)(2,1)S(1)}, u32[]{:S(2)}, u32[]{:S(2)}) async-start(bf16[128,72,128]{2,1,0:T(8,128)(2,1)} %get-tuple-element.143), calls=%async_computation | async-start | bytes 4718592 | tf_op jit(solution)/shard_map/all_to_all | solution.py:950
  40.2 44.8 %copy-start.20 = (bf16[256,32]{1,0:T(8,128)(2,1)}, bf16[256,32]{1,0:T(8,128)(2,1)S(1)}, u32[]{:S(2)}) copy-start(bf16[256,32]{1,0:T(8,128)(2,1)S(1)} %get-tuple-element.347) | copy-start | bytes 49156
  40.3 44.8 %copy-start.22 = (bf16[256,32]{1,0:T(8,128)(2,1)}, bf16[256,32]{1,0:T(8,128)(2,1)S(1)}, u32[]{:S(2)}) copy-start(bf16[256,32]{1,0:T(8,128)(2,1)S(1)} %get-tuple-element.348) | copy-start | bytes 49156
  40.3 44.8 %copy-start.24 = (bf16[256,32]{1,0:T(8,128)(2,1)}, bf16[256,32]{1,0:T(8,128)(2,1)S(1)}, u32[]{:S(2)}) copy-start(bf16[256,32]{1,0:T(8,128)(2,1)S(1)} %get-tuple-element.349) | copy-start | bytes 49156
  73.0 12.1 %copy-start.2 = (bf16[128,72,128]{2,1,0:T(8,128)(2,1)}, bf16[128,72,128]{2,1,0:T(8,128)(2,1)S(1)}, u32[]{:S(2)}) copy-start(bf16[128,72,128]{2,1,0:T(8,128)(2,1)S(1)} %all-to-all-done.s_ref) | copy-start | bytes 7077892
  73.8 13.0 %all-to-all-start.1 = ((bf16[16,48,128]{2,1,0:T(8,128)(2,1)}), bf16[16,48,128]{2,1,0:T(8,128)(2,1)S(1)}, u32[]{:S(2)}, u32[]{:S(2)}) async-start(bf16[16,48,128]{2,1,0:T(8,128)(2,1)} %broadcast_in_dim.28), calls=%async_computation.1 | async-start | bytes 393216 | tf_op jit(solution)/shard_map/all_to_all | solution.py:950
  87.0 7.6 %copy-start.55 = (bf16[128,8]{0,1:T(8,128)(2,1)S(1)}, bf16[128,8]{0,1:T(8,128)(2,1)}, u32[]{:S(2)}) copy-start(bf16[128,8]{0,1:T(8,128)(2,1)} %param.37) | copy-start | bytes 6148
  87.0 8.3 %copy-start.53 = (f32[8]{0:T(128)S(1)}, f32[8]{0:T(128)}, u32[]{:S(2)}) copy-start(f32[8]{0:T(128)} %param.38) | copy-start | bytes 100
  87.0 28.7 %all-to-all-start.2 = ((bf16[128,36,128]{2,1,0:T(8,128)(2,1)}), bf16[128,36,128]{2,1,0:T(8,128)(2,1)S(1)}, u32[]{:S(2)}, u32[]{:S(2)}) async-start(bf16[128,36,128]{2,1,0:T(8,128)(2,1)} %copy-done.5), calls=%async_computation.2 | async-start | bytes 2621440 | tf_op jit(solution)/shard_map/all_to_all | solution.py:950
  106.1 10.9 %copy-start.43 = (bf16[8,4608]{1,0:T(8,128)(2,1)S(1)}, bf16[8,4608]{1,0:T(8,128)(2,1)}, u32[]{:S(2)}) copy-start(bf16[8,4608]{1,0:T(8,128)(2,1)} %get-tuple-element.154) | copy-start | bytes 221188
  117.6 12.5 %all-to-all-start.3 = ((bf16[8,36,128]{2,1,0:T(8,128)(2,1)}), bf16[8,36,128]{2,1,0:T(8,128)(2,1)S(1)}, u32[]{:S(2)}, u32[]{:S(2)}) async-start(bf16[8,36,128]{2,1,0:T(8,128)(2,1)} %copy.293), calls=%async_computation.3 | async-start | bytes 163840 | tf_op jit(solution)/shard_map/all_to_all | solution.py:950
  130.2 8.4 %copy-start.56 = (s32[4]{0:T(128)S(1)}, s32[4]{0:T(128)}, u32[]{:S(2)}) copy-start(s32[4]{0:T(128)} %param.33) | copy-start | bytes 52
  130.2 40.1 %all-to-all-start.4 = ((bf16[128,72,128]{2,1,0:T(8,128)(2,1)}), bf16[128,72,128]{2,1,0:T(8,128)(2,1)S(1)}, u32[]{:S(2)}, u32[]{:S(2)}) async-start(bf16[128,72,128]{2,1,0:T(8,128)(2,1)} %get-tuple-element.155), calls=%async_computation.4 | async-start | bytes 4718592 | tf_op jit(solution)/shard_map/all_to_all | solution.py:950
  153.7 20.7 %copy-start.6 = (bf16[256,256]{1,0:T(8,128)(2,1)S(1)}, bf16[256,256]{1,0:T(8,128)(2,1)}, u32[]{:S(2)}) copy-start(bf16[256,256]{1,0:T(8,128)(2,1)} %constant.221.clone.eye_ref) | copy-start | bytes 393220
  156.5 14.5 %copy-start.35 = (bf16[24,4,1,32]{3,1,0,2:T(4,128)(2,1)}, bf16[24,4,1,32]{3,1,0,2:T(4,128)(2,1)S(1)}, u32[]{:S(2)}) copy-start(bf16[24,4,1,32]{3,1,0,2:T(4,128)(2,1)S(1)} %copy.306) | copy-start | bytes 18436
  170.3 12.2 %copy-start.3 = (bf16[128,72,128]{2,1,0:T(8,128)(2,1)}, bf16[128,72,128]{2,1,0:T(8,128)(2,1)S(1)}, u32[]{:S(2)}) copy-start(bf16[128,72,128]{2,1,0:T(8,128)(2,1)S(1)} %all-to-all-done.4.s_ref) | copy-start | bytes 7077892
  171.0 12.5 %all-to-all-start.5 = ((bf16[8,60,128]{2,1,0:T(8,128)(2,1)}), bf16[8,60,128]{2,1,0:T(8,128)(2,1)S(1)}, u32[]{:S(2)}, u32[]{:S(2)}) async-start(bf16[8,60,128]{2,1,0:T(8,128)(2,1)} %copy.308), calls=%async_computation.5 | async-start | bytes 262144 | tf_op jit(solution)/shard_map/all_to_all | solution.py:950
  183.6 122.8 %copy-start.11 = (bf16[8,36,128]{2,0,1:T(8,128)(2,1)}, bf16[8,36,128]{2,0,1:T(8,128)(2,1)S(1)}, u32[]{:S(2)}) copy-start(bf16[8,36,128]{2,0,1:T(8,128)(2,1)S(1)} %copy.351) | copy-start | bytes 221188
  184.2 29.3 %all-to-all-start.6 = ((bf16[128,36,128]{2,1,0:T(8,128)(2,1)}), bf16[128,36,128]{2,1,0:T(8,128)(2,1)S(1)}, u32[]{:S(2)}, u32[]{:S(2)}) async-start(bf16[128,36,128]{2,1,0:T(8,128)(2,1)} %copy-done.4), calls=%async_computation.6 | async-start | bytes 2621440 | tf_op jit(solution)/shard_map/all_to_all | solution.py:950
  215.7 18.2 %all-to-all-start.7 = ((bf16[16,48,128]{2,1,0:T(8,128)(2,1)}), bf16[16,48,128]{2,1,0:T(8,128)(2,1)S(1)}, u32[]{:S(2)}, u32[]{:S(2)}) async-start(bf16[16,48,128]{2,1,0:T(8,128)(2,1)} %reshape.505), calls=%async_computation.7 | async-start | bytes 393216 | tf_op jit(solution)/shard_map/all_to_all | solution.py:950
  237.0 29.3 %all-to-all-start.8 = ((bf16[128,36,128]{2,1,0:T(8,128)(2,1)}), bf16[128,36,128]{2,1,0:T(8,128)(2,1)S(1)}, u32[]{:S(2)}, u32[]{:S(2)}) async-start(bf16[128,36,128]{2,1,0:T(8,128)(2,1)} %bitcast.166), calls=%async_computation.8 | async-start | bytes 2621440 | tf_op jit(solution)/shard_map/all_to_all | solution.py:950
  248.8 16.5 %copy-start.21 = (bf16[256,32]{1,0:T(8,128)(2,1)S(1)}, bf16[256,32]{1,0:T(8,128)(2,1)}, u32[]{:S(2)}) copy-start(bf16[256,32]{1,0:T(8,128)(2,1)} %copy-done.20) | copy-start | bytes 49156
  248.8 16.5 %copy-start.23 = (bf16[256,32]{1,0:T(8,128)(2,1)S(1)}, bf16[256,32]{1,0:T(8,128)(2,1)}, u32[]{:S(2)}) copy-start(bf16[256,32]{1,0:T(8,128)(2,1)} %copy-done.22) | copy-start | bytes 49156
  248.9 16.5 %copy-start.25 = (bf16[256,32]{1,0:T(8,128)(2,1)S(1)}, bf16[256,32]{1,0:T(8,128)(2,1)}, u32[]{:S(2)}) copy-start(bf16[256,32]{1,0:T(8,128)(2,1)} %copy-done.24) | copy-start | bytes 49156
  266.3 18.7 %all-to-all-start.9 = ((bf16[8,24,128]{2,1,0:T(8,128)(2,1)}), bf16[8,24,128]{2,1,0:T(8,128)(2,1)S(1)}, u32[]{:S(2)}, u32[]{:S(2)}) async-start(bf16[8,24,128]{2,1,0:T(8,128)(2,1)} %reshape.508), calls=%async_computation.9 | async-start | bytes 98304 | tf_op jit(solution)/shard_map/all_to_all | solution.py:950
  285.7 42.9 %all-to-all-start.10 = ((bf16[128,72,128]{2,1,0:T(8,128)(2,1)}), bf16[128,72,128]{2,1,0:T(8,128)(2,1)S(1)}, u32[]{:S(2)}, u32[]{:S(2)}) async-start(bf16[128,72,128]{2,1,0:T(8,128)(2,1)} %in_back_kernel.1), calls=%async_computation.10 | async-start | bytes 4718592 | tf_op jit(solution)/shard_map/all_to_all | solution.py:950
  330.5 18.9 %all-to-all-start.11 = ((bf16[128,16,128]{2,1,0:T(8,128)(2,1)}), bf16[128,16,128]{2,1,0:T(8,128)(2,1)S(1)}, u32[]{:S(2)}, u32[]{:S(2)}) async-start(bf16[128,16,128]{2,1,0:T(8,128)(2,1)} %bitcast.190), calls=%async_computation.11 | async-start | bytes 1048576 | tf_op jit(solution)/shard_map/all_to_all | solution.py:950
  352.5 7.7 %copy-start.16 = (bf16[96,256]{1,0:T(8,128)(2,1)S(1)}, bf16[96,256]{1,0:T(8,128)(2,1)}, u32[]{:S(2)}) copy-start(bf16[96,256]{1,0:T(8,128)(2,1)} %copy-done.15) | copy-start | bytes 147460
  352.5 8.6 %copy-start.39 = (bf16[256,64]{0,1:T(8,128)(2,1)S(1)}, bf16[256,64]{0,1:T(8,128)(2,1)}, u32[]{:S(2)}) copy-start(bf16[256,64]{0,1:T(8,128)(2,1)} %param.41) | copy-start | bytes 98308
  352.5 8.6 %copy-start.52 = (f32[256]{0:T(256)S(1)}, f32[256]{0:T(256)}, u32[]{:S(2)}) copy-start(f32[256]{0:T(256)} %param.40) | copy-start | bytes 3076
  352.5 29.3 %all-to-all-start.12 = ((bf16[128,36,128]{2,1,0:T(8,128)(2,1)}), bf16[128,36,128]{2,1,0:T(8,128)(2,1)S(1)}, u32[]{:S(2)}, u32[]{:S(2)}) async-start(bf16[128,36,128]{2,1,0:T(8,128)(2,1)} %bitcast.165), calls=%async_computation.12 | async-start | bytes 2621440 | tf_op jit(solution)/shard_map/all_to_all | solution.py:950
  359.7 7.6 %copy-start.29 = (bf16[96,256]{1,0:T(8,128)(2,1)S(1)}, bf16[96,256]{1,0:T(8,128)(2,1)}, u32[]{:S(2)}) copy-start(bf16[96,256]{1,0:T(8,128)(2,1)} %copy-done.28) | copy-start | bytes 147460
  359.7 7.6 %copy-start.36 = (bf16[24,4,1,32]{3,1,0,2:T(4,128)(2,1)S(1)}, bf16[24,4,1,32]{3,1,0,2:T(4,128)(2,1)}, u32[]{:S(2)}) copy-start(bf16[24,4,1,32]{3,1,0,2:T(4,128)(2,1)} %copy-done.35) | copy-start | bytes 18436
  382.5 20.4 %all-to-all-start.13 = ((f32[16,16,128]{2,1,0:T(8,128)}), f32[16,16,128]{2,1,0:T(8,128)S(1)}, u32[]{:S(2)}, u32[]{:S(2)}) async-start(f32[16,16,128]{2,1,0:T(8,128)} %reshape.510), calls=%async_computation.13 | async-start | bytes 262144 | tf_op jit(solution)/shard_map/all_to_all | solution.py:950
  402.9 8.2 %copy-start.45 = (f32[2,12,4]{2,1,0:T(8,128)S(1)}, f32[2,12,4]{2,1,0:T(8,128)}, u32[]{:S(2)}) copy-start(f32[2,12,4]{2,1,0:T(8,128)} %copy.337) | copy-start | bytes 1156
  402.9 9.0 %copy-start.7 = (bf16[32,4096]{1,0:T(8,128)(2,1)S(1)}, bf16[32,4096]{1,0:T(8,128)(2,1)}, u32[]{:S(2)}) copy-start(bf16[32,4096]{1,0:T(8,128)(2,1)} %refs_10_.1) | copy-start | bytes 786436
  403.6 40.3 %all-to-all-start.14 = ((bf16[128,72,128]{2,1,0:T(8,128)(2,1)}), bf16[128,72,128]{2,1,0:T(8,128)(2,1)S(1)}, u32[]{:S(2)}, u32[]{:S(2)}) async-start(bf16[128,72,128]{2,1,0:T(8,128)(2,1)} %out_back_kernel.1), calls=%async_computation.14 | async-start | bytes 4718592 | tf_op jit(solution)/shard_map/all_to_all | solution.py:950
  416.8 11.0 %copy-start.27 = (f32[16,16,128]{2,1,0:T(8,128)S(1)}, f32[16,16,128]{2,1,0:T(8,128)}, u32[]{:S(2)}) copy-start(f32[16,16,128]{2,1,0:T(8,128)} %copy-done.26) | copy-start | bytes 393220
  447.1 24.3 %all-to-all-start.15 = ((bf16[128,32,128]{2,1,0:T(8,128)(2,1)}), bf16[128,32,128]{2,1,0:T(8,128)(2,1)S(1)}, u32[]{:S(2)}, u32[]{:S(2)}) async-start(bf16[128,32,128]{2,1,0:T(8,128)(2,1)} %broadcast_in_dim.30), calls=%async_computation.15 | async-start | bytes 2097152 | tf_op jit(solution)/shard_map/all_to_all | solution.py:950
  479.5 26.5 %all-to-all-start.16 = ((bf16[128,32,128]{2,1,0:T(8,128)(2,1)}), bf16[128,32,128]{2,1,0:T(8,128)(2,1)S(1)}, u32[]{:S(2)}, u32[]{:S(2)}) async-start(bf16[128,32,128]{2,1,0:T(8,128)(2,1)} %tail_kernel.1), calls=%async_computation.16 | async-start | bytes 2097152 | tf_op jit(solution)/shard_map/all_to_all | solution.py:950
  494.2 17.3 %copy-start.40 = (bf16[256,64]{0,1:T(8,128)(2,1)S(1)}, bf16[256,64]{0,1:T(8,128)(2,1)}, u32[]{:S(2)}) copy-start(bf16[256,64]{0,1:T(8,128)(2,1)} %param.41) | copy-start | bytes 98308
  507.3 21.1 %all-to-all-start.17 = ((bf16[128,24,128]{2,1,0:T(8,128)(2,1)}), bf16[128,24,128]{2,1,0:T(8,128)(2,1)S(1)}, u32[]{:S(2)}, u32[]{:S(2)}) async-start(bf16[128,24,128]{2,1,0:T(8,128)(2,1)} %broadcast_in_dim.32), calls=%async_computation.17 | async-start | bytes 1572864 | tf_op jit(solution)/shard_map/all_to_all | solution.py:950
  531.6 9.2 %all-to-all-start.18 = ((f32[8,48,128]{2,1,0:T(8,128)}), f32[8,48,128]{2,1,0:T(8,128)S(1)}, u32[]{:S(2)}, u32[]{:S(2)}) async-start(f32[8,48,128]{2,1,0:T(8,128)} %broadcast_in_dim.33), calls=%async_computation.18 | async-start | bytes 393216 | tf_op jit(solution)/shard_map/all_to_all | solution.py:950
  (31 other events, 125.4 us)
